TPU v7x, 32 devices: a whole 2x2x4 slice. The times are simulated.
32 devices in a mesh: ep: 8 (over z, x), etp: 4 (over y, core).
Axes of the slice: x: 2, y: 2, z: 4, core: 2. Of those that a mesh axis runs over, the one named last changes fastest.
Arguments:
- tokens: bfloat16 [1024, 3072], P('ep', 'etp'), may hold values from -6 to 6
- grad_out: bfloat16 [1024, 3072], P('ep', 'etp'), may hold values from -6 to 6
- probs: float32 [1024, 4], P('ep'), may hold values from 0.1 to 1
- expert_ids: int32 [1024, 4], P('ep'), may hold values from 0 to 7, all different within a row; in each aligned block of 128 rows (0 to 127, 128 to 255, ...) at most 96 rows name the same one
- w_gate: bfloat16 [8, 3072, 5376], P('ep', None, 'etp'), may hold values from -0.109375 to 0.109375
- w_up: bfloat16 [8, 3072, 5376], P('ep', None, 'etp'), may hold values from -0.109375 to 0.109375
- w_down: bfloat16 [8, 5376, 3072], P('ep', 'etp'), may hold values from -0.078125 to 0.078125
Outputs:
- grad_tokens: bfloat16 [1024, 3072], P('ep', 'etp')
- grad_gate: bfloat16 [8, 3072, 5376], P('ep', None, 'etp')
- grad_up: bfloat16 [8, 3072, 5376], P('ep', None, 'etp')
- grad_down: bfloat16 [8, 5376, 3072], P('ep', 'etp')
Inputs may be any that keep to these rules, and one draw needn't show every extreme that they name: `expert_ids`: each row names 4 different experts. In the rows of one index of ep (aligned blocks of 128 rows) no expert is named by more than 96 rows, a bound that some block reaches.
All inputs are finite; a program needn't handle non-finite values.
Results may differ from a plain program's by a relative error of at most 0.02.
Values may be sent and summed in bfloat16 or wider, within the bound.
No kernel may reach another device: no remote copies, remote signals or barrier semaphores. Data moves between devices by JAX's collectives and lax.ppermute only.
A program may use at most 128 MiB of HBM per device.

v0:
```python
import jax
import jax.numpy as jnp
from jax import lax
from jax.sharding import PartitionSpec as P


def slot_index(block_ids, capacity, expert_count):
    flat_ids = block_ids.reshape(-1)
    onehot = (flat_ids[:, None] == jnp.arange(expert_count, dtype=jnp.int32)[None, :]).astype(
        jnp.int32
    )
    earlier = jnp.cumsum(onehot, axis=0) - onehot
    position = jnp.sum(earlier * onehot, axis=1)
    return flat_ids * capacity + position


def swiglu_back(gate_pre, up_pre, grad_hidden):
    sigmoid_gate = jax.nn.sigmoid(gate_pre)
    silu_gate = gate_pre * sigmoid_gate
    hidden = silu_gate * up_pre
    grad_pre_gate = grad_hidden * up_pre * sigmoid_gate * (1.0 + gate_pre * (1.0 - sigmoid_gate))
    grad_pre_up = grad_hidden * silu_gate
    return (hidden, grad_pre_gate, grad_pre_up)


def place_rows(slot_ids, copies, slot_count):
    return jnp.zeros((slot_count, copies.shape[1]), copies.dtype).at[slot_ids].set(copies)


def right_product(left, right):
    return lax.dot_general(
        left, right, (((1,), (1,)), ((), ())), preferred_element_type=jnp.float32
    )


def left_product(left, right):
    return lax.dot_general(
        left, right, (((0,), (0,)), ((), ())), preferred_element_type=jnp.float32
    )


def local(tokens, grad_out, probs, expert_ids, w_gate, w_up, w_down):
    experts = lax.axis_size("ep")
    tok_rows, top_count = expert_ids.shape
    capacity = 3 * tok_rows * top_count // (2 * experts)
    slot_count = experts * capacity
    slot_ids = slot_index(expert_ids, capacity, experts)
    scaled = (probs[:, :, None] * grad_out[:, None, :]).astype(jnp.bfloat16)
    scaled = scaled.reshape(tok_rows * top_count, tokens.shape[1])
    full_in, full_grad = (
        lax.all_gather(tokens, "etp", axis=1, tiled=True),
        lax.all_gather(scaled, "etp", axis=1, tiled=True),
    )
    full_width = full_in.shape[1]
    send_in = place_rows(slot_ids, jnp.repeat(full_in, top_count, axis=0), slot_count)
    send_grad = place_rows(slot_ids, full_grad, slot_count)
    expert_in, expert_grad = (
        lax.all_to_all(
            send_in.reshape(experts, capacity, full_width),
            "ep",
            split_axis=0,
            concat_axis=0,
            tiled=True,
        ),
        lax.all_to_all(
            send_grad.reshape(experts, capacity, full_width),
            "ep",
            split_axis=0,
            concat_axis=0,
            tiled=True,
        ),
    )
    model_width = expert_in.shape[2]
    expert_in = expert_in.reshape(slot_count, model_width)
    expert_grad = expert_grad.reshape(slot_count, model_width)
    gate_w = w_gate[0]
    up_w = w_up[0]
    down_w = w_down[0]
    gate_pre = jnp.dot(expert_in, gate_w, preferred_element_type=jnp.float32)
    up_pre = jnp.dot(expert_in, up_w, preferred_element_type=jnp.float32)
    grad_hidden = right_product(expert_grad, down_w)
    hidden, grad_pre_gate, grad_pre_up = swiglu_back(gate_pre, up_pre, grad_hidden)
    hidden = hidden.astype(jnp.bfloat16)
    grad_pre_gate = grad_pre_gate.astype(jnp.bfloat16)
    grad_pre_up = grad_pre_up.astype(jnp.bfloat16)
    grad_down = left_product(hidden, expert_grad).astype(jnp.bfloat16)[None]
    grad_gate = left_product(expert_in, grad_pre_gate).astype(jnp.bfloat16)[None]
    grad_up = left_product(expert_in, grad_pre_up).astype(jnp.bfloat16)[None]
    partial_value = (
        right_product(grad_pre_gate, gate_w) + right_product(grad_pre_up, up_w)
    ).astype(jnp.bfloat16)
    returned = lax.all_to_all(
        partial_value.reshape(experts, capacity, model_width),
        "ep",
        split_axis=0,
        concat_axis=0,
        tiled=True,
    )
    picked = returned.reshape(slot_count, model_width)[slot_ids].astype(jnp.float32)
    combined = jnp.sum(picked.reshape(tok_rows, top_count, model_width), axis=1)
    grad_tokens = lax.psum_scatter(
        combined.astype(jnp.bfloat16), "etp", scatter_dimension=1, tiled=True
    )
    return (grad_tokens, grad_gate, grad_up, grad_down)


def solution(mesh):
    return jax.shard_map(
        local,
        mesh=mesh,
        in_specs=(
            P("ep", "etp"),
            P("ep", "etp"),
            P("ep", None),
            P("ep", None),
            P("ep", None, "etp"),
            P("ep", None, "etp"),
            P("ep", "etp", None),
        ),
        out_specs=(
            P("ep", "etp"),
            P("ep", None, "etp"),
            P("ep", None, "etp"),
            P("ep", "etp", None),
        ),
        check_vma=False,
    )
```

profile of v0, /device:TPU:0, one launch (start us, length us, event | category | flops | bytes accessed | tf_op | source)
XLA Modules:
  0.0 446.1 jit_solution(1728488412034647479)
XLA Ops:
  7.2 0.8 copy.12
  8.2 0.7 broadcast_multiply_fusion
  8.9 1.1 reduce-window.6
  10.0 0.2 slice_reduce_fusion
  10.5 10.3 %all_gather.7 = bf16[128,3072]{1,0:T(8,128)(2,1)S(1)} all-gather(bf16[128,768]{1,0:T(8,128)(2,1)} %param.7), channel_id=1, replica_groups=mesh['ep'=8,'etp'=4] {'etp'}, dimensions={1}, use_global_device_ids=true | all-gather | bytes 983040 | tf_op jit(solution)/shard_map/all_gather | solution.py:51
  20.8 0.9 broadcast_in_dim.8
  21.7 2.4 reshape.112
  24.2 9.1 %scatter_custom_fusion.1 = bf16[768,3072]{1,0:T(8,128)(2,1)} fusion(s32[512]{0:T(512)S(1)} %bitcast.52, bf16[512,3072]{1,0:T(8,128)(2,1)} %reshape.112, bf16[]{:T(256)} %constant.5.clone.1), kind=kCustom, calls=%fused_computation.25 | custom fusion | bytes 4719104 | tf_op jit(solution)/shard_map/scatter | solution.py:27
  33.3 5.9 %all-to-all-start.1 = ((bf16[8,96,3072]{2,1,0:T(8,128)(2,1)}), bf16[8,96,3072]{2,1,0:T(8,128)(2,1)}, u32[]{:S(2)}, u32[]{:S(2)}) async-start(bf16[8,96,3072]{2,1,0:T(8,128)(2,1)} %bitcast.49), calls=%async_computation.1 | async-start | bytes 9437184 | tf_op jit(solution)/shard_map/all_to_all | solution.py:58
  39.2 0.3 all-gather.2.cloned.1.call-start
  39.5 0.2 mul.64
  39.7 0.5 mul.65
  40.5 1.0 multiply_convert_fusion.4
  41.5 30.2 %all-gather.2.cloned.1.call-done = bf16[512,3072]{1,0:T(8,128)(2,1)} async-done(((bf16[512,768]{1,0:T(8,128)(2,1)}), bf16[512,3072]{1,0:T(8,128)(2,1)}) %all-gather.2.cloned.1.call-update) | async-done | bytes 3145744 | tf_op jit(solution)/shard_map/all_gather | solution.py:52
  71.8 9.1 %scatter_custom_fusion = bf16[768,3072]{1,0:T(8,128)(2,1)} fusion(s32[512]{0:T(512)S(1)} %bitcast.53, bf16[512,3072]{1,0:T(8,128)(2,1)} %all-gather.2.cloned.1.call-done, bf16[]{:T(256)} %constant.5.clone.1), kind=kCustom, calls=%fused_computation.27 | custom fusion | bytes 4719104 | tf_op jit(solution)/shard_map/scatter | solution.py:27
  80.8 63.4 %all-to-all-done.1 = bf16[8,96,3072]{2,1,0:T(8,128)(2,1)} async-done(((bf16[8,96,3072]{2,1,0:T(8,128)(2,1)}), bf16[8,96,3072]{2,1,0:T(8,128)(2,1)}, u32[]{:S(2)}, u32[]{:S(2)}) %all-to-all-start.1) | async-done | bytes 4718624 | tf_op jit(solution)/shard_map/all_to_all | solution.py:58
  144.2 5.0 %all-to-all-start = ((bf16[8,96,3072]{2,1,0:T(8,128)(2,1)}), bf16[8,96,3072]{2,1,0:T(8,128)(2,1)}, u32[]{:S(2)}, u32[]{:S(2)}) async-start(bf16[8,96,3072]{2,1,0:T(8,128)(2,1)} %bitcast.50), calls=%async_computation | async-start | bytes 9437184 | tf_op jit(solution)/shard_map/all_to_all | solution.py:65
  149.3 11.7 %fusion.5 = f32[768,1344]{0,1:T(8,128)} fusion(bf16[768,3072]{1,0:T(8,128)(2,1)} %bitcast.8, bf16[1,3072,1344]{1,2,0:T(8,128)(2,1)} %param.11), kind=kOutput, calls=%fused_computation.12 | convolution fusion | flops 6341787648 | bytes 17104896 | tf_op jit(solution)/shard_map/dot_general | solution.py:79
  161.0 11.7 %fusion.9 = f32[768,1344]{0,1:T(8,128)} fusion(bf16[768,3072]{1,0:T(8,128)(2,1)} %bitcast.8, bf16[1,3072,1344]{1,2,0:T(8,128)(2,1)} %param.12), kind=kOutput, calls=%fused_computation.16 | convolution fusion | flops 6341787648 | bytes 17104896 | tf_op jit(solution)/shard_map/dot_general | solution.py:80
  172.7 80.6 %all-to-all-done = bf16[8,96,3072]{2,1,0:T(8,128)(2,1)} async-done(((bf16[8,96,3072]{2,1,0:T(8,128)(2,1)}), bf16[8,96,3072]{2,1,0:T(8,128)(2,1)}, u32[]{:S(2)}, u32[]{:S(2)}) %all-to-all-start) | async-done | bytes 4718624 | tf_op jit(solution)/shard_map/all_to_all | solution.py:65
  253.3 13.2 %multiply_convert_fusion.1 = (bf16[768,1344]{0,1:T(8,128)(2,1)S(1)}, bf16[768,1344]{0,1:T(8,128)(2,1)S(1)}) fusion(f32[768,1344]{0,1:T(8,128)} %fusion.5, f32[768,1344]{0,1:T(8,128)} %fusion.9, bf16[768,3072]{1,0:T(8,128)(2,1)} %bitcast.5, bf16[1,1344,3072]{2,1,0:T(8,128)(2,1)} %param.13), kind=kOutput, calls=%fused_computation.21 | convolution fusion | flops 6355206144 | bytes 25362432 | tf_op jit(solution)/shard_map/dot_general | solution.py:31
  266.5 10.7 %fusion.3 = f32[768,3072]{1,0:T(8,128)S(1)} fusion(bf16[768,1344]{0,1:T(8,128)(2,1)S(1)} %get-tuple-element.5, bf16[1,3072,1344]{1,2,0:T(8,128)(2,1)} %param.11), kind=kOutput, calls=%fused_computation.10 | convolution fusion | flops 6341787648 | bytes 19759104 | tf_op jit(solution)/shard_map/dot_general | solution.py:31
  277.2 12.7 %add_convert_fusion = bf16[768,3072]{1,0:T(8,128)(2,1)} fusion(f32[768,3072]{1,0:T(8,128)S(1)} %fusion.3, bf16[768,1344]{0,1:T(8,128)(2,1)S(1)} %get-tuple-element.4, bf16[1,3072,1344]{1,2,0:T(8,128)(2,1)} %param.12), kind=kOutput, calls=%fused_computation.9 | convolution fusion | flops 6346506240 | bytes 24477696 | tf_op jit(solution)/shard_map/dot_general | solution.py:31
  289.9 4.6 %all-to-all-start.2 = ((bf16[8,96,3072]{2,1,0:T(8,128)(2,1)}), bf16[8,96,3072]{2,1,0:T(8,128)(2,1)}, u32[]{:S(2)}, u32[]{:S(2)}) async-start(bf16[8,96,3072]{2,1,0:T(8,128)(2,1)} %bitcast.51), calls=%async_computation.2 | async-start | bytes 9437184 | tf_op jit(solution)/shard_map/all_to_all | solution.py:92
  294.6 11.2 %fusion.1 = bf16[1,3072,1344]{1,2,0:T(8,128)(2,1)} fusion(bf16[768,1344]{0,1:T(8,128)(2,1)S(1)} %get-tuple-element.5, bf16[768,3072]{1,0:T(8,128)(2,1)} %bitcast.8), kind=kOutput, calls=%fused_computation.7 | convolution fusion | flops 6345916416 | bytes 15040512 | tf_op jit(solution)/shard_map/dot_general | solution.py:37
  305.9 11.2 %fusion = bf16[1,1344,3072]{2,1,0:T(8,128)(2,1)} fusion(bf16[768,3072]{1,0:T(8,128)(2,1)} %bitcast.5, f32[768,1344]{0,1:T(8,128)S(1)} %copy-done.5, f32[768,1344]{0,1:T(8,128)S(1)} %copy-done.4), kind=kOutput, calls=%fused_computation.6 | convolution fusion | flops 6352109568 | bytes 21233664 | tf_op jit(solution)/shard_map/dot_general | solution.py:37
  317.0 81.3 %all-to-all-done.2 = bf16[8,96,3072]{2,1,0:T(8,128)(2,1)} async-done(((bf16[8,96,3072]{2,1,0:T(8,128)(2,1)}), bf16[8,96,3072]{2,1,0:T(8,128)(2,1)}, u32[]{:S(2)}, u32[]{:S(2)}) %all-to-all-start.2) | async-done | bytes 4718624 | tf_op jit(solution)/shard_map/all_to_all | solution.py:92
  398.3 9.0 %gather_fusion = bf16[512,3072]{1,0:T(8,128)(2,1)S(1)} fusion(bf16[768,3072]{1,0:T(8,128)(2,1)} %bitcast.12, s32[1024]{0:T(1024)S(1)} %pad_clamp_fusion), kind=kCustom, calls=%fused_computation | custom fusion | bytes 6293504 | tf_op jit(solution)/shard_map/gather | solution.py:99
  407.3 2.8 gather.6
  410.2 6.7 %reduce_sum.25 = bf16[128,3072]{1,0:T(8,128)(2,1)} reduce(bf16[128,4,3072]{2,1,0:T(4,128)(2,1)} %gather.6, bf16[]{:T(256)} %constant.5.clone.1), dimensions={1}, to_apply=%region_5.6 | reduce | flops 1179648 | bytes 3932162 | tf_op jit(solution)/shard_map/reduce_sum | solution.py:100
  416.9 11.1 %fusion.2 = bf16[1,3072,1344]{1,2,0:T(8,128)(2,1)} fusion(bf16[768,1344]{0,1:T(8,128)(2,1)S(1)} %copy-done.3, bf16[768,3072]{1,0:T(8,128)(2,1)} %bitcast.8), kind=kOutput, calls=%fused_computation.8 | convolution fusion | flops 6345916416 | bytes 15040512 | tf_op jit(solution)/shard_map/dot_general | solution.py:37
  428.0 11.0 %reduce-scatter.2.cloned.1.call-done = bf16[128,768]{1,0:T(8,128)(2,1)} async-done(((bf16[128,3072]{1,0:T(8,128)(2,1)}), bf16[128,768]{1,0:T(8,128)(2,1)}) %reduce-scatter.2.cloned.1.call-update) | async-done | bytes 196624 | tf_op jit(solution)/shard_map/reduce_scatter | solution.py:101
  (27 shorter events, 0.9 us)
Async XLA Ops:
  33.3 6.2 %copy-start = (bf16[128,768]{1,0:T(8,128)(2,1)S(1)}, bf16[128,768]{1,0:T(8,128)(2,1)}, u32[]{:S(2)}) copy-start(bf16[128,768]{1,0:T(8,128)(2,1)} %param.8) | copy-start | bytes 589828
  33.3 111.0 %all-to-all-start.1 = ((bf16[8,96,3072]{2,1,0:T(8,128)(2,1)}), bf16[8,96,3072]{2,1,0:T(8,128)(2,1)}, u32[]{:S(2)}, u32[]{:S(2)}) async-start(bf16[8,96,3072]{2,1,0:T(8,128)(2,1)} %bitcast.49), calls=%async_computation.1 | async-start | bytes 9437184 | tf_op jit(solution)/shard_map/all_to_all | solution.py:58
  39.2 1.0 copy-start.1
  39.2 32.5 %all-gather.2.cloned.1.call-start = ((), (), s32[]{:S(2)}) async-start(), calls=%async_computation.4 | async-start | bytes 3932160 | tf_op jit(solution)/shard_map/all_gather | solution.py:52
  144.2 109.1 %all-to-all-start = ((bf16[8,96,3072]{2,1,0:T(8,128)(2,1)}), bf16[8,96,3072]{2,1,0:T(8,128)(2,1)}, u32[]{:S(2)}, u32[]{:S(2)}) async-start(bf16[8,96,3072]{2,1,0:T(8,128)(2,1)} %bitcast.50), calls=%async_computation | async-start | bytes 9437184 | tf_op jit(solution)/shard_map/all_to_all | solution.py:65
  266.5 10.7 %copy-start.2 = (bf16[768,1344]{0,1:T(8,128)(2,1)}, bf16[768,1344]{0,1:T(8,128)(2,1)S(1)}, u32[]{:S(2)}) copy-start(bf16[768,1344]{0,1:T(8,128)(2,1)S(1)} %get-tuple-element.4) | copy-start | bytes 6193156
  289.9 108.3 %all-to-all-start.2 = ((bf16[8,96,3072]{2,1,0:T(8,128)(2,1)}), bf16[8,96,3072]{2,1,0:T(8,128)(2,1)}, u32[]{:S(2)}, u32[]{:S(2)}) async-start(bf16[8,96,3072]{2,1,0:T(8,128)(2,1)} %bitcast.51), calls=%async_computation.2 | async-start | bytes 9437184 | tf_op jit(solution)/shard_map/all_to_all | solution.py:92
  294.5 144.5 %reduce-scatter.2.cloned.1.call-start = ((), (), s32[]{:S(2)}) async-start(), calls=%async_computation.5 | async-start | bytes 983040 | tf_op jit(solution)/shard_map/reduce_scatter | solution.py:101
  294.6 11.3 %copy-start.4 = (f32[768,1344]{0,1:T(8,128)S(1)}, f32[768,1344]{0,1:T(8,128)}, u32[]{:S(2)}) copy-start(f32[768,1344]{0,1:T(8,128)} %fusion.5) | copy-start | bytes 12386308
  294.6 11.3 %copy-start.5 = (f32[768,1344]{0,1:T(8,128)S(1)}, f32[768,1344]{0,1:T(8,128)}, u32[]{:S(2)}) copy-start(f32[768,1344]{0,1:T(8,128)} %fusion.9) | copy-start | bytes 12386308
  410.2 6.8 %copy-start.3 = (bf16[768,1344]{0,1:T(8,128)(2,1)S(1)}, bf16[768,1344]{0,1:T(8,128)(2,1)}, u32[]{:S(2)}) copy-start(bf16[768,1344]{0,1:T(8,128)(2,1)} %copy-done.2) | copy-start | bytes 6193156
Sparse Core Ops, SparseCore 0:
  42.2 29.5 all-gather.1
  417.1 21.9 reduce-scatter.1
where the time goes:
time: 453 us; the launch traced here: 446 us
  waiting for transfers between devices  267 us (59%)
  matrix products  93.5 us (21%)
  local copies, waits for them, and re-layouts  35.8 us (8%)
  starting transfers between devices  15.8 us (3%)
  between operations  14.4 us (3%)
  blocking collectives  10.3 us (2%)
  other arithmetic  9.73 us (2%)
    all_to_all x1, waiting for transfers between devices, local(): lax.all_to_all(partial_value.reshape(experts, capacity, model_width), 'ep...  81.3 us
    all_to_all x1, waiting for transfers between devices, local(): lax.all_to_all(send_grad.reshape(experts, capacity, full_width), 'ep', sp...  80.6 us
    all_to_all x1, waiting for transfers between devices, local(): lax.all_to_all(send_in.reshape(experts, capacity, full_width), 'ep', spli...  63.4 us
    dot_general x3, matrix products, right_product(): lax.dot_general(left, right, (((1,), (1,)), ((), ())), preferred_element_...  36.6 us
    dot_general x3, matrix products, left_product(): lax.dot_general(left, right, (((0,), (0,)), ((), ())), preferred_element_...  33.5 us
    all_gather x1, waiting for transfers between devices, local(): lax.all_gather(scaled, 'etp', axis=1, tiled=True)  30.2 us
    scatter x2, local copies, waits for them, and re-layouts, place_rows(): jnp.zeros((slot_count, copies.shape[1]), copies.dtype).at[slot_ids]  18.1 us
    gather x2, local copies, waits for them, and re-layouts, local(): returned.reshape(slot_count, model_width)[slot_ids].astype(jnp.float32)  11.9 us
  transfers between devices with their start and end apart: 5, of which 5 were waited for; matrix products, arithmetic and copies ran while one was open for 15% of the time, Pallas kernels for 0%

commit v1 on v0

v1 whole, which is shorter than its diff:
```python
import jax
import jax.numpy as jnp
from jax import lax
from jax.experimental import pallas as pl
from jax.experimental.pallas import tpu as pltpu
from jax.sharding import PartitionSpec as P

VMEM_LIMIT = 58 * 1024 * 1024
CORES = 2
DEPTH = 4
PAIRS = ((0, 1), (2, 3))
EVEN, ODD = (0, 2), (1, 3)
TILES = 3
COLUMN_PARTS = 6
ELEMENT_COLUMNS = 256
ROUTING_ROWS = 16
ANY = pl.BlockSpec(memory_space=pl.ANY)
VMEM = pl.BlockSpec(memory_space=pltpu.VMEM)
SMEM = pl.BlockSpec(memory_space=pltpu.SMEM)


def product(left, right):
    return jnp.dot(left, right, preferred_element_type=jnp.float32)


def left_product(left, right):
    return lax.dot_general(
        left, right, (((0,), (0,)), ((), ())), preferred_element_type=jnp.float32
    )


def half(*shape):
    return jax.ShapeDtypeStruct(shape, jnp.bfloat16)


def full32(*shape):
    return jax.ShapeDtypeStruct(shape, jnp.float32)


def params():
    return pltpu.CompilerParams(vmem_limit_bytes=VMEM_LIMIT)


def shifted(value, axis, stride, count, step):
    step %= count
    if step == 0:
        return value
    pairs = []
    for src in range(lax.axis_size(axis)):
        place = src // stride % count
        pairs.append((src, src + ((place + step) % count - place) * stride))
    return lax.ppermute(value, axis, pairs)


def whole_call(kernel, args, out_shapes, experts=None, after=()):
    moved = sum(a.size * a.dtype.itemsize for a in args)
    moved += sum(o.size * o.dtype.itemsize for o in out_shapes)
    scalars = [] if experts is None else [experts]
    skipped = len(after)

    def body(*refs):
        kernel(*refs[skipped:])

    return pl.pallas_call(
        body,
        in_specs=[ANY] * skipped + [SMEM] * len(scalars) + [VMEM] * len(args),
        out_specs=[VMEM] * len(out_shapes),
        out_shape=out_shapes,
        compiler_params=params(),
        cost_estimate=pl.CostEstimate(flops=0, bytes_accessed=moved, transcendentals=0),
    )(*after, *scalars, *args)


def pack(tokens, probs, expert_ids):
    tok_rows, width = tokens.shape

    def kernel(t_ref, p_ref, id_ref, out_ref):
        out_ref[:tok_rows, :] = t_ref[...]
        rest = p_ref[...]
        rows = [id_ref[...].astype(jnp.float32)]
        for _ in range(3):
            part = rest.astype(jnp.bfloat16).astype(jnp.float32)
            rows.append(part)
            rest = rest - part
        out_ref[tok_rows:, :] = jnp.zeros((ROUTING_ROWS, width), jnp.bfloat16)
        out_ref[tok_rows:, :tok_rows] = jnp.concatenate(rows, axis=0).astype(jnp.bfloat16)

    assert 4 * probs.shape[0] == ROUTING_ROWS
    return whole_call(
        kernel, [tokens, probs, expert_ids], [half(tok_rows + ROUTING_ROWS, width)]
    )[0]


def routes(ref, tok_rows, expert):
    rows = ref[tok_rows:, :tok_rows].astype(jnp.float32)
    top = ROUTING_ROWS // 4
    hit = rows[:top] == expert.astype(jnp.float32)
    weights = rows[top : 2 * top] + rows[2 * top : 3 * top] + rows[3 * top :]
    prob = jnp.sum(jnp.where(hit, weights, 0.0), axis=0, keepdims=True)
    named = jnp.sum(hit.astype(jnp.float32), axis=0, keepdims=True)
    before = lax.broadcasted_iota(jnp.int32, (tok_rows, tok_rows), 0)
    here = lax.broadcasted_iota(jnp.int32, (tok_rows, tok_rows), 1)
    ahead = (before < here).astype(jnp.float32).astype(jnp.bfloat16)
    many = jnp.broadcast_to(named, (8, tok_rows)).astype(jnp.bfloat16)
    pos = product(many, ahead)[:1]
    return jnp.where(named > 0.0, pos, -1.0).astype(jnp.int32), prob


def hits(pos, capacity):
    slots = lax.broadcasted_iota(jnp.int32, (capacity, pos.shape[1]), 0)
    return slots == pos


def one_hot(pos, capacity):
    return hits(pos, capacity).astype(jnp.float32).astype(jnp.bfloat16)


def pick_rows(even_refs, odd_refs, pick_even, pick_odd, capacity, out_refs):
    keep_ref, even_ref, odd_out = out_refs[0], out_refs[1], out_refs[2:]
    blocks, ranges = len(even_refs), len(odd_refs)
    for dx in range(blocks):
        rows = slice(dx * capacity, (dx + 1) * capacity)
        value = pick_even(dx, even_refs[dx])
        keep_ref[rows, :] = value
        even_ref[rows, :] = value
    for dx in range(blocks):
        for dy in range(ranges):
            value = pick_odd(dx, odd_refs[dy])
            if dx == 0:
                start = (blocks + dy) * capacity
                keep_ref[start : start + capacity, :] = value
            else:
                odd_out[dx - 1][dy * capacity : (dy + 1) * capacity, :] = value


def picked_shapes(blocks, ranges, capacity, width):
    shapes = [half((blocks + ranges) * capacity, width), half(blocks * capacity, width)]
    return shapes + [half(ranges * capacity, width)] * (blocks - 1)


def pick_tokens(experts, even, odd, capacity, after):
    blocks, ranges = len(even), len(odd)
    tok_rows, width = even[0].shape[0] - ROUTING_ROWS, even[0].shape[1]

    def kernel(e_ref, *refs):
        even_refs, refs = refs[:blocks], refs[blocks:]
        odd_refs, refs = refs[:ranges], refs[ranges:]
        pos_ref, prob_ref = refs[-2:]
        for dx in range(blocks):
            pos_ref[0, dx], prob_ref[0, dx] = routes(even_refs[dx], tok_rows, e_ref[0])
            pos_ref[1, dx], prob_ref[1, dx] = routes(odd_refs[0], tok_rows, e_ref[dx])
            pos_ref[2, dx], prob_ref[2, dx] = routes(even_refs[0], tok_rows, e_ref[dx])

        def pick(kind):
            def value(dx, ref):
                chosen = one_hot(pos_ref[kind, dx], capacity)
                return product(chosen, ref[:tok_rows, :]).astype(jnp.bfloat16)

            return value

        pick_rows(even_refs, odd_refs, pick(0), pick(1), capacity, refs[:-2])

    shapes = picked_shapes(blocks, ranges, capacity, width)
    shapes += [jax.ShapeDtypeStruct((3, blocks, 1, tok_rows), jnp.int32)]
    shapes += [full32(3, blocks, 1, tok_rows)]
    outs = whole_call(kernel, [*even, *odd], shapes, experts, after)
    return outs[:-2], outs[-2], outs[-1]


def pick_grads(pos, prob, even, odd, capacity, after):
    blocks, ranges = len(even), len(odd)
    width = even[0].shape[1]

    def kernel(pos_ref, prob_ref, *refs):
        even_refs, refs = refs[:blocks], refs[blocks:]
        odd_refs, out_refs = refs[:ranges], refs[ranges:]

        def pick(kind):
            def value(dx, ref):
                hit = hits(pos_ref[kind, dx], capacity)
                weight = jnp.sum(jnp.where(hit, prob_ref[kind, dx], 0.0), axis=1, keepdims=True)
                chosen = hit.astype(jnp.float32).astype(jnp.bfloat16)
                return (weight * product(chosen, ref[...])).astype(jnp.bfloat16)

            return value

        pick_rows(even_refs, odd_refs, pick(0), pick(1), capacity, out_refs)

    shapes = picked_shapes(blocks, ranges, capacity, width)
    return whole_call(kernel, [pos, prob, *even, *odd], shapes, after=after)


def assemble(x_ref, xt_ref, columns, pieces, refs, blocks, ranges, capacity):
    k_rows = blocks * capacity
    for (pair, kind, d, dc), ref in zip(pieces, refs):
        even_at = pair * k_rows
        odd_at = len(EVEN) * k_rows + pair * capacity
        if kind == "even":
            x_ref[even_at : even_at + k_rows, columns(dc, d)] = ref[...]
        elif kind == "odd":
            start = odd_at + d * len(ODD) * capacity
            for dy in range(ranges):
                x_ref[start : start + capacity, columns(dc, dy)] = ref[
                    dy * capacity : (dy + 1) * capacity, :
                ]
        else:
            x_ref[even_at : even_at + k_rows, columns(dc, 0)] = ref[:k_rows, :]
            for dy in range(ranges):
                x_ref[odd_at : odd_at + capacity, columns(dc, dy)] = ref[
                    k_rows + dy * capacity : k_rows + (dy + 1) * capacity, :
                ]
    part = x_ref.shape[1] // COLUMN_PARTS
    for n in range(COLUMN_PARTS):
        at = slice(n * part, (n + 1) * part)
        xt_ref[at, :] = x_ref[:, at].T


def fixed(a):
    return pl.BlockSpec(a.shape, lambda f, *_: (0,) * a.ndim)


def gate_units(order, names, pieces, weight, blocks, ranges, capacity, after):
    ff, full = weight.shape
    tile, rows, width = ff // TILES, DEPTH * blocks * capacity, pieces[0].shape[1]
    n_in = len(pieces)

    def kernel(order_ref, *refs):
        in_refs, w_ref = refs[:n_in], refs[n_in]
        x_out, xt_out, gate_ref, x_ref, xt_ref, sems = refs[n_in + 1 + len(after) :]
        step = pl.program_id(0)
        saved = [
            pltpu.make_async_copy(x_ref, x_out, sems.at[0]),
            pltpu.make_async_copy(xt_ref, xt_out, sems.at[1]),
        ]

        def columns(dc, dy):
            at = order_ref[dc * ranges + dy] * width
            return pl.ds(pl.multiple_of(at, width), width)

        @pl.when(step == 0)
        def _():
            assemble(x_ref, xt_ref, columns, names, in_refs, blocks, ranges, capacity)
            for copy in saved:
                copy.start()

        gate_ref[...] = product(w_ref[...], xt_ref[...])

        @pl.when(step == TILES - 1)
        def _():
            for copy in saved:
                copy.wait()

    return pl.pallas_call(
        kernel,
        grid_spec=pltpu.PrefetchScalarGridSpec(
            num_scalar_prefetch=1,
            grid=(TILES,),
            in_specs=[fixed(a) for a in pieces]
            + [pl.BlockSpec((tile, full), lambda f, _: (f, 0))]
            + [ANY] * len(after),
            out_specs=[ANY, ANY, pl.BlockSpec((tile, rows), lambda f, _: (f, 0))],
            scratch_shapes=[
                pltpu.VMEM((rows, full), jnp.bfloat16),
                pltpu.VMEM((full, rows), jnp.bfloat16),
                pltpu.SemaphoreType.DMA((2,)),
            ],
        ),
        out_shape=[half(rows, full), half(full, rows), full32(ff, rows)],
        compiler_params=params(),
        cost_estimate=pl.CostEstimate(
            flops=2 * rows * ff * full,
            bytes_accessed=2 * ff * full + 6 * rows * full + 4 * rows * ff,
            transcendentals=0,
        ),
    )(order, *pieces, weight, *after)


def up_units(x_t, weight, after):
    ff, full = weight.shape
    tile, rows = ff // TILES, x_t.shape[1]

    def kernel(w_ref, xt_ref, *refs):
        refs[-1][...] = product(w_ref[...], xt_ref[...])

    return pl.pallas_call(
        kernel,
        grid=(TILES,),
        in_specs=[pl.BlockSpec((tile, full), lambda f: (f, 0)), fixed(x_t)] + [ANY] * len(after),
        out_specs=pl.BlockSpec((tile, rows), lambda f: (f, 0)),
        out_shape=full32(ff, rows),
        compiler_params=params(),
        cost_estimate=pl.CostEstimate(
            flops=2 * rows * ff * full,
            bytes_accessed=2 * ff * full + 2 * rows * full + 4 * rows * ff,
            transcendentals=0,
        ),
    )(weight, x_t, *after)


def hidden_units(order, names, pieces, weight, gate, up, blocks, ranges, capacity, after):
    ff, full = weight.shape
    tile, rows, width = ff // TILES, gate.shape[1], pieces[0].shape[1]
    n_in = len(pieces)

    def kernel(order_ref, *refs):
        in_refs, refs = refs[:n_in], refs[n_in:]
        w_ref, gate_ref, up_ref = refs[:3]
        g_out, hid_ref, gpg_ref, gpu_ref, g_ref, gt_ref, sem = refs[3 + len(after) :]
        step = pl.program_id(0)
        saved = pltpu.make_async_copy(g_ref, g_out, sem)

        def columns(dc, dy):
            at = order_ref[dc * ranges + dy] * width
            return pl.ds(pl.multiple_of(at, width), width)

        @pl.when(step == 0)
        def _():
            assemble(g_ref, gt_ref, columns, names, in_refs, blocks, ranges, capacity)
            saved.start()

        for n in range(0, rows, ELEMENT_COLUMNS):
            at = slice(n, min(n + ELEMENT_COLUMNS, rows))
            grad_hidden = product(w_ref[...], gt_ref[:, at])
            gate_pre, up_pre = gate_ref[:, at], up_ref[:, at]
            sig = jax.nn.sigmoid(gate_pre)
            silu = gate_pre * sig
            hid_ref[:, at] = (silu * up_pre).astype(jnp.bfloat16)
            gpg_ref[:, at] = (
                grad_hidden * up_pre * sig * (1.0 + gate_pre * (1.0 - sig))
            ).astype(jnp.bfloat16)
            gpu_ref[:, at] = (grad_hidden * silu).astype(jnp.bfloat16)

        @pl.when(step == TILES - 1)
        def _():
            saved.wait()

    by_tile = pl.BlockSpec((tile, rows), lambda f, _: (f, 0))
    return pl.pallas_call(
        kernel,
        grid_spec=pltpu.PrefetchScalarGridSpec(
            num_scalar_prefetch=1,
            grid=(TILES,),
            in_specs=[fixed(a) for a in pieces]
            + [pl.BlockSpec((tile, full), lambda f, _: (f, 0)), by_tile, by_tile]
            + [ANY] * len(after),
            out_specs=[ANY, by_tile, by_tile, by_tile],
            scratch_shapes=[
                pltpu.VMEM((rows, full), jnp.bfloat16),
                pltpu.VMEM((full, rows), jnp.bfloat16),
                pltpu.SemaphoreType.DMA,
            ],
        ),
        out_shape=[half(rows, full)] + [half(ff, rows)] * 3,
        compiler_params=params(),
        cost_estimate=pl.CostEstimate(
            flops=2 * rows * ff * full,
            bytes_accessed=2 * ff * full + 4 * rows * full + 14 * rows * ff,
            transcendentals=rows * ff,
        ),
    )(order, *pieces, weight, gate, up, *after)


def partials(order, dc, lefts, weights, ranges, turn, after):
    ff, full = weights[0].shape
    rows = lefts[0].shape[1 if turn else 0]
    width = full // (CORES * ranges)

    def kernel(order_ref, lg_ref, lu_ref, wg_ref, wu_ref, *refs):
        refs = refs[len(after) :]
        if turn:

            @pl.when(pl.program_id(0) == 0)
            def _():
                refs[1][...] = lg_ref[...].T
                refs[2][...] = lu_ref[...].T

            lg_ref, lu_ref = refs[1:]
        value = product(lg_ref[...], wg_ref[...]) + product(lu_ref[...], wu_ref[...])
        refs[0][0] = value.astype(jnp.bfloat16)

    right = pl.BlockSpec((ff, width), lambda r, order: (0, order[dc * ranges + r]))
    turned = pl.BlockSpec((rows, ff), lambda r, _: (0, 0))
    return pl.pallas_call(
        kernel,
        grid_spec=pltpu.PrefetchScalarGridSpec(
            num_scalar_prefetch=1,
            grid=(ranges,),
            in_specs=[fixed(a) for a in lefts] + [right, right] + [ANY] * len(after),
            out_specs=[pl.BlockSpec((1, rows, width), lambda r, _: (r, 0, 0))]
            + [turned] * (2 * turn),
        ),
        out_shape=[half(ranges, rows, width)] + [half(rows, ff)] * (2 * turn),
        compiler_params=params(),
        cost_estimate=pl.CostEstimate(
            flops=4 * rows * ff * full // CORES,
            bytes_accessed=2 * ff * full + 2 * rows * full + 6 * rows * ff,
            transcendentals=0,
        ),
    )(order, *lefts, *weights[:2], *after)


def weight_grad(left, right, after):
    ff, rows = left.shape
    full = right.shape[1]
    part = full // COLUMN_PARTS

    def kernel(left_ref, right_ref, *refs):
        refs[-1][...] = product(left_ref[...], right_ref[...]).astype(jnp.bfloat16)

    return pl.pallas_call(
        kernel,
        grid=(COLUMN_PARTS,),
        in_specs=[fixed(left), pl.BlockSpec((rows, part), lambda n: (0, n))] + [ANY] * len(after),
        out_specs=pl.BlockSpec((ff, part), lambda n: (0, n)),
        out_shape=half(ff, full),
        compiler_params=params(),
        cost_estimate=pl.CostEstimate(
            flops=2 * rows * ff * full,
            bytes_accessed=2 * (rows * ff + full * (ff + rows)),
            transcendentals=0,
        ),
    )(left, right, *after)


def first_returns(own, other, blocks, capacity):
    ranges = own.shape[0]
    evens, odds = len(EVEN) * blocks * capacity, len(ODD) * capacity

    def total(at):
        value = own[at].astype(jnp.float32) + other[at].astype(jnp.float32)
        return value.astype(jnp.bfloat16)

    even = [total((dy, slice(0, evens))) for dy in range(ranges)]
    odd = [
        total((slice(None), slice(evens + dx * odds, evens + (dx + 1) * odds)))
        for dx in range(blocks)
    ]
    return even, odd


def spread(pos, rows):
    return left_product(one_hot(pos, rows.shape[0]), rows)


def second_returns(positions, even, odd, capacity, after):
    ranges, blocks = len(even), len(odd)
    tok_rows, width = positions[0].shape[3], even[0].shape[1]

    def kernel(*refs):
        pos_refs, refs = refs[: len(PAIRS)], refs[len(PAIRS) :]
        even_refs, refs = refs[:ranges], refs[ranges:]
        odd_refs, out_refs = refs[:blocks], refs[blocks:]
        for i in range(len(EVEN)):
            for dx in range(blocks):
                start = (i * blocks + dx) * capacity
                value = even_refs[0][start : start + capacity, :].astype(jnp.float32)
                for dy in range(1, ranges):
                    value += even_refs[dy][start : start + capacity, :].astype(jnp.float32)
                out_refs[dx][i * capacity : (i + 1) * capacity, :] = value.astype(jnp.bfloat16)
        for i in range(len(ODD)):
            rows = slice(i * capacity, (i + 1) * capacity)
            for dy in range(ranges):
                value = spread(pos_refs[i][1, 0], odd_refs[0][dy, rows, :])
                for dx in range(1, blocks):
                    value += spread(pos_refs[i][1, dx], odd_refs[dx][dy, rows, :])
                out_refs[blocks + dy][i * tok_rows : (i + 1) * tok_rows, :] = value.astype(
                    jnp.bfloat16
                )

    shapes = [half(len(EVEN) * capacity, width)] * blocks
    shapes += [half(len(ODD) * tok_rows, width)] * ranges
    outs = whole_call(kernel, [*positions, *even, *odd], shapes, after=after)
    return outs[:blocks], outs[blocks:]


def third_returns(positions, even, odd, capacity, after):
    blocks, ranges = len(even), len(odd)
    tok_rows, width = positions[0].shape[3], even[0].shape[1]

    def kernel(*refs):
        pos_refs, refs = refs[: len(PAIRS)], refs[len(PAIRS) :]
        even_refs, refs = refs[:blocks], refs[blocks:]
        odd_refs, out_refs = refs[:ranges], refs[ranges:]
        for i, k in enumerate(EVEN):
            rows = slice(i * capacity, (i + 1) * capacity)
            value = spread(pos_refs[i][2, 0], even_refs[0][rows, :])
            for dx in range(1, blocks):
                value += spread(pos_refs[i][2, dx], even_refs[dx][rows, :])
            out_refs[k][...] = value.astype(jnp.bfloat16)
        for i, k in enumerate(ODD):
            rows = slice(i * tok_rows, (i + 1) * tok_rows)
            value = odd_refs[0][rows, :].astype(jnp.float32)
            for dy in range(1, ranges):
                value += odd_refs[dy][rows, :].astype(jnp.float32)
            out_refs[k][...] = value.astype(jnp.bfloat16)

    return whole_call(
        kernel, [*positions, *even, *odd], [half(tok_rows, width)] * DEPTH, after=after
    )


def add_up(parts):
    value = parts[0].astype(jnp.float32)
    for part in parts[1:]:
        value += part.astype(jnp.float32)
    return value.astype(jnp.bfloat16)


def ordered(value, after):
    return lax.optimization_barrier((value, tuple(after)))[0] if after else value


def local(tokens, grad_out, probs, expert_ids, w_gate, w_up, w_down):
    experts, etp = lax.axis_size("ep"), lax.axis_size("etp")
    blocks, ranges = experts // DEPTH, etp // CORES
    tok_rows, top_count = expert_ids.shape
    capacity = 3 * tok_rows * top_count // (2 * experts)
    me, mine = lax.axis_index("ep"), lax.axis_index("etp")
    my_z, my_x = me // blocks, me % blocks
    my_y, my_c = mine // CORES, mine % CORES

    def along_z(value, step):
        return shifted(value, "ep", blocks, DEPTH, step)

    def along_x(value, step):
        return shifted(value, "ep", 1, blocks, step)

    def along_y(value, step):
        return shifted(value, "etp", CORES, ranges, step)

    def along_c(value, step):
        return shifted(value, "etp", 1, CORES, step)

    own_experts = jnp.stack([my_z * blocks + (my_x + dx) % blocks for dx in range(blocks)])
    own_experts = own_experts.astype(jnp.int32)
    order = [
        (my_y - dy) % ranges * CORES + (my_c - dc) % CORES
        for dc in range(CORES)
        for dy in range(ranges)
    ]
    order = jnp.stack(order).astype(jnp.int32)
    weights = (w_gate[0].T, w_up[0].T, w_down[0])

    def first_hops(line):
        even = [[along_x(line[k], dx) for dx in range(blocks)] for k in EVEN]
        odd = [[along_y(line[k], dy) for dy in range(ranges)] for k in ODD]
        return list(zip(even, odd))

    def second_hops(outs):
        keep, even, odd = outs[0], outs[1], outs[2:]
        names, arrays = [("keep", 0)], [keep]
        for dy in range(1, ranges):
            names.append(("even", dy))
            arrays.append(along_y(even, dy))
        for dx in range(1, blocks):
            names.append(("odd", dx))
            arrays.append(along_x(odd[dx - 1], dx))
        return names, arrays

    def core_hops(hopped):
        names, arrays = [], []
        for pair, (kinds, values) in enumerate(hopped):
            for (kind, d), value in zip(kinds, values):
                for dc in range(CORES):
                    names.append((pair, kind, d, dc))
                    arrays.append(along_c(value, dc))
        return names, arrays

    packed = pack(tokens, probs.T, expert_ids.T)
    t_line = [along_z(packed, k) for k in range(DEPTH)]
    positions, weightings = [], []

    def picked_tokens(held, after):
        outs, pos, prob = pick_tokens(own_experts, *held, capacity, after)
        positions.append(pos)
        weightings.append(prob)
        return second_hops(outs), (outs[0],)

    t_near, after = picked_tokens(first_hops(t_line)[0], ())
    t_line = [ordered(t, after if k in PAIRS[1] else ()) for k, t in enumerate(t_line)]
    g_line = [grad_out] + [along_z(ordered(grad_out, after), k) for k in range(1, DEPTH)]
    g_near_held = first_hops(g_line)[0]
    after = (*t_near[1][1:], *g_near_held[0][1:], *g_near_held[1][1:])
    t_far, after = picked_tokens(first_hops(t_line)[1], after)
    t_names, t_pieces = core_hops([t_near, t_far])
    after += tuple(t_far[1][1:])
    g_line = [ordered(g, after if k in PAIRS[1] else ()) for k, g in enumerate(g_line)]
    g_first = [g_near_held, first_hops(g_line)[1]]
    sizes = (blocks, ranges, capacity)

    def picked_grads(pair, after):
        outs = pick_grads(positions[pair], weightings[pair], *g_first[pair], capacity, after)
        return second_hops(outs), (outs[0],)

    g_near, after = picked_grads(0, after)
    after += tuple(g_line[k] for k in PAIRS[1])
    x_all, x_t, gate = gate_units(order, t_names, t_pieces, weights[0], *sizes, after)
    g_far, after = picked_grads(1, (gate,))
    up = up_units(x_t, weights[1], after)
    g_names, g_pieces = core_hops([g_near, g_far])
    g_all, hidden, grad_pre_gate, grad_pre_up = hidden_units(
        order, g_names, g_pieces, weights[2], gate, up, *sizes, ()
    )
    other, *lefts = partials(order, 1, (grad_pre_gate, grad_pre_up), weights, ranges, True, ())
    (own,) = partials(order, 0, lefts, weights, ranges, False, ())

    even, odd = first_returns(own, along_c(other, -1), blocks, capacity)
    after = (*even, *odd)
    even = [along_y(a, -dy) for dy, a in enumerate(even)]
    odd = [along_x(a, -dx) for dx, a in enumerate(odd)]
    grad_down = weight_grad(hidden, g_all, after)
    even, odd = second_returns(positions, even, odd, capacity, (grad_down,))
    after = (*even, *odd)
    even = [along_x(a, -dx) for dx, a in enumerate(even)]
    odd = [along_y(a, -dy) for dy, a in enumerate(odd)]
    grad_gate = weight_grad(grad_pre_gate, x_all, after)
    third = third_returns(positions, even, odd, capacity, (grad_gate,))
    grad_up = weight_grad(grad_pre_up, x_all, tuple(third))
    returned = [along_z(a, -k) for k, a in enumerate(third)]
    grad_tokens = add_up(returned)
    return (grad_tokens, grad_gate.T[None], grad_up.T[None], grad_down[None])


def solution(mesh):
    return jax.shard_map(
        local,
        mesh=mesh,
        in_specs=(
            P("ep", "etp"),
            P("ep", "etp"),
            P("ep", None),
            P("ep", None),
            P("ep", None, "etp"),
            P("ep", None, "etp"),
            P("ep", "etp", None),
        ),
        out_specs=(
            P("ep", "etp"),
            P("ep", None, "etp"),
            P("ep", None, "etp"),
            P("ep", "etp", None),
        ),
        check_vma=False,
    )
```

time: 453 us -> 209 us (0.46); the launches traced: 446 us -> 208 us
  waiting for transfers between devices: 267 us -> 41.3 us
  Pallas kernels: 0 us -> 120 us
  matrix products: 93.5 us -> 0 us
  local copies, waits for them, and re-layouts: 35.8 us -> 6.74 us
  starting transfers between devices: 15.8 us -> 33.9 us
  between operations: 14.4 us -> 0.98 us
  blocking collectives: 10.3 us -> 0 us
    all_to_all x3 -> x0, waiting for transfers between devices: 225 us -> none  [the longest x1 81.3 us: local(): lax.all_to_all(partial_value.reshape(experts, capacity, model_width), 'ep...]
    pallas_call x0 -> x15, Pallas kernels: none -> 120 us  [the longest x3 33.8 us: weight_grad(): pl.pallas_call(kernel, grid=(COLUMN_PARTS,), in_specs=[fixed(left), pl.Bl...]
    dot_general x8 -> x0, matrix products: 93.5 us -> none  [the longest x3 36.6 us: right_product(): lax.dot_general(left, right, (((1,), (1,)), ((), ())), preferred_element_...]
    ppermute x0 -> x42, waiting for transfers between devices: none -> 41.3 us  [shifted(): return lax.ppermute(value, axis, pairs)]
    ppermute x0 -> x42, starting transfers between devices: none -> 33.9 us  [shifted(): return lax.ppermute(value, axis, pairs)]
    all_gather x1 -> x0, waiting for transfers between devices: 30.2 us -> none  [local(): lax.all_gather(scaled, 'etp', axis=1, tiled=True)]
    scatter x2 -> x0, local copies, waits for them, and re-layouts: 18.1 us -> none  [place_rows(): jnp.zeros((slot_count, copies.shape[1]), copies.dtype).at[slot_ids]]
    all_to_all x3 -> x0, starting transfers between devices: 15.5 us -> none  [the longest x1 5.94 us: local(): lax.all_to_all(send_in.reshape(experts, capacity, full_width), 'ep', spli...]
  transfers between devices with their start and end apart: 5 -> 42, of which waited for: 5 -> 14; matrix products, arithmetic and copies ran while one was open for 15% -> 1% of each run, Pallas kernels for 0% -> 39%
where the time goes in v1:
time: 209 us; the launch traced here: 208 us
  Pallas kernels  120 us (57%)
  waiting for transfers between devices  41.3 us (20%)
  starting transfers between devices  33.9 us (16%)
  local copies, waits for them, and re-layouts  6.74 us (3%)
  other arithmetic  5.63 us (3%)
    ppermute x42, waiting for transfers between devices, shifted(): return lax.ppermute(value, axis, pairs)  41.3 us
    ppermute x42, starting transfers between devices, shifted(): return lax.ppermute(value, axis, pairs)  33.9 us
    pallas_call x3, Pallas kernels, weight_grad(): pl.pallas_call(kernel, grid=(COLUMN_PARTS,), in_specs=[fixed(left), pl.Bl...  33.8 us
    pallas_call x2, Pallas kernels, partials(): pl.pallas_call(kernel, grid_spec=pltpu.PrefetchScalarGridSpec(num_scalar_...  27.1 us
    pallas_call x7, Pallas kernels, whole_call(): pl.pallas_call(body, in_specs=[ANY] * skipped + [SMEM] * len(scalars) + [...  17.8 us
    pallas_call x1, Pallas kernels, hidden_units(): pl.pallas_call(kernel, grid_spec=pltpu.PrefetchScalarGridSpec(num_scalar_...  16.4 us
    pallas_call x1, Pallas kernels, gate_units(): pl.pallas_call(kernel, grid_spec=pltpu.PrefetchScalarGridSpec(num_scalar_...  13.5 us
    pallas_call x1, Pallas kernels, up_units(): pl.pallas_call(kernel, grid=(TILES,), in_specs=[pl.BlockSpec((tile, full)...  11.2 us
  transfers between devices with their start and end apart: 42, of which 14 were waited for; matrix products, arithmetic and copies ran while one was open for 1% of the time, Pallas kernels for 39%

profile of v1, /device:TPU:0, one launch (start us, length us, event | category | flops | bytes accessed | tf_op | source)
XLA Modules:
  0.0 208.4 jit_solution(2480334397235845531)
XLA Ops:
  0.6 1.6 shard_map.102.refs_1_
  2.3 3.0 %collective-permute-start.1 = (bf16[144,768]{1,0:T(8,128)(2,1)}, bf16[144,768]{1,0:T(8,128)(2,1)S(1)}, u32[]{:S(2)}, u32[]{:S(2)}) collective-permute-start(bf16[144,768]{1,0:T(8,128)(2,1)} %shard_map.102.refs_1_), channel_id=1, source_target_pairs={{0,8},{4,12},{8,16},{12,20},{16,24},{20,28},{24,0},{28,4},{1,9},{5... | collective-permute-start | bytes 663560 | tf_op jit(solution)/shard_map/ppermute | solution.py:52
  6.8 6.2 %collective-permute-done.1.refs_3_ = bf16[144,768]{1,0:T(8,128)(2,1)S(1)} collective-permute-done((bf16[144,768]{1,0:T(8,128)(2,1)}, bf16[144,768]{1,0:T(8,128)(2,1)S(1)}, u32[]{:S(2)}, u32[]{:S(2)}) %collective-permute-start.1) | collective-permute-done | bytes 221216 | tf_op jit(solution)/shard_map/ppermute | solution.py:52
  13.0 1.5 collective-permute-start.2
  14.5 1.7 collective-permute-start.10
  20.3 2.7 %shard_map.103 = (bf16[384,768]{1,0:T(8,128)(2,1)}, bf16[192,768]{1,0:T(8,128)(2,1)}, bf16[192,768]{1,0:T(8,128)(2,1)}, s32[3,2,1,128]{3,2,1,0:T(1,128)}, f32[3,2,1,128]{3,2,1,0:T(1,128)}) custom-call(s32[2]{0:T(128)} %pad_add_fusion.1.refs_0_.refs_4_, bf16[144,768]{1,0:T(8,128)(2,1)} %shard_map.102.refs_1_, bf16[144,768]{1,0:T(8,128)(2,1)} %copy-done.14, ...), custom_call_target="tpu_custom_call" | custom-call | bytes 2070528 | tf_op jit(solution)/shard_map/pallas_call | solution.py:64
  24.3 5.1 %collective-permute-done.8.refs_5_ = bf16[144,768]{1,0:T(8,128)(2,1)S(1)} collective-permute-done((bf16[144,768]{1,0:T(8,128)(2,1)}, bf16[144,768]{1,0:T(8,128)(2,1)S(1)}, u32[]{:S(2)}, u32[]{:S(2)}) %collective-permute-start.8) | collective-permute-done | bytes 221216 | tf_op jit(solution)/shard_map/ppermute | solution.py:52
  29.3 1.5 collective-permute-start.9
  32.8 5.9 %collective-permute-done.6.refs_7_ = bf16[128,768]{1,0:T(8,128)(2,1)S(1)} collective-permute-done((bf16[128,768]{1,0:T(8,128)(2,1)}, bf16[128,768]{1,0:T(8,128)(2,1)S(1)}, u32[]{:S(2)}, u32[]{:S(2)}) %collective-permute-start.6) | collective-permute-done | bytes 196640 | tf_op jit(solution)/shard_map/ppermute | solution.py:52
  39.2 1.7 collective-permute-start.26
  41.6 2.8 %collective-permute-done.7.refs_3_.refs_8_ = bf16[128,768]{1,0:T(8,128)(2,1)S(1)} collective-permute-done((bf16[128,768]{1,0:T(8,128)(2,1)S(1)}, bf16[128,768]{1,0:T(8,128)(2,1)S(1)}, u32[]{:S(2)}, u32[]{:S(2)}) %collective-permute-start.7) | collective-permute-done | bytes 196640 | tf_op jit(solution)/shard_map/ppermute | solution.py:52
  45.2 2.6 %shard_map.104 = (bf16[384,768]{1,0:T(8,128)(2,1)}, bf16[192,768]{1,0:T(8,128)(2,1)}, bf16[192,768]{1,0:T(8,128)(2,1)}, s32[3,2,1,128]{3,2,1,0:T(1,128)}, f32[3,2,1,128]{3,2,1,0:T(1,128)}) custom-call(bf16[192,768]{1,0:T(8,128)(2,1)} %copy-done.9, bf16[192,768]{1,0:T(8,128)(2,1)} %copy-done.10, bf16[128,768]{1,0:T(8,128)(2,1)} %copy-done.1, ...), custom_call_target="tpu_custom_call" | custom-call | bytes 2070528 | tf_op jit(solution)/shard_map/pallas_call | solution.py:64
  48.8 3.2 %collective-permute-done.25.refs_14_.refs_3_ = bf16[128,768]{1,0:T(8,128)(2,1)S(1)} collective-permute-done((bf16[128,768]{1,0:T(8,128)(2,1)}, bf16[128,768]{1,0:T(8,128)(2,1)S(1)}, u32[]{:S(2)}, u32[]{:S(2)}) %collective-permute-start.25) | collective-permute-done | bytes 196640 | tf_op jit(solution)/shard_map/ppermute | solution.py:52
  52.5 2.3 %collective-permute-done.12.refs_1_.refs_8_ = bf16[192,768]{1,0:T(8,128)(2,1)S(1)} collective-permute-done((bf16[192,768]{1,0:T(8,128)(2,1)}, bf16[192,768]{1,0:T(8,128)(2,1)S(1)}, u32[]{:S(2)}, u32[]{:S(2)}) %collective-permute-start.12) | collective-permute-done | bytes 294944 | tf_op jit(solution)/shard_map/ppermute | solution.py:52
  56.7 2.5 %shard_map.105 = (bf16[384,768]{1,0:T(8,128)(2,1)}, bf16[192,768]{1,0:T(8,128)(2,1)}, bf16[192,768]{1,0:T(8,128)(2,1)}) custom-call(bf16[384,768]{1,0:T(8,128)(2,1)} %get-tuple-element.49.refs_0_.refs_6_, bf16[192,768]{1,0:T(8,128)(2,1)} %copy-done.11, bf16[192,768]{1,0:T(8,128)(2,1)} %copy-done.12, s32[3,2,1,128]{3,2,1,0:T(1,128)} %get-tuple-element.52.refs_3_.refs_1_, ...), custom_call_target="tpu_custom_call" | custom-call | bytes 1972224 | tf_op jit(solution)/shard_map/pallas_call | solution.py:64
  64.2 13.5 %shard_map.106 = (bf16[768,3072]{1,0:T(8,128)(2,1)}, bf16[3072,768]{1,0:T(8,128)(2,1)}, f32[1344,768]{1,0:T(8,128)}) custom-call(s32[4]{0:T(128)} %pad_add_fusion.order_ref, bf16[384,768]{1,0:T(8,128)(2,1)} %get-tuple-element.45.refs_0_, bf16[384,768]{1,0:T(8,128)(2,1)} %copy-done.26, bf16[192,768]{1,0:T(8,128)(2,1)} %copy-done.9, ...), custom_call_target="tpu_custom_call" | custom-call | flops 6341787648 | bytes 26542080 | tf_op jit(solution)/shard_map/pallas_call | solution.py:253
  78.5 2.5 %shard_map.107 = (bf16[384,768]{1,0:T(8,128)(2,1)}, bf16[192,768]{1,0:T(8,128)(2,1)}, bf16[192,768]{1,0:T(8,128)(2,1)}) custom-call(f32[1344,768]{1,0:T(8,128)} %get-tuple-element.59.refs_0_.refs_13_, s32[3,2,1,128]{3,2,1,0:T(1,128)} %get-tuple-element.60.refs_1_.refs_2_, f32[3,2,1,128]{3,2,1,0:T(1,128)} %get-tuple-element.61.refs_2_, ...), custom_call_target="tpu_custom_call" | custom-call | bytes 1972224 | tf_op jit(solution)/shard_map/pallas_call | solution.py:64
  83.4 6.0 %collective-permute-done.30.refs_8_ = bf16[192,768]{1,0:T(8,128)(2,1)S(1)} collective-permute-done((bf16[192,768]{1,0:T(8,128)(2,1)}, bf16[192,768]{1,0:T(8,128)(2,1)S(1)}, u32[]{:S(2)}, u32[]{:S(2)}) %collective-permute-start.30) | collective-permute-done | bytes 294944 | tf_op jit(solution)/shard_map/ppermute | solution.py:52
  90.3 11.2 %shard_map.108.refs_14_ = f32[1344,768]{1,0:T(8,128)} custom-call(bf16[1344,3072]{1,0:T(8,128)(2,1)} %bitcast.34, bf16[3072,768]{1,0:T(8,128)(2,1)} %get-tuple-element.65.xt_ref, bf16[384,768]{1,0:T(8,128)(2,1)} %get-tuple-element.62.refs_0_.refs_6_), custom_call_target="tpu_custom_call" | custom-call | flops 6341787648 | bytes 17104896 | tf_op jit(solution)/shard_map/pallas_call | solution.py:285
  102.9 16.4 %shard_map.109 = (bf16[768,3072]{1,0:T(8,128)(2,1)}, bf16[1344,768]{1,0:T(8,128)(2,1)}, bf16[1344,768]{1,0:T(8,128)(2,1)}, bf16[1344,768]{1,0:T(8,128)(2,1)}) custom-call(s32[4]{0:T(128)} %pad_add_fusion.order_ref, bf16[384,768]{1,0:T(8,128)(2,1)} %get-tuple-element.54.refs_13_.refs_0_, bf16[384,768]{1,0:T(8,128)(2,1)} %copy-done.29, ...), custom_call_target="tpu_custom_call" | custom-call | flops 6341787648 | bytes 32145408 | tf_op jit(solution)/shard_map/pallas_call | solution.py:338
  119.3 14.2 %shard_map.110 = (bf16[2,768,768]{2,1,0:T(8,128)(2,1)}, bf16[768,1344]{1,0:T(8,128)(2,1)}, bf16[768,1344]{1,0:T(8,128)(2,1)}) custom-call(s32[4]{0:T(128)} %pad_add_fusion.order_ref, bf16[1344,768]{1,0:T(8,128)(2,1)} %get-tuple-element.66.lg_ref.left_ref, bf16[1344,768]{1,0:T(8,128)(2,1)} %get-tuple-element.70.lu_ref.left_ref, bf16[1344,3072]{1,0:T(8,128)(2,1)} %bitcast.32, ...), custom_call_target="tpu_custom_call" | custom-call | flops 6341787648 | bytes 19169280 | tf_op jit(solution)/shard_map/pallas_call | solution.py:383
  133.6 12.9 %shard_map.111 = bf16[2,768,768]{2,1,0:T(8,128)(2,1)} custom-call(s32[4]{0:T(128)} %pad_add_fusion.order_ref, bf16[768,1344]{1,0:T(8,128)(2,1)} %get-tuple-element.71.lg_ref, bf16[768,1344]{1,0:T(8,128)(2,1)} %get-tuple-element.72.lu_ref, bf16[1344,3072]{1,0:T(8,128)(2,1)} %bitcast.33, bf16[1344,3072]{1,0:T(8,128)(2,1)} %bitcast.36), custom_call_target="tpu_custom_call" | custom-call | flops 6341787648 | bytes 19169280 | tf_op jit(solution)/shard_map/pallas_call | solution.py:383
  146.5 2.5 %add_convert_fusion = (bf16[2,192,768]{2,1,0:T(8,128)(2,1)S(1)}, bf16[2,192,768]{2,1,0:T(8,128)(2,1)}) fusion(bf16[2,768,768]{2,1,0:T(8,128)(2,1)S(1)} %collective-permute-done.34, bf16[2,768,768]{2,1,0:T(8,128)(2,1)} %shard_map.111), kind=kLoop, calls=%fused_computation | loop fusion | flops 2359296 | bytes 3538944 | tf_op jit(solution)/shard_map/convert_element_type | solution.py:431
  152.0 11.3 %shard_map.112.refs_0_ = bf16[1344,3072]{1,0:T(8,128)(2,1)} custom-call(bf16[1344,768]{1,0:T(8,128)(2,1)} %get-tuple-element.68.left_ref, bf16[768,3072]{1,0:T(8,128)(2,1)} %get-tuple-element.69.right_ref, bf16[384,768]{1,0:T(8,128)(2,1)} %get-tuple-element.85.refs_0_.refs_3_, bf16[384,768]{1,0:T(8,128)(2,1)} %copy-done.4, ...), custom_call_target="tpu_custom_call" | custom-call | flops 6341787648 | bytes 15040512 | tf_op jit(solution)/shard_map/pallas_call | solution.py:410
  164.6 1.9 collective-permute-done.35.refs_4_
  167.3 3.4 %shard_map.113 = (bf16[192,768]{1,0:T(8,128)(2,1)}, bf16[192,768]{1,0:T(8,128)(2,1)}, bf16[256,768]{1,0:T(8,128)(2,1)}, bf16[256,768]{1,0:T(8,128)(2,1)}) custom-call(bf16[1344,3072]{1,0:T(8,128)(2,1)} %shard_map.112.refs_0_, s32[3,2,1,128]{3,2,1,0:T(1,128)} %get-tuple-element.52.refs_3_.refs_1_, s32[3,2,1,128]{3,2,1,0:T(1,128)} %get-tuple-element.60.refs_1_.refs_2_, ...), custom_call_target="tpu_custom_call" | custom-call | bytes 3741696 | tf_op jit(solution)/shard_map/pallas_call | solution.py:64
  173.0 11.3 %shard_map.114.refs_0_ = bf16[1344,3072]{1,0:T(8,128)(2,1)} custom-call(bf16[1344,768]{1,0:T(8,128)(2,1)} %get-tuple-element.66.lg_ref.left_ref, bf16[768,3072]{1,0:T(8,128)(2,1)} %get-tuple-element.67.right_ref, bf16[192,768]{1,0:T(8,128)(2,1)} %get-tuple-element.74.refs_0_.refs_3_, bf16[192,768]{1,0:T(8,128)(2,1)} %get-tuple-element.75.refs_1_, ...), custom_call_target="tpu_custom_call" | custom-call | flops 6341787648 | bytes 15040512 | tf_op jit(solution)/shard_map/pallas_call | solution.py:410
  185.7 2.5 %shard_map.115 = (bf16[128,768]{1,0:T(8,128)(2,1)}, bf16[128,768]{1,0:T(8,128)(2,1)}, bf16[128,768]{1,0:T(8,128)(2,1)}, bf16[128,768]{1,0:T(8,128)(2,1)}) custom-call(bf16[1344,3072]{1,0:T(8,128)(2,1)} %shard_map.114.refs_0_, s32[3,2,1,128]{3,2,1,0:T(1,128)} %get-tuple-element.52.refs_3_.refs_1_, s32[3,2,1,128]{3,2,1,0:T(1,128)} %get-tuple-element.60.refs_1_.refs_2_, ...), custom_call_target="tpu_custom_call" | custom-call | bytes 2168832 | tf_op jit(solution)/shard_map/pallas_call | solution.py:64
  188.2 3.1 %collective-permute-start.39 = (bf16[128,768]{1,0:T(8,128)(2,1)}, bf16[128,768]{1,0:T(8,128)(2,1)S(1)}, u32[]{:S(2)}, u32[]{:S(2)}) collective-permute-start(bf16[128,768]{1,0:T(8,128)(2,1)} %get-tuple-element.79.refs_1_), channel_id=1, source_target_pairs={{0,24},{4,28},{8,0},{12,4},{16,8},{20,12},{24,16},{28,20},{1,25},{... | collective-permute-start | bytes 589832 | tf_op jit(solution)/shard_map/ppermute | solution.py:52
  191.3 1.8 collective-permute-start.41
  193.1 11.3 %shard_map.116 = bf16[1344,3072]{1,0:T(8,128)(2,1)} custom-call(bf16[1344,768]{1,0:T(8,128)(2,1)} %get-tuple-element.70.lu_ref.left_ref, bf16[768,3072]{1,0:T(8,128)(2,1)} %get-tuple-element.67.right_ref, bf16[128,768]{1,0:T(8,128)(2,1)} %get-tuple-element.78.refs_0_, bf16[128,768]{1,0:T(8,128)(2,1)} %get-tuple-element.79.refs_1_, ...), custom_call_target="tpu_custom_call" | custom-call | flops 6341787648 | bytes 15040512 | tf_op jit(solution)/shard_map/pallas_call | solution.py:410
  204.4 3.2 %collective-permute-done.40 = bf16[128,768]{1,0:T(8,128)(2,1)S(1)} collective-permute-done((bf16[128,768]{1,0:T(8,128)(2,1)}, bf16[128,768]{1,0:T(8,128)(2,1)S(1)}, u32[]{:S(2)}, u32[]{:S(2)}) %collective-permute-start.40) | collective-permute-done | bytes 196640 | tf_op jit(solution)/shard_map/ppermute | solution.py:52
  (154 shorter events, 34.2 us)
Async XLA Ops:
  2.3 10.7 %collective-permute-start.1 = (bf16[144,768]{1,0:T(8,128)(2,1)}, bf16[144,768]{1,0:T(8,128)(2,1)S(1)}, u32[]{:S(2)}, u32[]{:S(2)}) collective-permute-start(bf16[144,768]{1,0:T(8,128)(2,1)} %shard_map.102.refs_1_), channel_id=1, source_target_pairs={{0,8},{4,12},{8,16},{12,20},{16,24},{20,28},{24,0},{28,4},{1,9},{5... | collective-permute-start | bytes 663560 | tf_op jit(solution)/shard_map/ppermute | solution.py:52
  5.3 13.1 %collective-permute-start = (bf16[144,768]{1,0:T(8,128)(2,1)}, bf16[144,768]{1,0:T(8,128)(2,1)S(1)}, u32[]{:S(2)}, u32[]{:S(2)}) collective-permute-start(bf16[144,768]{1,0:T(8,128)(2,1)} %shard_map.102.refs_1_), channel_id=1, source_target_pairs={{0,4},{4,0},{8,12},{12,8},{16,20},{20,16},{24,28},{28,24},{1,5},{5... | collective-permute-start | bytes 663560 | tf_op jit(solution)/shard_map/ppermute | solution.py:52
  14.5 8.4 %collective-permute-start.10 = (bf16[144,768]{1,0:T(8,128)(2,1)}, bf16[144,768]{1,0:T(8,128)(2,1)S(1)}, u32[]{:S(2)}, u32[]{:S(2)}) collective-permute-start(bf16[144,768]{1,0:T(8,128)(2,1)} %shard_map.102.refs_1_), channel_id=1, source_target_pairs={{0,24},{4,28},{8,0},{12,4},{16,8},{20,12},{24,16},{28,20},{1,25},{... | collective-permute-start | bytes 663560 | tf_op jit(solution)/shard_map/ppermute | solution.py:52
  16.2 13.1 %collective-permute-start.8 = (bf16[144,768]{1,0:T(8,128)(2,1)}, bf16[144,768]{1,0:T(8,128)(2,1)S(1)}, u32[]{:S(2)}, u32[]{:S(2)}) collective-permute-start(bf16[144,768]{1,0:T(8,128)(2,1)} %shard_map.102.refs_1_), channel_id=1, source_target_pairs={{0,16},{4,20},{8,24},{12,28},{16,0},{20,4},{24,8},{28,12},{1,17},{... | collective-permute-start | bytes 663560 | tf_op jit(solution)/shard_map/ppermute | solution.py:52
  16.2 16.1 %collective-permute-start.5 = (bf16[128,768]{1,0:T(8,128)(2,1)}, bf16[128,768]{1,0:T(8,128)(2,1)S(1)}, u32[]{:S(2)}, u32[]{:S(2)}) collective-permute-start(bf16[128,768]{1,0:T(8,128)(2,1)} %refs_5_.1), channel_id=1, source_target_pairs={{0,4},{4,0},{8,12},{12,8},{16,20},{20,16},{24,28},{28,24},{1,5},{5... | collective-permute-start | bytes 589832 | tf_op jit(solution)/shard_map/ppermute | solution.py:52
  22.9 16.3 %collective-permute-start.11 = (bf16[144,768]{1,0:T(8,128)(2,1)S(1)}, bf16[144,768]{1,0:T(8,128)(2,1)S(1)}, u32[]{:S(2)}, u32[]{:S(2)}) collective-permute-start(bf16[144,768]{1,0:T(8,128)(2,1)S(1)} %collective-permute-done.10.refs_7_), channel_id=1, source_target_pairs={{0,2},{1,3},{2,0},{3,1},{4,6},{5,7},{6,4},{7,5},{8,10},{9,11},{10,... | collective-permute-start | bytes 663560 | tf_op jit(solution)/shard_map/ppermute | solution.py:52
  29.3 11.6 %collective-permute-start.9 = (bf16[144,768]{1,0:T(8,128)(2,1)S(1)}, bf16[144,768]{1,0:T(8,128)(2,1)S(1)}, u32[]{:S(2)}, u32[]{:S(2)}) collective-permute-start(bf16[144,768]{1,0:T(8,128)(2,1)S(1)} %collective-permute-done.8.refs_5_), channel_id=1, source_target_pairs={{0,4},{4,0},{8,12},{12,8},{16,20},{20,16},{24,28},{28,24},{1,5},{5... | collective-permute-start | bytes 663560 | tf_op jit(solution)/shard_map/ppermute | solution.py:52
  31.8 9.2 %collective-permute-start.3 = (bf16[192,768]{1,0:T(8,128)(2,1)}, bf16[192,768]{1,0:T(8,128)(2,1)S(1)}, u32[]{:S(2)}, u32[]{:S(2)}) collective-permute-start(bf16[192,768]{1,0:T(8,128)(2,1)} %get-tuple-element.43), channel_id=1, source_target_pairs={{0,2},{1,3},{2,0},{3,1},{4,6},{5,7},{6,4},{7,5},{8,10},{9,11},{10,... | collective-permute-start | bytes 884744 | tf_op jit(solution)/shard_map/ppermute | solution.py:52
  32.3 9.3 %collective-permute-start.4 = (bf16[192,768]{1,0:T(8,128)(2,1)}, bf16[192,768]{1,0:T(8,128)(2,1)S(1)}, u32[]{:S(2)}, u32[]{:S(2)}) collective-permute-start(bf16[192,768]{1,0:T(8,128)(2,1)} %get-tuple-element.44), channel_id=1, source_target_pairs={{0,4},{4,0},{8,12},{12,8},{16,20},{20,16},{24,28},{28,24},{1,5},{5... | collective-permute-start | bytes 884744 | tf_op jit(solution)/shard_map/ppermute | solution.py:52
  39.2 9.0 %collective-permute-start.26 = (bf16[128,768]{1,0:T(8,128)(2,1)}, bf16[128,768]{1,0:T(8,128)(2,1)S(1)}, u32[]{:S(2)}, u32[]{:S(2)}) collective-permute-start(bf16[128,768]{1,0:T(8,128)(2,1)} %refs_5_.1), channel_id=1, source_target_pairs={{0,24},{4,28},{8,0},{12,4},{16,8},{20,12},{24,16},{28,20},{1,25},{... | collective-permute-start | bytes 589832 | tf_op jit(solution)/shard_map/ppermute | solution.py:52
  41.0 11.0 %collective-permute-start.25 = (bf16[128,768]{1,0:T(8,128)(2,1)}, bf16[128,768]{1,0:T(8,128)(2,1)S(1)}, u32[]{:S(2)}, u32[]{:S(2)}) collective-permute-start(bf16[128,768]{1,0:T(8,128)(2,1)} %refs_5_.1), channel_id=1, source_target_pairs={{0,16},{4,20},{8,24},{12,28},{16,0},{20,4},{24,8},{28,12},{1,17},{... | collective-permute-start | bytes 589832 | tf_op jit(solution)/shard_map/ppermute | solution.py:52
  41.0 11.0 %collective-permute-start.20 = (bf16[192,768]{1,0:T(8,128)(2,1)S(1)}, bf16[192,768]{1,0:T(8,128)(2,1)S(1)}, u32[]{:S(2)}, u32[]{:S(2)}) collective-permute-start(bf16[192,768]{1,0:T(8,128)(2,1)S(1)} %collective-permute-done.3.refs_0_.refs_2_), channel_id=1, source_target_pairs={{0,1},{1,0},{2,3},{3,2},{4,5},{5,4},{6,7},{7,6},{8,9},{9,8},{10,11... | collective-permute-start | bytes 884744 | tf_op jit(solution)/shard_map/ppermute | solution.py:52
  41.6 18.5 %collective-permute-start.19 = (bf16[384,768]{1,0:T(8,128)(2,1)}, bf16[384,768]{1,0:T(8,128)(2,1)S(1)}, u32[]{:S(2)}, u32[]{:S(2)}) collective-permute-start(bf16[384,768]{1,0:T(8,128)(2,1)} %get-tuple-element.45.refs_0_), channel_id=1, source_target_pairs={{0,1},{1,0},{2,3},{3,2},{4,5},{5,4},{6,7},{7,6},{8,9},{9,8},{10,11... | collective-permute-start | bytes 1769480 | tf_op jit(solution)/shard_map/ppermute | solution.py:52
  52.0 11.4 %collective-permute-start.22 = (bf16[384,768]{1,0:T(8,128)(2,1)}, bf16[384,768]{1,0:T(8,128)(2,1)S(1)}, u32[]{:S(2)}, u32[]{:S(2)}) collective-permute-start(bf16[384,768]{1,0:T(8,128)(2,1)} %get-tuple-element.49.refs_0_.refs_6_), channel_id=1, source_target_pairs={{0,1},{1,0},{2,3},{3,2},{4,5},{5,4},{6,7},{7,6},{8,9},{9,8},{10,11... | collective-permute-start | bytes 1769480 | tf_op jit(solution)/shard_map/ppermute | solution.py:52
  59.2 18.5 %collective-permute-start.28 = (bf16[128,768]{1,0:T(8,128)(2,1)S(1)}, bf16[128,768]{1,0:T(8,128)(2,1)S(1)}, u32[]{:S(2)}, u32[]{:S(2)}) collective-permute-start(bf16[128,768]{1,0:T(8,128)(2,1)S(1)} %collective-permute-done.26.refs_15_.refs_5_), channel_id=1, source_target_pairs={{0,2},{1,3},{2,0},{3,1},{4,6},{5,7},{6,4},{7,5},{8,10},{9,11},{10,... | collective-permute-start | bytes 589832 | tf_op jit(solution)/shard_map/ppermute | solution.py:52
  60.1 17.7 %collective-permute-start.27 = (bf16[128,768]{1,0:T(8,128)(2,1)S(1)}, bf16[128,768]{1,0:T(8,128)(2,1)S(1)}, u32[]{:S(2)}, u32[]{:S(2)}) collective-permute-start(bf16[128,768]{1,0:T(8,128)(2,1)S(1)} %collective-permute-done.25.refs_14_.refs_3_), channel_id=1, source_target_pairs={{0,4},{4,0},{8,12},{12,8},{16,20},{20,16},{24,28},{28,24},{1,5},{5... | collective-permute-start | bytes 589832 | tf_op jit(solution)/shard_map/ppermute | solution.py:52
  61.1 21.7 %collective-permute-start.15 = (bf16[192,768]{1,0:T(8,128)(2,1)}, bf16[192,768]{1,0:T(8,128)(2,1)S(1)}, u32[]{:S(2)}, u32[]{:S(2)}) collective-permute-start(bf16[192,768]{1,0:T(8,128)(2,1)} %get-tuple-element.55), channel_id=1, source_target_pairs={{0,2},{1,3},{2,0},{3,1},{4,6},{5,7},{6,4},{7,5},{8,10},{9,11},{10,... | collective-permute-start | bytes 884744 | tf_op jit(solution)/shard_map/ppermute | solution.py:52
  61.9 21.4 %collective-permute-start.17 = (bf16[192,768]{1,0:T(8,128)(2,1)}, bf16[192,768]{1,0:T(8,128)(2,1)S(1)}, u32[]{:S(2)}, u32[]{:S(2)}) collective-permute-start(bf16[192,768]{1,0:T(8,128)(2,1)} %get-tuple-element.56), channel_id=1, source_target_pairs={{0,4},{4,0},{8,12},{12,8},{16,20},{20,16},{24,28},{28,24},{1,5},{5... | collective-permute-start | bytes 884744 | tf_op jit(solution)/shard_map/ppermute | solution.py:52
  81.0 8.4 %collective-permute-start.30 = (bf16[192,768]{1,0:T(8,128)(2,1)}, bf16[192,768]{1,0:T(8,128)(2,1)S(1)}, u32[]{:S(2)}, u32[]{:S(2)}) collective-permute-start(bf16[192,768]{1,0:T(8,128)(2,1)} %get-tuple-element.63), channel_id=1, source_target_pairs={{0,2},{1,3},{2,0},{3,1},{4,6},{5,7},{6,4},{7,5},{8,10},{9,11},{10,... | collective-permute-start | bytes 884744 | tf_op jit(solution)/shard_map/ppermute | solution.py:52
  82.8 18.8 %collective-permute-start.14 = (bf16[384,768]{1,0:T(8,128)(2,1)S(1)}, bf16[384,768]{1,0:T(8,128)(2,1)S(1)}, u32[]{:S(2)}, u32[]{:S(2)}) collective-permute-start(bf16[384,768]{1,0:T(8,128)(2,1)S(1)} %copy-done.28), channel_id=1, source_target_pairs={{0,1},{1,0},{2,3},{3,2},{4,5},{5,4},{6,7},{7,6},{8,9},{9,8},{10,11... | collective-permute-start | bytes 1769480 | tf_op jit(solution)/shard_map/ppermute | solution.py:52
  83.3 18.3 %collective-permute-start.29 = (bf16[384,768]{1,0:T(8,128)(2,1)}, bf16[384,768]{1,0:T(8,128)(2,1)S(1)}, u32[]{:S(2)}, u32[]{:S(2)}) collective-permute-start(bf16[384,768]{1,0:T(8,128)(2,1)} %get-tuple-element.62.refs_0_.refs_6_), channel_id=1, source_target_pairs={{0,1},{1,0},{2,3},{3,2},{4,5},{5,4},{6,7},{7,6},{8,9},{9,8},{10,11... | collective-permute-start | bytes 1769480 | tf_op jit(solution)/shard_map/ppermute | solution.py:52
  89.4 12.2 %collective-permute-start.18 = (bf16[192,768]{1,0:T(8,128)(2,1)S(1)}, bf16[192,768]{1,0:T(8,128)(2,1)S(1)}, u32[]{:S(2)}, u32[]{:S(2)}) collective-permute-start(bf16[192,768]{1,0:T(8,128)(2,1)S(1)} %collective-permute-done.17.refs_4_), channel_id=1, source_target_pairs={{0,1},{1,0},{2,3},{3,2},{4,5},{5,4},{6,7},{7,6},{8,9},{9,8},{10,11... | collective-permute-start | bytes 884744 | tf_op jit(solution)/shard_map/ppermute | solution.py:52
  89.8 11.8 %collective-permute-start.31 = (bf16[192,768]{1,0:T(8,128)(2,1)S(1)}, bf16[192,768]{1,0:T(8,128)(2,1)S(1)}, u32[]{:S(2)}, u32[]{:S(2)}) collective-permute-start(bf16[192,768]{1,0:T(8,128)(2,1)S(1)} %collective-permute-done.30.refs_8_), channel_id=1, source_target_pairs={{0,1},{1,0},{2,3},{3,2},{4,5},{5,4},{6,7},{7,6},{8,9},{9,8},{10,11... | collective-permute-start | bytes 884744 | tf_op jit(solution)/shard_map/ppermute | solution.py:52
  89.9 11.7 %collective-permute-start.33 = (bf16[192,768]{1,0:T(8,128)(2,1)S(1)}, bf16[192,768]{1,0:T(8,128)(2,1)S(1)}, u32[]{:S(2)}, u32[]{:S(2)}) collective-permute-start(bf16[192,768]{1,0:T(8,128)(2,1)S(1)} %collective-permute-done.32.refs_10_), channel_id=1, source_target_pairs={{0,1},{1,0},{2,3},{3,2},{4,5},{5,4},{6,7},{7,6},{8,9},{9,8},{10,11... | collective-permute-start | bytes 884744 | tf_op jit(solution)/shard_map/ppermute | solution.py:52
  133.5 13.0 %collective-permute-start.34 = (bf16[2,768,768]{2,1,0:T(8,128)(2,1)}, bf16[2,768,768]{2,1,0:T(8,128)(2,1)S(1)}, u32[]{:S(2)}, u32[]{:S(2)}) collective-permute-start(bf16[2,768,768]{2,1,0:T(8,128)(2,1)} %get-tuple-element.73), channel_id=1, source_target_pairs={{0,1},{1,0},{2,3},{3,2},{4,5},{5,4},{6,7},{7,6},{8,9},{9,8},{10,11... | collective-permute-start | bytes 7077896 | tf_op jit(solution)/shard_map/ppermute | solution.py:52
  149.0 15.6 %collective-permute-start.36 = (bf16[2,192,768]{2,1,0:T(8,128)(2,1)S(1)}, bf16[2,192,768]{2,1,0:T(8,128)(2,1)S(1)}, u32[]{:S(2)}, u32[]{:S(2)}) collective-permute-start(bf16[2,192,768]{2,1,0:T(8,128)(2,1)S(1)} %get-tuple-element.82.refs_3_), channel_id=1, source_target_pairs={{0,4},{4,0},{8,12},{12,8},{16,20},{20,16},{24,28},{28,24},{1,5},{5... | collective-permute-start | bytes 1769480 | tf_op jit(solution)/shard_map/ppermute | solution.py:52
  151.2 15.3 %collective-permute-start.35 = (bf16[384,768]{1,0:T(8,128)(2,1)S(1)}, bf16[384,768]{1,0:T(8,128)(2,1)S(1)}, u32[]{:S(2)}, u32[]{:S(2)}) collective-permute-start(bf16[384,768]{1,0:T(8,128)(2,1)S(1)} %get-tuple-element.84.refs_1_), channel_id=1, source_target_pairs={{0,2},{1,3},{2,0},{3,1},{4,6},{5,7},{6,4},{7,5},{8,10},{9,11},{10,... | collective-permute-start | bytes 1769480 | tf_op jit(solution)/shard_map/ppermute | solution.py:52
  170.7 13.5 %collective-permute-start.38 = (bf16[256,768]{1,0:T(8,128)(2,1)}, bf16[256,768]{1,0:T(8,128)(2,1)S(1)}, u32[]{:S(2)}, u32[]{:S(2)}) collective-permute-start(bf16[256,768]{1,0:T(8,128)(2,1)} %get-tuple-element.77.refs_3_), channel_id=1, source_target_pairs={{0,2},{1,3},{2,0},{3,1},{4,6},{5,7},{6,4},{7,5},{8,10},{9,11},{10,... | collective-permute-start | bytes 1179656 | tf_op jit(solution)/shard_map/ppermute | solution.py:52
  171.5 12.8 %collective-permute-start.37 = (bf16[192,768]{1,0:T(8,128)(2,1)}, bf16[192,768]{1,0:T(8,128)(2,1)S(1)}, u32[]{:S(2)}, u32[]{:S(2)}) collective-permute-start(bf16[192,768]{1,0:T(8,128)(2,1)} %get-tuple-element.75.refs_1_), channel_id=1, source_target_pairs={{0,4},{4,0},{8,12},{12,8},{16,20},{20,16},{24,28},{28,24},{1,5},{5... | collective-permute-start | bytes 884744 | tf_op jit(solution)/shard_map/ppermute | solution.py:52
  188.2 16.2 %collective-permute-start.39 = (bf16[128,768]{1,0:T(8,128)(2,1)}, bf16[128,768]{1,0:T(8,128)(2,1)S(1)}, u32[]{:S(2)}, u32[]{:S(2)}) collective-permute-start(bf16[128,768]{1,0:T(8,128)(2,1)} %get-tuple-element.79.refs_1_), channel_id=1, source_target_pairs={{0,24},{4,28},{8,0},{12,4},{16,8},{20,12},{24,16},{28,20},{1,25},{... | collective-permute-start | bytes 589832 | tf_op jit(solution)/shard_map/ppermute | solution.py:52
  191.3 16.2 %collective-permute-start.40 = (bf16[128,768]{1,0:T(8,128)(2,1)}, bf16[128,768]{1,0:T(8,128)(2,1)S(1)}, u32[]{:S(2)}, u32[]{:S(2)}) collective-permute-start(bf16[128,768]{1,0:T(8,128)(2,1)} %get-tuple-element.80.refs_2_), channel_id=1, source_target_pairs={{0,16},{4,20},{8,24},{12,28},{16,0},{20,4},{24,8},{28,12},{1,17},{... | collective-permute-start | bytes 589832 | tf_op jit(solution)/shard_map/ppermute | solution.py:52
  191.3 16.2 %collective-permute-start.41 = (bf16[128,768]{1,0:T(8,128)(2,1)}, bf16[128,768]{1,0:T(8,128)(2,1)S(1)}, u32[]{:S(2)}, u32[]{:S(2)}) collective-permute-start(bf16[128,768]{1,0:T(8,128)(2,1)} %get-tuple-element.81.refs_3_), channel_id=1, source_target_pairs={{0,8},{4,12},{8,16},{12,20},{16,24},{20,28},{24,0},{28,4},{1,9},{5... | collective-permute-start | bytes 589832 | tf_op jit(solution)/shard_map/ppermute | solution.py:52
  (51 other events, 318.2 us)

commit v2 on v0

v2 whole, which is shorter than its diff:
```python
import jax
import jax.numpy as jnp
from jax import lax
from jax.experimental import pallas as pl
from jax.experimental.pallas import tpu as pltpu
from jax.sharding import PartitionSpec as P

VMEM_LIMIT = 58 * 1024 * 1024
CORES = 2
DEPTH = 4
PAIRS = ((0, 1), (2, 3))
TILES = 6
COLUMN_PARTS = 4
ROUTING_ROWS = 16
ANY = pl.BlockSpec(memory_space=pl.ANY)
VMEM = pl.BlockSpec(memory_space=pltpu.VMEM)
SMEM = pl.BlockSpec(memory_space=pltpu.SMEM)


def product(left, right):
    return jnp.dot(left, right, preferred_element_type=jnp.float32)


def left_product(left, right):
    return lax.dot_general(
        left, right, (((0,), (0,)), ((), ())), preferred_element_type=jnp.float32
    )


def half(*shape):
    return jax.ShapeDtypeStruct(shape, jnp.bfloat16)


def right_product(left, right):
    return lax.dot_general(
        left, right, (((1,), (1,)), ((), ())), preferred_element_type=jnp.float32
    )


def full32(*shape):
    return jax.ShapeDtypeStruct(shape, jnp.float32)


def params():
    return pltpu.CompilerParams(vmem_limit_bytes=VMEM_LIMIT)


def shifted(value, axis, stride, count, step):
    step %= count
    if step == 0:
        return value
    pairs = []
    for src in range(lax.axis_size(axis)):
        place = src // stride % count
        pairs.append((src, src + ((place + step) % count - place) * stride))
    return lax.ppermute(value, axis, pairs)


def whole_call(kernel, args, out_shapes, experts=None, after=()):
    scalars = [] if experts is None else [experts]
    skipped = len(after)

    def body(*refs):
        kernel(*refs[skipped:])

    return pl.pallas_call(
        body,
        in_specs=[ANY] * skipped + [SMEM] * len(scalars) + [VMEM] * len(args),
        out_specs=[VMEM] * len(out_shapes),
        out_shape=out_shapes,
        compiler_params=params(),
        cost_estimate=pl.CostEstimate(flops=0, bytes_accessed=1, transcendentals=0),
    )(*after, *scalars, *args)


def pack(tokens, grad_out, probs, expert_ids):
    tok_rows, width = tokens.shape

    def kernel(t_ref, g_ref, p_ref, id_ref, out_ref):
        out_ref[:tok_rows, :] = t_ref[...]
        out_ref[tok_rows : 2 * tok_rows, :] = g_ref[...]
        rest = p_ref[...]
        rows = [id_ref[...].astype(jnp.float32)]
        for _ in range(3):
            part = rest.astype(jnp.bfloat16).astype(jnp.float32)
            rows.append(part)
            rest = rest - part
        out_ref[2 * tok_rows :, :] = jnp.zeros((ROUTING_ROWS, width), jnp.bfloat16)
        out_ref[2 * tok_rows :, :tok_rows] = jnp.concatenate(rows, axis=0).astype(jnp.bfloat16)

    assert 4 * probs.shape[0] == ROUTING_ROWS
    return whole_call(
        kernel, [tokens, grad_out, probs, expert_ids], [half(2 * tok_rows + ROUTING_ROWS, width)]
    )[0]


def routes(ref, tok_rows, expert):
    rows = ref[2 * tok_rows :, :tok_rows].astype(jnp.float32)
    top = ROUTING_ROWS // 4
    hit = rows[:top] == expert.astype(jnp.float32)
    weights = rows[top : 2 * top] + rows[2 * top : 3 * top] + rows[3 * top :]
    prob = jnp.sum(jnp.where(hit, weights, 0.0), axis=0, keepdims=True)
    named = jnp.sum(hit.astype(jnp.float32), axis=0, keepdims=True)
    before = lax.broadcasted_iota(jnp.int32, (tok_rows, tok_rows), 0)
    here = lax.broadcasted_iota(jnp.int32, (tok_rows, tok_rows), 1)
    ahead = (before < here).astype(jnp.float32).astype(jnp.bfloat16)
    many = jnp.broadcast_to(named, (8, tok_rows)).astype(jnp.bfloat16)
    pos = product(many, ahead)[:1]
    return jnp.where(named > 0.0, pos, -1.0).astype(jnp.int32), prob


def hits(pos, capacity):
    slots = lax.broadcasted_iota(jnp.int32, (capacity, pos.shape[1]), 0)
    return slots == pos


def one_hot(pos, capacity):
    return hits(pos, capacity).astype(jnp.float32).astype(jnp.bfloat16)


def pick_pair(experts, even, odd, capacity, after):
    blocks, ranges = len(even), len(odd)
    tok_rows, width = (even[0].shape[0] - ROUTING_ROWS) // 2, even[0].shape[1]

    def kernel(e_ref, *refs):
        even_refs, refs = refs[:blocks], refs[blocks:]
        odd_refs, refs = refs[:ranges], refs[ranges:]
        keep_ref, even_out, odd_out, pos_ref = refs[0], refs[1], refs[2:-1], refs[-1]

        def picked(ref, pos, prob):
            hit = hits(pos, capacity)
            chosen = hit.astype(jnp.float32).astype(jnp.bfloat16)
            weight = jnp.sum(jnp.where(hit, prob, 0.0), axis=1, keepdims=True)
            rows = product(chosen, ref[:tok_rows, :])
            grads = product(chosen, ref[tok_rows : 2 * tok_rows, :])
            return rows.astype(jnp.bfloat16), (weight * grads).astype(jnp.bfloat16)

        for dx in range(blocks):
            pos, prob = routes(even_refs[dx], tok_rows, e_ref[0])
            rows = slice(dx * capacity, (dx + 1) * capacity)
            for i, value in enumerate(picked(even_refs[dx], pos, prob)):
                keep_ref[i, rows, :] = value
                even_out[i, rows, :] = value
            pos_ref[1, dx] = routes(even_refs[0], tok_rows, e_ref[dx])[0]
        for dx in range(blocks):
            pos, prob = routes(odd_refs[0], tok_rows, e_ref[dx])
            pos_ref[0, dx] = pos
            for dy in range(ranges):
                start = (blocks + dy if dx == 0 else dy) * capacity
                out_ref = keep_ref if dx == 0 else odd_out[dx - 1]
                for i, value in enumerate(picked(odd_refs[dy], pos, prob)):
                    out_ref[i, start : start + capacity, :] = value

    shapes = [half(2, (blocks + ranges) * capacity, width), half(2, blocks * capacity, width)]
    shapes += [half(2, ranges * capacity, width)] * (blocks - 1)
    shapes += [jax.ShapeDtypeStruct((2, blocks, 1, tok_rows), jnp.int32)]
    outs = whole_call(kernel, [*even, *odd], shapes, experts, after)
    return outs[:-1], outs[-1]


def fixed(a):
    return pl.BlockSpec(a.shape, lambda f, *_: (0,) * a.ndim)


def hidden_units(chunk, chunks, order, names, pieces, weights, sizes, carried, after):
    ff, full = weights[0].shape
    blocks, ranges, capacity = sizes
    tile, width, k_rows = ff // TILES, pieces[0].shape[2], blocks * capacity
    rows, n_in = 2 * k_rows, len(pieces)

    def kernel(order_ref, *refs):
        in_refs, refs = refs[:n_in], refs[n_in:]
        (wg_ref, wu_ref, wd_ref), refs = refs[:3], refs[3 + len(carried) + len(after) :]
        x_ref, g_ref, hid_ref, gpg_ref, gpu_ref = refs

        def columns(dc, dy):
            at = order_ref[dc * ranges + dy] * width
            return pl.ds(pl.multiple_of(at, width), width)

        def put(out_ref, i):
            for (kind, d, dc), ref in zip(names, in_refs):
                if kind == "even":
                    out_ref[:k_rows, columns(dc, d)] = ref[i]
                    continue
                start = k_rows + d * capacity
                first = k_rows if kind == "keep" else 0
                if kind == "keep":
                    out_ref[:k_rows, columns(dc, 0)] = ref[i, :k_rows, :]
                for dy in range(ranges):
                    at = first + dy * capacity
                    out_ref[start : start + capacity, columns(dc, dy)] = ref[
                        i, at : at + capacity, :
                    ]

        @pl.when(pl.program_id(0) == 0)
        def _():
            put(x_ref, 0)
            put(g_ref, 1)

        gate = right_product(x_ref[...], wg_ref[...])
        up = right_product(x_ref[...], wu_ref[...])
        sig = jax.nn.sigmoid(gate)
        silu = gate * sig
        hid_ref[...] = (silu * up).astype(jnp.bfloat16).T
        slope = up * sig * (1.0 + gate * (1.0 - sig))
        grad_hidden = right_product(g_ref[...], wd_ref[...])
        gpg_ref[...] = (grad_hidden * slope).astype(jnp.bfloat16).T
        gpu_ref[...] = (grad_hidden * silu).astype(jnp.bfloat16).T

    out_shapes = [half(chunks * rows, full)] * 2 + [half(ff, chunks * rows)] * 3
    out_specs = [pl.BlockSpec((rows, full), lambda f, _: (chunk, 0))] * 2
    out_specs += [pl.BlockSpec((tile, rows), lambda f, _: (f, chunk))] * 3
    in_specs = [fixed(a) for a in pieces]
    in_specs += [pl.BlockSpec((tile, full), lambda f, _: (f, 0))] * 3
    first = 1 + len(in_specs)
    in_specs += [ANY] * (len(carried) + len(after))
    return pl.pallas_call(
        kernel,
        grid_spec=pltpu.PrefetchScalarGridSpec(
            num_scalar_prefetch=1, grid=(TILES,), in_specs=in_specs, out_specs=out_specs
        ),
        out_shape=out_shapes,
        input_output_aliases={first + i: i for i in range(len(carried))},
        compiler_params=params(),
        cost_estimate=pl.CostEstimate(
            flops=6 * rows * ff * full,
            bytes_accessed=6 * ff * full + 8 * rows * full + 6 * rows * ff,
            transcendentals=rows * ff,
        ),
    )(order, *pieces, *weights, *carried, *after)


def partials(chunk, chunks, order, lefts, weights, ranges, after):
    ff, full = weights[0].shape
    rows = lefts[0].shape[1] // chunks
    steps = CORES * ranges
    width = full // steps

    def kernel(order_ref, gpg_ref, gpu_ref, wg_ref, wu_ref, *refs):
        own_ref, other_ref, lg_ref, lu_ref = refs[len(after) :]
        step = pl.program_id(0)

        @pl.when(step == 0)
        def _():
            lg_ref[...] = gpg_ref[...].T
            lu_ref[...] = gpu_ref[...].T

        value = product(lg_ref[...], wg_ref[...]) + product(lu_ref[...], wu_ref[...])

        @pl.when(step < ranges)
        def _():
            other_ref[0] = value.astype(jnp.bfloat16)

        @pl.when(step >= ranges)
        def _():
            own_ref[0] = value.astype(jnp.bfloat16)

    left = pl.BlockSpec((ff, rows), lambda r, _: (0, chunk))
    right = pl.BlockSpec((ff, width), lambda r, order: (0, order[lax.rem(r + ranges, steps)]))
    own = pl.BlockSpec((1, rows, width), lambda r, _: (jnp.maximum(r - ranges, 0), 0, 0))
    other = pl.BlockSpec((1, rows, width), lambda r, _: (jnp.minimum(r, ranges - 1), 0, 0))
    return pl.pallas_call(
        kernel,
        grid_spec=pltpu.PrefetchScalarGridSpec(
            num_scalar_prefetch=1,
            grid=(steps,),
            in_specs=[left, left, right, right] + [ANY] * len(after),
            out_specs=[own, other],
            scratch_shapes=[pltpu.VMEM((rows, ff), jnp.bfloat16)] * 2,
        ),
        out_shape=[half(ranges, rows, width)] * 2,
        compiler_params=params(),
        cost_estimate=pl.CostEstimate(
            flops=4 * rows * ff * full,
            bytes_accessed=4 * ff * full + 2 * rows * full + 4 * rows * ff,
            transcendentals=0,
        ),
    )(order, *lefts, *weights[:2], *after)


def weight_grad(left, right, parts, held, after):
    ff, rows = left.shape
    full = right.shape[1]
    part = full // COLUMN_PARTS
    start, stop = parts

    def kernel(left_ref, right_ref, *refs):
        refs[-1][...] = product(left_ref[...], right_ref[...]).astype(jnp.bfloat16)

    return pl.pallas_call(
        kernel,
        grid=(stop - start,),
        in_specs=[fixed(left), pl.BlockSpec((rows, part), lambda n: (0, start + n))]
        + [ANY] * (len(held) + len(after)),
        out_specs=pl.BlockSpec((ff, part), lambda n: (0, start + n)),
        out_shape=half(ff, full),
        input_output_aliases={2: 0} if held else {},
        compiler_params=params(),
        cost_estimate=pl.CostEstimate(
            flops=2 * rows * ff * part * (stop - start),
            bytes_accessed=2 * (rows * ff + part * (stop - start) * (ff + rows)),
            transcendentals=0,
        ),
    )(left, right, *held, *after)


def first_returns(own, other, sizes):
    blocks, ranges, capacity = sizes

    def total(at):
        value = own[at].astype(jnp.float32) + other[at].astype(jnp.float32)
        return value.astype(jnp.bfloat16)

    k_rows = blocks * capacity
    even = [total((dy, slice(0, k_rows))) for dy in range(ranges)]
    starts = [k_rows + dx * capacity for dx in range(blocks)]
    return even, [total((slice(None), slice(at, at + capacity))) for at in starts]


def spread(pos, rows):
    chosen = hits(pos, rows.shape[0]).astype(jnp.float32).astype(jnp.bfloat16)
    return left_product(chosen, rows)


def second_returns(pos, even, odd, after):
    ranges, blocks = len(even), len(odd)
    tok_rows, width = pos.shape[3], even[0].shape[1]
    capacity = even[0].shape[0] // blocks

    def kernel(pos_ref, *refs):
        even_refs, refs = refs[:ranges], refs[ranges:]
        odd_refs, out_refs = refs[:blocks], refs[blocks:]
        for dx in range(blocks):
            rows = slice(dx * capacity, (dx + 1) * capacity)
            value = even_refs[0][rows, :].astype(jnp.float32)
            for dy in range(1, ranges):
                value += even_refs[dy][rows, :].astype(jnp.float32)
            out_refs[dx][...] = value.astype(jnp.bfloat16)
        for dy in range(ranges):
            value = spread(pos_ref[0, 0], odd_refs[0][dy])
            for dx in range(1, blocks):
                value += spread(pos_ref[0, dx], odd_refs[dx][dy])
            out_refs[blocks + dy][...] = value.astype(jnp.bfloat16)

    shapes = [half(capacity, width)] * blocks + [half(tok_rows, width)] * ranges
    outs = whole_call(kernel, [pos, *even, *odd], shapes, after=after)
    return outs[:blocks], outs[blocks:]


def third_returns(pos, even, odd, after):
    blocks, ranges = len(even), len(odd)
    tok_rows, width = pos.shape[3], even[0].shape[1]

    def kernel(pos_ref, *refs):
        even_refs, refs = refs[:blocks], refs[blocks:]
        odd_refs, out_refs = refs[:ranges], refs[ranges:]
        value = spread(pos_ref[1, 0], even_refs[0][...])
        for dx in range(1, blocks):
            value += spread(pos_ref[1, dx], even_refs[dx][...])
        out_refs[0][...] = value.astype(jnp.bfloat16)
        value = odd_refs[0][...].astype(jnp.float32)
        for dy in range(1, ranges):
            value += odd_refs[dy][...].astype(jnp.float32)
        out_refs[1][...] = value.astype(jnp.bfloat16)

    return whole_call(kernel, [pos, *even, *odd], [half(tok_rows, width)] * 2, after=after)


def add_up(parts):
    value = parts[0].astype(jnp.float32)
    for part in parts[1:]:
        value += part.astype(jnp.float32)
    return value.astype(jnp.bfloat16)


def ordered(value, after):
    return lax.optimization_barrier((value, tuple(after)))[0] if after else value


def local(tokens, grad_out, probs, expert_ids, w_gate, w_up, w_down):
    experts, etp = lax.axis_size("ep"), lax.axis_size("etp")
    blocks, ranges = experts // DEPTH, etp // CORES
    tok_rows, top_count = expert_ids.shape
    capacity = 3 * tok_rows * top_count // (2 * experts)
    me, mine = lax.axis_index("ep"), lax.axis_index("etp")
    my_z, my_x = me // blocks, me % blocks
    my_y, my_c = mine // CORES, mine % CORES

    def along_z(value, step):
        return shifted(value, "ep", blocks, DEPTH, step)

    def along_x(value, step):
        return shifted(value, "ep", 1, blocks, step)

    def along_y(value, step):
        return shifted(value, "etp", CORES, ranges, step)

    def along_c(value, step):
        return shifted(value, "etp", 1, CORES, step)

    own_experts = jnp.stack([my_z * blocks + (my_x + dx) % blocks for dx in range(blocks)])
    own_experts = own_experts.astype(jnp.int32)
    order = [
        (my_y - dy) % ranges * CORES + (my_c - dc) % CORES
        for dc in range(CORES)
        for dy in range(ranges)
    ]
    order = jnp.stack(order).astype(jnp.int32)
    weights = (w_gate[0].T, w_up[0].T, w_down[0])

    def first_hops(line):
        even = [[along_x(line[k], dx) for dx in range(blocks)] for k in EVEN]
        odd = [[along_y(line[k], dy) for dy in range(ranges)] for k in ODD]
        return list(zip(even, odd))

    def second_hops(outs):
        keep, even, odd = outs[0], outs[1], outs[2:]
        names, arrays = [("keep", 0)], [keep]
        for dy in range(1, ranges):
            names.append(("even", dy))
            arrays.append(along_y(even, dy))
        for dx in range(1, blocks):
            names.append(("odd", dx))
            arrays.append(along_x(odd[dx - 1], dx))
        return names, arrays

    def core_hops(hopped):
        names, arrays = [], []
        for pair, (kinds, values) in enumerate(hopped):
            for (kind, d), value in zip(kinds, values):
                for dc in range(CORES):
                    names.append((pair, kind, d, dc))
                    arrays.append(along_c(value, dc))
        return names, arrays

    sizes = (blocks, ranges, capacity)
    packed = pack(tokens, grad_out, probs.T, expert_ids.T)
    line = [along_z(packed, k) for k in range(DEPTH)]

    def first_hops(pair):
        even = [along_x(line[pair[0]], dx) for dx in range(blocks)]
        return even, [along_y(line[pair[1]], dy) for dy in range(ranges)]

    def gathered(even, odd, after):
        outs, pos = pick_pair(own_experts, even, odd, capacity, after)
        names, arrays = [("keep", 0)], [outs[0]]
        for dy in range(1, ranges):
            names.append(("even", dy))
            arrays.append(along_y(outs[1], dy))
        for dx in range(1, blocks):
            names.append(("odd", dx))
            arrays.append(along_x(outs[1 + dx], dx))
        return pos, names, arrays

    def units(chunk, names, arrays, carried, after):
        names = [(kind, d, dc) for kind, d in names for dc in range(CORES)]
        pieces = [along_c(a, dc) for a in arrays for dc in range(CORES)]
        return hidden_units(
            chunk, len(PAIRS), order, names, pieces, weights, sizes, carried, after
        )

    def sums(chunk, carried, after):
        return partials(chunk, len(PAIRS), order, carried[3:], weights, ranges, after)

    def first_step(parts, after):
        own, other = ordered((parts[0], along_c(parts[1], -1)), after)
        even, odd = first_returns(own, other, sizes)
        arrived = [along_y(a, -dy) for dy, a in enumerate(even)]
        return (*even, *odd), arrived, [along_x(a, -dx) for dx, a in enumerate(odd)]

    def second_step(pos, even, odd, after):
        even, odd = second_returns(pos, even, odd, after)
        arrived = [along_x(a, -dx) for dx, a in enumerate(even)]
        return (*even, *odd), arrived, [along_y(a, -dy) for dy, a in enumerate(odd)]

    def third_step(pair, pos, even, odd, after):
        outs = third_returns(pos, even, odd, after)
        return tuple(outs), [along_z(a, -k) for k, a in zip(pair, outs)]

    pos_a, names, arrays_a = gathered(*first_hops(PAIRS[0]), ())
    even_b, odd_b = first_hops(PAIRS[1])
    pos_b, names, arrays_b = gathered(even_b, odd_b, tuple(arrays_a))
    arrays_a = [arrays_a[0], *ordered(tuple(arrays_a[1:]), (*even_b[1:], *odd_b[1:]))]
    carried = units(0, names, arrays_a, [], (arrays_b[0],))
    arrays_b = [arrays_b[0], *ordered(tuple(arrays_b[1:]), (carried[2],))]
    parts_a = sums(0, carried, tuple(arrays_b[1:]))
    carried = units(1, names, arrays_b, carried, (parts_a[0],))
    done, even_a, odd_a = first_step(parts_a, (carried[2],))
    parts_b = sums(1, carried, done)
    x_all, g_all, hidden, grad_pre_gate, grad_pre_up = carried
    done, even_a, odd_a = second_step(pos_a, even_a, odd_a, (parts_b[0],))
    middle, end = COLUMN_PARTS // 2, COLUMN_PARTS
    grad_down = weight_grad(hidden, g_all, (0, middle), [], done)
    done_a, returned_a = third_step(PAIRS[0], pos_a, even_a, odd_a, (grad_down,))
    done, even_b, odd_b = first_step(parts_b, (grad_down,))
    grad_down = weight_grad(hidden, g_all, (middle, end), [grad_down], done_a + done)
    done, even_b, odd_b = second_step(pos_b, even_b, odd_b, (grad_down,))
    grad_gate = weight_grad(grad_pre_gate, x_all, (0, end), [], done)
    done, returned_b = third_step(PAIRS[1], pos_b, even_b, odd_b, (grad_gate,))
    grad_up = weight_grad(grad_pre_up, x_all, (0, end), [], done)
    grad_tokens = add_up(returned_a + returned_b)
    return (grad_tokens, grad_gate.T[None], grad_up.T[None], grad_down[None])


def solution(mesh):
    return jax.shard_map(
        local,
        mesh=mesh,
        in_specs=(
            P("ep", "etp"),
            P("ep", "etp"),
            P("ep", None),
            P("ep", None),
            P("ep", None, "etp"),
            P("ep", None, "etp"),
            P("ep", "etp", None),
        ),
        out_specs=(
            P("ep", "etp"),
            P("ep", None, "etp"),
            P("ep", None, "etp"),
            P("ep", "etp", None),
        ),
        check_vma=False,
    )
```

time: 453 us -> 210 us (0.46); the launches traced: 446 us -> 209 us
  waiting for transfers between devices: 267 us -> 45 us
  Pallas kernels: 0 us -> 121 us
  matrix products: 93.5 us -> 0 us
  local copies, waits for them, and re-layouts: 35.8 us -> 7.53 us
  between operations: 14.4 us -> 0.85 us
  starting transfers between devices: 15.8 us -> 29 us
  blocking collectives: 10.3 us -> 0 us
    all_to_all x3 -> x0, waiting for transfers between devices: 225 us -> none  [the longest x1 81.3 us: local(): lax.all_to_all(partial_value.reshape(experts, capacity, model_width), 'ep...]
    pallas_call x0 -> x15, Pallas kernels: none -> 121 us  [the longest x2 40.2 us: hidden_units(): pl.pallas_call(kernel, grid_spec=pltpu.PrefetchScalarGridSpec(num_scalar_...]
    dot_general x8 -> x0, matrix products: 93.5 us -> none  [the longest x3 36.6 us: right_product(): lax.dot_general(left, right, (((1,), (1,)), ((), ())), preferred_element_...]
    ppermute x0 -> x30, waiting for transfers between devices: none -> 45 us  [shifted(): return lax.ppermute(value, axis, pairs)]
    all_gather x1 -> x0, waiting for transfers between devices: 30.2 us -> none  [local(): lax.all_gather(scaled, 'etp', axis=1, tiled=True)]
    ppermute x0 -> x30, starting transfers between devices: none -> 29 us  [shifted(): return lax.ppermute(value, axis, pairs)]
    scatter x2 -> x0, local copies, waits for them, and re-layouts: 18.1 us -> none  [place_rows(): jnp.zeros((slot_count, copies.shape[1]), copies.dtype).at[slot_ids]]
    all_to_all x3 -> x0, starting transfers between devices: 15.5 us -> none  [the longest x1 5.94 us: local(): lax.all_to_all(send_in.reshape(experts, capacity, full_width), 'ep', spli...]
  transfers between devices with their start and end apart: 5 -> 30, of which waited for: 5 -> 8; matrix products, arithmetic and copies ran while one was open for 15% -> 1% of each run, Pallas kernels for 0% -> 50%
where the time goes in v2:
time: 210 us; the launch traced here: 209 us
  Pallas kernels  121 us (58%)
  waiting for transfers between devices  45 us (21%)
  starting transfers between devices  29 us (14%)
  local copies, waits for them, and re-layouts  7.53 us (4%)
  other arithmetic  5.63 us (3%)
    ppermute x30, waiting for transfers between devices, shifted(): return lax.ppermute(value, axis, pairs)  45 us
    pallas_call x2, Pallas kernels, hidden_units(): pl.pallas_call(kernel, grid_spec=pltpu.PrefetchScalarGridSpec(num_scalar_...  40.2 us
    pallas_call x4, Pallas kernels, weight_grad(): pl.pallas_call(kernel, grid=(stop - start,), in_specs=[fixed(left), pl.Bl...  35.3 us
    ppermute x30, starting transfers between devices, shifted(): return lax.ppermute(value, axis, pairs)  29 us
    pallas_call x2, Pallas kernels, partials(): pl.pallas_call(kernel, grid_spec=pltpu.PrefetchScalarGridSpec(num_scalar_...  27.7 us
    pallas_call x7, Pallas kernels, whole_call(): pl.pallas_call(body, in_specs=[ANY] * skipped + [SMEM] * len(scalars) + [...  18.1 us
    unnamed x60, local copies, waits for them, and re-layouts  7.53 us
  transfers between devices with their start and end apart: 30, of which 8 were waited for; matrix products, arithmetic and copies ran while one was open for 1% of the time, Pallas kernels for 50%

profile of v2, /device:TPU:0, one launch (start us, length us, event | category | flops | bytes accessed | tf_op | source)
XLA Modules:
  0.0 209.3 jit_solution(10105509058164629081)
XLA Ops:
  0.6 1.8 shard_map.102.refs_1_
  2.4 3.0 %collective-permute-start.1 = (bf16[272,768]{1,0:T(8,128)(2,1)}, bf16[272,768]{1,0:T(8,128)(2,1)S(1)}, u32[]{:S(2)}, u32[]{:S(2)}) collective-permute-start(bf16[272,768]{1,0:T(8,128)(2,1)} %shard_map.102.refs_1_), channel_id=1, source_target_pairs={{0,8},{4,12},{8,16},{12,20},{16,24},{20,28},{24,0},{28,4},{1,9},{5... | collective-permute-start | bytes 1253384 | tf_op jit(solution)/shard_map/ppermute | solution.py:56
  5.5 1.5 collective-permute-start
  7.0 10.4 %collective-permute-done.1.refs_3_ = bf16[272,768]{1,0:T(8,128)(2,1)S(1)} collective-permute-done((bf16[272,768]{1,0:T(8,128)(2,1)}, bf16[272,768]{1,0:T(8,128)(2,1)S(1)}, u32[]{:S(2)}, u32[]{:S(2)}) %collective-permute-start.1) | collective-permute-done | bytes 417824 | tf_op jit(solution)/shard_map/ppermute | solution.py:56
  17.3 1.5 collective-permute-start.2
  18.9 1.7 collective-permute-start.7
  21.3 6.9 %collective-permute-done.2.refs_4_ = bf16[272,768]{1,0:T(8,128)(2,1)S(1)} collective-permute-done((bf16[272,768]{1,0:T(8,128)(2,1)S(1)}, bf16[272,768]{1,0:T(8,128)(2,1)S(1)}, u32[]{:S(2)}, u32[]{:S(2)}) %collective-permute-start.2) | collective-permute-done | bytes 417824 | tf_op jit(solution)/shard_map/ppermute | solution.py:56
  28.9 3.5 %shard_map.103 = (bf16[2,384,768]{2,1,0:T(8,128)(2,1)}, bf16[2,192,768]{2,1,0:T(8,128)(2,1)}, bf16[2,192,768]{2,1,0:T(8,128)(2,1)}, s32[2,2,1,128]{3,2,1,0:T(1,128)}) custom-call(s32[2]{0:T(128)} %pad_add_fusion.1.refs_0_.refs_3_, bf16[272,768]{1,0:T(8,128)(2,1)} %shard_map.102.refs_1_, bf16[272,768]{1,0:T(8,128)(2,1)} %copy-done.17, ...), custom_call_target="tpu_custom_call" | custom-call | bytes 1 | tf_op jit(solution)/shard_map/pallas_call | solution.py:66
  32.4 1.3 collective-permute-start.3
  33.7 1.5 collective-permute-start.4
  35.8 10.6 %collective-permute-done.5.refs_4_ = bf16[272,768]{1,0:T(8,128)(2,1)S(1)} collective-permute-done((bf16[272,768]{1,0:T(8,128)(2,1)}, bf16[272,768]{1,0:T(8,128)(2,1)S(1)}, u32[]{:S(2)}, u32[]{:S(2)}) %collective-permute-start.5) | collective-permute-done | bytes 417824 | tf_op jit(solution)/shard_map/ppermute | solution.py:56
  46.4 1.5 collective-permute-start.6
  47.9 7.3 %collective-permute-done.8.refs_7_ = bf16[272,768]{1,0:T(8,128)(2,1)S(1)} collective-permute-done((bf16[272,768]{1,0:T(8,128)(2,1)S(1)}, bf16[272,768]{1,0:T(8,128)(2,1)S(1)}, u32[]{:S(2)}, u32[]{:S(2)}) %collective-permute-start.8) | collective-permute-done | bytes 417824 | tf_op jit(solution)/shard_map/ppermute | solution.py:56
  57.1 3.5 %shard_map.104 = (bf16[2,384,768]{2,1,0:T(8,128)(2,1)}, bf16[2,192,768]{2,1,0:T(8,128)(2,1)}, bf16[2,192,768]{2,1,0:T(8,128)(2,1)}, s32[2,2,1,128]{3,2,1,0:T(1,128)}) custom-call(bf16[2,384,768]{2,1,0:T(8,128)(2,1)} %get-tuple-element.46.refs_0_, bf16[2,192,768]{2,1,0:T(8,128)(2,1)} %copy-done.6, bf16[2,192,768]{2,1,0:T(8,128)(2,1)} %copy-done.7, ...), custom_call_target="tpu_custom_call" | custom-call | bytes 1 | tf_op jit(solution)/shard_map/pallas_call | solution.py:66
  63.5 20.5 %shard_map.105 = (bf16[768,3072]{1,0:T(8,128)(2,1)}, bf16[768,3072]{1,0:T(8,128)(2,1)}, bf16[1344,768]{1,0:T(8,128)(2,1)}, bf16[1344,768]{1,0:T(8,128)(2,1)}, bf16[1344,768]{1,0:T(8,128)(2,1)}) custom-call(s32[4]{0:T(128)} %pad_add_fusion.order_ref, bf16[2,384,768]{2,1,0:T(8,128)(2,1)} %get-tuple-element.46.refs_0_, ...), custom_call_target="tpu_custom_call" | custom-call | flops 9512681472 | bytes 37306368 | tf_op jit(solution)/shard_map/pallas_call | solution.py:217
  85.0 13.8 %shard_map.106 = (bf16[2,384,768]{2,1,0:T(8,128)(2,1)}, bf16[2,384,768]{2,1,0:T(8,128)(2,1)}) custom-call(s32[4]{0:T(128)} %pad_add_fusion.order_ref, bf16[1344,768]{1,0:T(8,128)(2,1)} %get-tuple-element.59.gpg_ref.refs_12_, bf16[1344,768]{1,0:T(8,128)(2,1)} %get-tuple-element.60.gpu_ref.refs_13_, bf16[1344,3072]{1,0:T(8,128)(2,1)} %bitcast.35, ...), custom_call_target="tpu_custom_call" | custom-call | flops 6341787648 | bytes 20938752 | tf_op jit(solution)/shard_map/pallas_call | solution.py:262
  100.7 19.7 %shard_map.107 = (bf16[768,3072]{1,0:T(8,128)(2,1)}, bf16[768,3072]{1,0:T(8,128)(2,1)}, bf16[1344,768]{1,0:T(8,128)(2,1)}, bf16[1344,768]{1,0:T(8,128)(2,1)}, bf16[1344,768]{1,0:T(8,128)(2,1)}) custom-call(s32[4]{0:T(128)} %pad_add_fusion.order_ref, ...), custom_call_target="tpu_custom_call", output_to_operand_aliasing={{0}: (10, {}), {1}: (11, {}), {2}: (12, {}), {3}: (13, {}),... | custom-call | flops 9512681472 | bytes 37306368 | tf_op jit(solution)/shard_map/pallas_call | solution.py:217
  122.4 13.9 %shard_map.108 = (bf16[2,384,768]{2,1,0:T(8,128)(2,1)}, bf16[2,384,768]{2,1,0:T(8,128)(2,1)}) custom-call(s32[4]{0:T(128)} %pad_add_fusion.order_ref, bf16[1344,768]{1,0:T(8,128)(2,1)} %get-tuple-element.64.gpg_ref.left_ref, bf16[1344,768]{1,0:T(8,128)(2,1)} %get-tuple-element.65.gpu_ref.left_ref, bf16[1344,3072]{1,0:T(8,128)(2,1)} %bitcast.37, ...), custom_call_target="tpu_custom_call" | custom-call | flops 6341787648 | bytes 20938752 | tf_op jit(solution)/shard_map/pallas_call | solution.py:262
  136.2 1.5 collective-permute-start.18
  138.3 7.4 %collective-permute-done.18.refs_3_ = bf16[192,768]{1,0:T(8,128)(2,1)S(1)} collective-permute-done((bf16[192,768]{1,0:T(8,128)(2,1)S(1)}, bf16[192,768]{1,0:T(8,128)(2,1)S(1)}, u32[]{:S(2)}, u32[]{:S(2)}) %collective-permute-start.18) | collective-permute-done | bytes 294944 | tf_op jit(solution)/shard_map/ppermute | solution.py:56
  145.7 1.2 collective-permute-done.19.refs_5_
  147.6 2.5 %shard_map.109 = (bf16[96,768]{1,0:T(8,128)(2,1)}, bf16[96,768]{1,0:T(8,128)(2,1)}, bf16[128,768]{1,0:T(8,128)(2,1)}, bf16[128,768]{1,0:T(8,128)(2,1)}) custom-call(bf16[2,384,768]{2,1,0:T(8,128)(2,1)} %get-tuple-element.79.refs_0_, s32[2,2,1,128]{3,2,1,0:T(1,128)} %get-tuple-element.70.refs_1_, bf16[192,768]{1,0:T(8,128)(2,1)} %get-tuple-element.95.refs_0_.refs_2_, ...), custom_call_target="tpu_custom_call" | custom-call | bytes 1 | tf_op jit(solution)/shard_map/pallas_call | solution.py:66
  151.6 6.8 %shard_map.110.refs_0_ = bf16[1344,3072]{1,0:T(8,128)(2,1)} custom-call(bf16[1344,768]{1,0:T(8,128)(2,1)} %get-tuple-element.62.left_ref, bf16[768,3072]{1,0:T(8,128)(2,1)} %get-tuple-element.63.right_ref, bf16[96,768]{1,0:T(8,128)(2,1)} %get-tuple-element.71.refs_0_.refs_2_, bf16[96,768]{1,0:T(8,128)(2,1)} %get-tuple-element.72.refs_1_, ...), custom_call_target="tpu_custom_call" | custom-call | flops 3170893824 | bytes 8552448 | tf_op jit(solution)/shard_map/pallas_call | solution.py:290
  159.8 2.2 %shard_map.111 = (bf16[128,768]{1,0:T(8,128)(2,1)}, bf16[128,768]{1,0:T(8,128)(2,1)}) custom-call(bf16[1344,3072]{1,0:T(8,128)(2,1)} %shard_map.110.refs_0_, s32[2,2,1,128]{3,2,1,0:T(1,128)} %get-tuple-element.70.refs_1_, bf16[96,768]{1,0:T(8,128)(2,1)} %get-tuple-element.71.refs_0_.refs_2_, bf16[96,768]{1,0:T(8,128)(2,1)} %copy-done.28, ...), custom_call_target="tpu_custom_call" | custom-call | bytes 1 | tf_op jit(solution)/shard_map/pallas_call | solution.py:66
  162.0 4.4 %collective-permute-start.22 = (bf16[128,768]{1,0:T(8,128)(2,1)}, bf16[128,768]{1,0:T(8,128)(2,1)S(1)}, u32[]{:S(2)}, u32[]{:S(2)}) collective-permute-start(bf16[128,768]{1,0:T(8,128)(2,1)} %get-tuple-element.76.refs_2_), channel_id=1, source_target_pairs={{0,24},{4,28},{8,0},{12,4},{16,8},{20,12},{24,16},{28,20},{1,25},{... | collective-permute-start | bytes 589832 | tf_op jit(solution)/shard_map/ppermute | solution.py:56
  168.1 1.4 collective-permute-start.24
  169.6 1.5 collective-permute-start.25
  171.1 7.1 %shard_map.112.refs_0_ = bf16[1344,3072]{1,0:T(8,128)(2,1)} custom-call(bf16[1344,768]{1,0:T(8,128)(2,1)} %get-tuple-element.62.left_ref, bf16[768,3072]{1,0:T(8,128)(2,1)} %get-tuple-element.63.right_ref, bf16[1344,3072]{1,0:T(8,128)(2,1)} %shard_map.110.refs_0_, bf16[128,768]{1,0:T(8,128)(2,1)} %get-tuple-element.75.refs_1_, ...), custom_call_target="tpu_custom_call", output_to_operand_aliasing={{}: (2, {})} | custom-call | flops 3170893824 | bytes 8552448 | tf_op jit(solution)/shard_map/pallas_call | solution.py:290
  178.9 2.5 %shard_map.113 = (bf16[96,768]{1,0:T(8,128)(2,1)}, bf16[96,768]{1,0:T(8,128)(2,1)}, bf16[128,768]{1,0:T(8,128)(2,1)}, bf16[128,768]{1,0:T(8,128)(2,1)}) custom-call(bf16[1344,3072]{1,0:T(8,128)(2,1)} %shard_map.112.refs_0_, s32[2,2,1,128]{3,2,1,0:T(1,128)} %get-tuple-element.81.refs_1_, bf16[192,768]{1,0:T(8,128)(2,1)} %get-tuple-element.91.refs_3_.refs_2_, ...), custom_call_target="tpu_custom_call" | custom-call | bytes 1 | tf_op jit(solution)/shard_map/pallas_call | solution.py:66
  182.5 10.7 %shard_map.114.refs_0_ = bf16[1344,3072]{1,0:T(8,128)(2,1)} custom-call(bf16[1344,768]{1,0:T(8,128)(2,1)} %get-tuple-element.64.gpg_ref.left_ref, bf16[768,3072]{1,0:T(8,128)(2,1)} %get-tuple-element.77.right_ref, bf16[96,768]{1,0:T(8,128)(2,1)} %get-tuple-element.82.refs_0_.refs_2_, bf16[96,768]{1,0:T(8,128)(2,1)} %get-tuple-element.83.refs_1_, ...), custom_call_target="tpu_custom_call" | custom-call | flops 6341787648 | bytes 15040512 | tf_op jit(solution)/shard_map/pallas_call | solution.py:290
  194.5 2.2 %shard_map.115 = (bf16[128,768]{1,0:T(8,128)(2,1)}, bf16[128,768]{1,0:T(8,128)(2,1)}) custom-call(bf16[1344,3072]{1,0:T(8,128)(2,1)} %shard_map.114.refs_0_, s32[2,2,1,128]{3,2,1,0:T(1,128)} %get-tuple-element.81.refs_1_, bf16[96,768]{1,0:T(8,128)(2,1)} %get-tuple-element.82.refs_0_.refs_2_, bf16[96,768]{1,0:T(8,128)(2,1)} %copy-done.27, ...), custom_call_target="tpu_custom_call" | custom-call | bytes 1 | tf_op jit(solution)/shard_map/pallas_call | solution.py:66
  197.3 10.7 %shard_map.116 = bf16[1344,3072]{1,0:T(8,128)(2,1)} custom-call(bf16[1344,768]{1,0:T(8,128)(2,1)} %get-tuple-element.65.gpu_ref.left_ref, bf16[768,3072]{1,0:T(8,128)(2,1)} %get-tuple-element.77.right_ref, bf16[128,768]{1,0:T(8,128)(2,1)} %get-tuple-element.86.refs_0_, bf16[128,768]{1,0:T(8,128)(2,1)} %get-tuple-element.87.refs_1_), custom_call_target="tpu_custom_call" | custom-call | flops 6341787648 | bytes 15040512 | tf_op jit(solution)/shard_map/pallas_call | solution.py:290
  (110 shorter events, 22.6 us)
Async XLA Ops:
  2.4 14.9 %collective-permute-start.1 = (bf16[272,768]{1,0:T(8,128)(2,1)}, bf16[272,768]{1,0:T(8,128)(2,1)S(1)}, u32[]{:S(2)}, u32[]{:S(2)}) collective-permute-start(bf16[272,768]{1,0:T(8,128)(2,1)} %shard_map.102.refs_1_), channel_id=1, source_target_pairs={{0,8},{4,12},{8,16},{12,20},{16,24},{20,28},{24,0},{28,4},{1,9},{5... | collective-permute-start | bytes 1253384 | tf_op jit(solution)/shard_map/ppermute | solution.py:56
  5.5 15.8 %collective-permute-start = (bf16[272,768]{1,0:T(8,128)(2,1)}, bf16[272,768]{1,0:T(8,128)(2,1)S(1)}, u32[]{:S(2)}, u32[]{:S(2)}) collective-permute-start(bf16[272,768]{1,0:T(8,128)(2,1)} %shard_map.102.refs_1_), channel_id=1, source_target_pairs={{0,4},{4,0},{8,12},{12,8},{16,20},{20,16},{24,28},{28,24},{1,5},{5... | collective-permute-start | bytes 1253384 | tf_op jit(solution)/shard_map/ppermute | solution.py:56
  17.3 10.8 %collective-permute-start.2 = (bf16[272,768]{1,0:T(8,128)(2,1)S(1)}, bf16[272,768]{1,0:T(8,128)(2,1)S(1)}, u32[]{:S(2)}, u32[]{:S(2)}) collective-permute-start(bf16[272,768]{1,0:T(8,128)(2,1)S(1)} %collective-permute-done.1.refs_3_), channel_id=1, source_target_pairs={{0,2},{1,3},{2,0},{3,1},{4,6},{5,7},{6,4},{7,5},{8,10},{9,11},{10,... | collective-permute-start | bytes 1253384 | tf_op jit(solution)/shard_map/ppermute | solution.py:56
  18.9 16.3 %collective-permute-start.7 = (bf16[272,768]{1,0:T(8,128)(2,1)}, bf16[272,768]{1,0:T(8,128)(2,1)S(1)}, u32[]{:S(2)}, u32[]{:S(2)}) collective-permute-start(bf16[272,768]{1,0:T(8,128)(2,1)} %shard_map.102.refs_1_), channel_id=1, source_target_pairs={{0,24},{4,28},{8,0},{12,4},{16,8},{20,12},{24,16},{28,20},{1,25},{... | collective-permute-start | bytes 1253384 | tf_op jit(solution)/shard_map/ppermute | solution.py:56
  20.6 25.8 %collective-permute-start.5 = (bf16[272,768]{1,0:T(8,128)(2,1)}, bf16[272,768]{1,0:T(8,128)(2,1)S(1)}, u32[]{:S(2)}, u32[]{:S(2)}) collective-permute-start(bf16[272,768]{1,0:T(8,128)(2,1)} %shard_map.102.refs_1_), channel_id=1, source_target_pairs={{0,16},{4,20},{8,24},{12,28},{16,0},{20,4},{24,8},{28,12},{1,17},{... | collective-permute-start | bytes 1253384 | tf_op jit(solution)/shard_map/ppermute | solution.py:56
  32.4 23.5 %collective-permute-start.3 = (bf16[2,192,768]{2,1,0:T(8,128)(2,1)}, bf16[2,192,768]{2,1,0:T(8,128)(2,1)S(1)}, u32[]{:S(2)}, u32[]{:S(2)}) collective-permute-start(bf16[2,192,768]{2,1,0:T(8,128)(2,1)} %get-tuple-element.47), channel_id=1, source_target_pairs={{0,2},{1,3},{2,0},{3,1},{4,6},{5,7},{6,4},{7,5},{8,10},{9,11},{10,... | collective-permute-start | bytes 1769480 | tf_op jit(solution)/shard_map/ppermute | solution.py:56
  33.7 22.2 %collective-permute-start.4 = (bf16[2,192,768]{2,1,0:T(8,128)(2,1)}, bf16[2,192,768]{2,1,0:T(8,128)(2,1)S(1)}, u32[]{:S(2)}, u32[]{:S(2)}) collective-permute-start(bf16[2,192,768]{2,1,0:T(8,128)(2,1)} %get-tuple-element.48), channel_id=1, source_target_pairs={{0,4},{4,0},{8,12},{12,8},{16,20},{20,16},{24,28},{28,24},{1,5},{5... | collective-permute-start | bytes 1769480 | tf_op jit(solution)/shard_map/ppermute | solution.py:56
  35.2 27.4 %collective-permute-start.12 = (bf16[2,384,768]{2,1,0:T(8,128)(2,1)}, bf16[2,384,768]{2,1,0:T(8,128)(2,1)}, u32[]{:S(2)}, u32[]{:S(2)}) collective-permute-start(bf16[2,384,768]{2,1,0:T(8,128)(2,1)} %get-tuple-element.46.refs_0_), channel_id=1, source_target_pairs={{0,1},{1,0},{2,3},{3,2},{4,5},{5,4},{6,7},{7,6},{8,9},{9,8},{10,11... | collective-permute-start | bytes 3538952 | tf_op jit(solution)/shard_map/ppermute | solution.py:56
  35.2 21.9 %copy-start.12 = (bf16[272,768]{1,0:T(8,128)(2,1)}, bf16[272,768]{1,0:T(8,128)(2,1)S(1)}, u32[]{:S(2)}) copy-start(bf16[272,768]{1,0:T(8,128)(2,1)S(1)} %collective-permute-done.7.refs_6_) | copy-start | bytes 1253380
  35.2 20.0 %collective-permute-start.8 = (bf16[272,768]{1,0:T(8,128)(2,1)S(1)}, bf16[272,768]{1,0:T(8,128)(2,1)S(1)}, u32[]{:S(2)}, u32[]{:S(2)}) collective-permute-start(bf16[272,768]{1,0:T(8,128)(2,1)S(1)} %collective-permute-done.7.refs_6_), channel_id=1, source_target_pairs={{0,2},{1,3},{2,0},{3,1},{4,6},{5,7},{6,4},{7,5},{8,10},{9,11},{10,... | collective-permute-start | bytes 1253384 | tf_op jit(solution)/shard_map/ppermute | solution.py:56
  46.4 9.5 %collective-permute-start.6 = (bf16[272,768]{1,0:T(8,128)(2,1)S(1)}, bf16[272,768]{1,0:T(8,128)(2,1)S(1)}, u32[]{:S(2)}, u32[]{:S(2)}) collective-permute-start(bf16[272,768]{1,0:T(8,128)(2,1)S(1)} %collective-permute-done.5.refs_4_), channel_id=1, source_target_pairs={{0,4},{4,0},{8,12},{12,8},{16,20},{20,16},{24,28},{28,24},{1,5},{5... | collective-permute-start | bytes 1253384 | tf_op jit(solution)/shard_map/ppermute | solution.py:56
  55.9 6.7 %collective-permute-start.13 = (bf16[2,192,768]{2,1,0:T(8,128)(2,1)S(1)}, bf16[2,192,768]{2,1,0:T(8,128)(2,1)S(1)}, u32[]{:S(2)}, u32[]{:S(2)}) collective-permute-start(bf16[2,192,768]{2,1,0:T(8,128)(2,1)S(1)} %collective-permute-done.3.refs_1_.refs_2_), channel_id=1, source_target_pairs={{0,1},{1,0},{2,3},{3,2},{4,5},{5,4},{6,7},{7,6},{8,9},{9,8},{10,11... | collective-permute-start | bytes 1769480 | tf_op jit(solution)/shard_map/ppermute | solution.py:56
  56.0 6.6 %collective-permute-start.14 = (bf16[2,192,768]{2,1,0:T(8,128)(2,1)S(1)}, bf16[2,192,768]{2,1,0:T(8,128)(2,1)}, u32[]{:S(2)}, u32[]{:S(2)}) collective-permute-start(bf16[2,192,768]{2,1,0:T(8,128)(2,1)S(1)} %collective-permute-done.4.refs_2_.refs_4_), channel_id=1, source_target_pairs={{0,1},{1,0},{2,3},{3,2},{4,5},{5,4},{6,7},{7,6},{8,9},{9,8},{10,11... | collective-permute-start | bytes 1769480 | tf_op jit(solution)/shard_map/ppermute | solution.py:56
  60.6 23.3 %collective-permute-start.10 = (bf16[2,192,768]{2,1,0:T(8,128)(2,1)}, bf16[2,192,768]{2,1,0:T(8,128)(2,1)S(1)}, u32[]{:S(2)}, u32[]{:S(2)}) collective-permute-start(bf16[2,192,768]{2,1,0:T(8,128)(2,1)} %get-tuple-element.50), channel_id=1, source_target_pairs={{0,2},{1,3},{2,0},{3,1},{4,6},{5,7},{6,4},{7,5},{8,10},{9,11},{10,... | collective-permute-start | bytes 1769480 | tf_op jit(solution)/shard_map/ppermute | solution.py:56
  61.6 22.3 %collective-permute-start.11 = (bf16[2,192,768]{2,1,0:T(8,128)(2,1)}, bf16[2,192,768]{2,1,0:T(8,128)(2,1)S(1)}, u32[]{:S(2)}, u32[]{:S(2)}) collective-permute-start(bf16[2,192,768]{2,1,0:T(8,128)(2,1)} %get-tuple-element.51), channel_id=1, source_target_pairs={{0,4},{4,0},{8,12},{12,8},{16,20},{20,16},{24,28},{28,24},{1,5},{5... | collective-permute-start | bytes 1769480 | tf_op jit(solution)/shard_map/ppermute | solution.py:56
  62.6 36.7 %collective-permute-start.9 = (bf16[2,384,768]{2,1,0:T(8,128)(2,1)}, bf16[2,384,768]{2,1,0:T(8,128)(2,1)S(1)}, u32[]{:S(2)}, u32[]{:S(2)}) collective-permute-start(bf16[2,384,768]{2,1,0:T(8,128)(2,1)} %get-tuple-element.49.refs_9_.refs_0_), channel_id=1, source_target_pairs={{0,1},{1,0},{2,3},{3,2},{4,5},{5,4},{6,7},{7,6},{8,9},{9,8},{10,11... | collective-permute-start | bytes 3538952 | tf_op jit(solution)/shard_map/ppermute | solution.py:56
  84.0 15.4 %collective-permute-start.15 = (bf16[2,192,768]{2,1,0:T(8,128)(2,1)S(1)}, bf16[2,192,768]{2,1,0:T(8,128)(2,1)S(1)}, u32[]{:S(2)}, u32[]{:S(2)}) collective-permute-start(bf16[2,192,768]{2,1,0:T(8,128)(2,1)S(1)} %collective-permute-done.10.refs_0_.refs_2_), channel_id=1, source_target_pairs={{0,1},{1,0},{2,3},{3,2},{4,5},{5,4},{6,7},{7,6},{8,9},{9,8},{10,11... | collective-permute-start | bytes 1769480 | tf_op jit(solution)/shard_map/ppermute | solution.py:56
  84.5 14.8 %collective-permute-start.16 = (bf16[2,192,768]{2,1,0:T(8,128)(2,1)S(1)}, bf16[2,192,768]{2,1,0:T(8,128)(2,1)S(1)}, u32[]{:S(2)}, u32[]{:S(2)}) collective-permute-start(bf16[2,192,768]{2,1,0:T(8,128)(2,1)S(1)} %collective-permute-done.11.refs_1_.refs_4_), channel_id=1, source_target_pairs={{0,1},{1,0},{2,3},{3,2},{4,5},{5,4},{6,7},{7,6},{8,9},{9,8},{10,11... | collective-permute-start | bytes 1769480 | tf_op jit(solution)/shard_map/ppermute | solution.py:56
  98.8 21.7 %collective-permute-start.17 = (bf16[2,384,768]{2,1,0:T(8,128)(2,1)}, bf16[2,384,768]{2,1,0:T(8,128)(2,1)S(1)}, u32[]{:S(2)}, u32[]{:S(2)}) collective-permute-start(bf16[2,384,768]{2,1,0:T(8,128)(2,1)} %get-tuple-element.66), channel_id=1, source_target_pairs={{0,1},{1,0},{2,3},{3,2},{4,5},{5,4},{6,7},{7,6},{8,9},{9,8},{10,11... | collective-permute-start | bytes 3538952 | tf_op jit(solution)/shard_map/ppermute | solution.py:56
  100.7 19.7 %copy-start = (bf16[2,384,768]{2,1,0:T(8,128)(2,1)S(1)}, bf16[2,384,768]{2,1,0:T(8,128)(2,1)}, u32[]{:S(2)}) copy-start(bf16[2,384,768]{2,1,0:T(8,128)(2,1)} %get-tuple-element.67.refs_14_) | copy-start | bytes 3538948
  136.2 30.2 %collective-permute-start.23 = (bf16[2,384,768]{2,1,0:T(8,128)(2,1)}, bf16[2,384,768]{2,1,0:T(8,128)(2,1)S(1)}, u32[]{:S(2)}, u32[]{:S(2)}) collective-permute-start(bf16[2,384,768]{2,1,0:T(8,128)(2,1)} %get-tuple-element.78), channel_id=1, source_target_pairs={{0,1},{1,0},{2,3},{3,2},{4,5},{5,4},{6,7},{7,6},{8,9},{9,8},{10,11... | collective-permute-start | bytes 3538952 | tf_op jit(solution)/shard_map/ppermute | solution.py:56
  136.2 9.4 %collective-permute-start.18 = (bf16[192,768]{1,0:T(8,128)(2,1)S(1)}, bf16[192,768]{1,0:T(8,128)(2,1)S(1)}, u32[]{:S(2)}, u32[]{:S(2)}) collective-permute-start(bf16[192,768]{1,0:T(8,128)(2,1)S(1)} %copy-done.22), channel_id=1, source_target_pairs={{0,2},{1,3},{2,0},{3,1},{4,6},{5,7},{6,4},{7,5},{8,10},{9,11},{10,... | collective-permute-start | bytes 884744 | tf_op jit(solution)/shard_map/ppermute | solution.py:56
  137.8 9.1 %collective-permute-start.19 = (bf16[2,96,768]{2,1,0:T(8,128)(2,1)S(1)}, bf16[2,96,768]{2,1,0:T(8,128)(2,1)S(1)}, u32[]{:S(2)}, u32[]{:S(2)}) collective-permute-start(bf16[2,96,768]{2,1,0:T(8,128)(2,1)S(1)} %copy-done.21), channel_id=1, source_target_pairs={{0,4},{4,0},{8,12},{12,8},{16,20},{20,16},{24,28},{28,24},{1,5},{5... | collective-permute-start | bytes 884744 | tf_op jit(solution)/shard_map/ppermute | solution.py:56
  150.0 8.4 %collective-permute-start.20 = (bf16[96,768]{1,0:T(8,128)(2,1)}, bf16[96,768]{1,0:T(8,128)(2,1)S(1)}, u32[]{:S(2)}, u32[]{:S(2)}) collective-permute-start(bf16[96,768]{1,0:T(8,128)(2,1)} %get-tuple-element.72.refs_1_), channel_id=1, source_target_pairs={{0,4},{4,0},{8,12},{12,8},{16,20},{20,16},{24,28},{28,24},{1,5},{5... | collective-permute-start | bytes 442376 | tf_op jit(solution)/shard_map/ppermute | solution.py:56
  150.5 7.9 %collective-permute-start.21 = (bf16[128,768]{1,0:T(8,128)(2,1)}, bf16[128,768]{1,0:T(8,128)(2,1)S(1)}, u32[]{:S(2)}, u32[]{:S(2)}) collective-permute-start(bf16[128,768]{1,0:T(8,128)(2,1)} %get-tuple-element.74.refs_3_), channel_id=1, source_target_pairs={{0,2},{1,3},{2,0},{3,1},{4,6},{5,7},{6,4},{7,5},{8,10},{9,11},{10,... | collective-permute-start | bytes 589832 | tf_op jit(solution)/shard_map/ppermute | solution.py:56
  162.0 46.0 %collective-permute-start.22 = (bf16[128,768]{1,0:T(8,128)(2,1)}, bf16[128,768]{1,0:T(8,128)(2,1)S(1)}, u32[]{:S(2)}, u32[]{:S(2)}) collective-permute-start(bf16[128,768]{1,0:T(8,128)(2,1)} %get-tuple-element.76.refs_2_), channel_id=1, source_target_pairs={{0,24},{4,28},{8,0},{12,4},{16,8},{20,12},{24,16},{28,20},{1,25},{... | collective-permute-start | bytes 589832 | tf_op jit(solution)/shard_map/ppermute | solution.py:56
  168.1 10.0 %collective-permute-start.24 = (bf16[192,768]{1,0:T(8,128)(2,1)S(1)}, bf16[192,768]{1,0:T(8,128)(2,1)S(1)}, u32[]{:S(2)}, u32[]{:S(2)}) collective-permute-start(bf16[192,768]{1,0:T(8,128)(2,1)S(1)} %get-tuple-element.90.refs_4_), channel_id=1, source_target_pairs={{0,2},{1,3},{2,0},{3,1},{4,6},{5,7},{6,4},{7,5},{8,10},{9,11},{10,... | collective-permute-start | bytes 884744 | tf_op jit(solution)/shard_map/ppermute | solution.py:56
  169.6 8.6 %collective-permute-start.25 = (bf16[2,96,768]{2,1,0:T(8,128)(2,1)S(1)}, bf16[2,96,768]{2,1,0:T(8,128)(2,1)S(1)}, u32[]{:S(2)}, u32[]{:S(2)}) collective-permute-start(bf16[2,96,768]{2,1,0:T(8,128)(2,1)S(1)} %get-tuple-element.88.refs_6_), channel_id=1, source_target_pairs={{0,4},{4,0},{8,12},{12,8},{16,20},{20,16},{24,28},{28,24},{1,5},{5... | collective-permute-start | bytes 884744 | tf_op jit(solution)/shard_map/ppermute | solution.py:56
  181.4 11.8 %collective-permute-start.26 = (bf16[96,768]{1,0:T(8,128)(2,1)}, bf16[96,768]{1,0:T(8,128)(2,1)S(1)}, u32[]{:S(2)}, u32[]{:S(2)}) collective-permute-start(bf16[96,768]{1,0:T(8,128)(2,1)} %get-tuple-element.83.refs_1_), channel_id=1, source_target_pairs={{0,4},{4,0},{8,12},{12,8},{16,20},{20,16},{24,28},{28,24},{1,5},{5... | collective-permute-start | bytes 442376 | tf_op jit(solution)/shard_map/ppermute | solution.py:56
  181.9 11.3 %collective-permute-start.27 = (bf16[128,768]{1,0:T(8,128)(2,1)}, bf16[128,768]{1,0:T(8,128)(2,1)S(1)}, u32[]{:S(2)}, u32[]{:S(2)}) collective-permute-start(bf16[128,768]{1,0:T(8,128)(2,1)} %get-tuple-element.85.refs_3_), channel_id=1, source_target_pairs={{0,2},{1,3},{2,0},{3,1},{4,6},{5,7},{6,4},{7,5},{8,10},{9,11},{10,... | collective-permute-start | bytes 589832 | tf_op jit(solution)/shard_map/ppermute | solution.py:56
  196.8 11.7 %collective-permute-start.28 = (bf16[128,768]{1,0:T(8,128)(2,1)}, bf16[128,768]{1,0:T(8,128)(2,1)S(1)}, u32[]{:S(2)}, u32[]{:S(2)}) collective-permute-start(bf16[128,768]{1,0:T(8,128)(2,1)} %get-tuple-element.86.refs_0_), channel_id=1, source_target_pairs={{0,16},{4,20},{8,24},{12,28},{16,0},{20,4},{24,8},{28,12},{1,17},{... | collective-permute-start | bytes 589832 | tf_op jit(solution)/shard_map/ppermute | solution.py:56
  196.8 11.7 %collective-permute-start.29 = (bf16[128,768]{1,0:T(8,128)(2,1)}, bf16[128,768]{1,0:T(8,128)(2,1)S(1)}, u32[]{:S(2)}, u32[]{:S(2)}) collective-permute-start(bf16[128,768]{1,0:T(8,128)(2,1)} %get-tuple-element.87.refs_1_), channel_id=1, source_target_pairs={{0,8},{4,12},{8,16},{12,20},{16,24},{20,28},{24,0},{28,4},{1,9},{5... | collective-permute-start | bytes 589832 | tf_op jit(solution)/shard_map/ppermute | solution.py:56
  (28 other events, 102.9 us)

commit v3 on v2

--- a/solution.py
+++ b/solution.py
@@ -10,7 +10,6 @@
 DEPTH = 4
 PAIRS = ((0, 1), (2, 3))
 TILES = 6
-COLUMN_PARTS = 4
 ROUTING_ROWS = 16
 ANY = pl.BlockSpec(memory_space=pl.ANY)
 VMEM = pl.BlockSpec(memory_space=pltpu.VMEM)
@@ -278,30 +277,48 @@
     )(order, *lefts, *weights[:2], *after)
 
 
-def weight_grad(left, right, parts, held, after):
-    ff, rows = left.shape
-    full = right.shape[1]
-    part = full // COLUMN_PARTS
-    start, stop = parts
-
-    def kernel(left_ref, right_ref, *refs):
-        refs[-1][...] = product(left_ref[...], right_ref[...]).astype(jnp.bfloat16)
-
+def partials_of_core(chunk, chunks, order, dc, lefts, weights, ranges, turn, after):
+    ff, full = weights[0].shape
+    rows = lefts[0].shape[1] // chunks if turn else lefts[0].shape[0]
+    width = full // (CORES * ranges)
+
+    def kernel(order_ref, lg_ref, lu_ref, wg_ref, wu_ref, *refs):
+        refs = refs[len(after) :]
+        if turn:
+
+            @pl.when(pl.program_id(0) == 0)
+            def _():
+                refs[1][...] = lg_ref[...].T
+                refs[2][...] = lu_ref[...].T
+
+            lg_ref, lu_ref = refs[1:]
+        value = product(lg_ref[...], wg_ref[...]) + product(lu_ref[...], wu_ref[...])
+        refs[0][0] = value.astype(jnp.bfloat16)
+
+    right = pl.BlockSpec((ff, width), lambda r, order: (0, order[dc * ranges + r]))
+    turned = pl.BlockSpec((rows, ff), lambda r, _: (0, 0))
+    left = pl.BlockSpec((ff, rows), lambda r, _: (0, chunk)) if turn else turned
     return pl.pallas_call(
         kernel,
-        grid=(stop - start,),
-        in_specs=[fixed(left), pl.BlockSpec((rows, part), lambda n: (0, start + n))]
-        + [ANY] * (len(held) + len(after)),
-        out_specs=pl.BlockSpec((ff, part), lambda n: (0, start + n)),
-        out_shape=half(ff, full),
-        input_output_aliases={2: 0} if held else {},
+        grid_spec=pltpu.PrefetchScalarGridSpec(
+            num_scalar_prefetch=1,
+            grid=(ranges,),
+            in_specs=[left, left, right, right] + [ANY] * len(after),
+            out_specs=[pl.BlockSpec((1, rows, width), lambda r, _: (r, 0, 0))]
+            + [turned] * (2 * turn),
+        ),
+        out_shape=[half(ranges, rows, width)] + [half(rows, ff)] * (2 * turn),
         compiler_params=params(),
         cost_estimate=pl.CostEstimate(
-            flops=2 * rows * ff * part * (stop - start),
-            bytes_accessed=2 * (rows * ff + part * (stop - start) * (ff + rows)),
+            flops=4 * rows * ff * full // CORES,
+            bytes_accessed=2 * ff * full + rows * full + 4 * rows * ff,
             transcendentals=0,
         ),
-    )(left, right, *held, *after)
+    )(order, *lefts, *weights[:2], *after)
+
+
+def weight_grad(left, right, after):
+    return product(ordered(left, after), right).astype(jnp.bfloat16)
 
 
 def first_returns(own, other, sizes):
@@ -462,9 +479,8 @@
     def sums(chunk, carried, after):
         return partials(chunk, len(PAIRS), order, carried[3:], weights, ranges, after)
 
-    def first_step(parts, after):
-        own, other = ordered((parts[0], along_c(parts[1], -1)), after)
-        even, odd = first_returns(own, other, sizes)
+    def first_step(own, other, after):
+        even, odd = first_returns(*ordered((own, other), after), sizes)
         arrived = [along_y(a, -dy) for dy, a in enumerate(even)]
         return (*even, *odd), arrived, [along_x(a, -dx) for dx, a in enumerate(odd)]
 
@@ -485,19 +501,21 @@
     arrays_b = [arrays_b[0], *ordered(tuple(arrays_b[1:]), (carried[2],))]
     parts_a = sums(0, carried, tuple(arrays_b[1:]))
     carried = units(1, names, arrays_b, carried, (parts_a[0],))
-    done, even_a, odd_a = first_step(parts_a, (carried[2],))
-    parts_b = sums(1, carried, done)
     x_all, g_all, hidden, grad_pre_gate, grad_pre_up = carried
-    done, even_a, odd_a = second_step(pos_a, even_a, odd_a, (parts_b[0],))
-    middle, end = COLUMN_PARTS // 2, COLUMN_PARTS
-    grad_down = weight_grad(hidden, g_all, (0, middle), [], done)
-    done_a, returned_a = third_step(PAIRS[0], pos_a, even_a, odd_a, (grad_down,))
-    done, even_b, odd_b = first_step(parts_b, (grad_down,))
-    grad_down = weight_grad(hidden, g_all, (middle, end), [grad_down], done_a + done)
+    done, even_a, odd_a = first_step(parts_a[0], along_c(parts_a[1], -1), (hidden,))
+    other_b, *lefts = partials_of_core(
+        1, len(PAIRS), order, 1, carried[3:], weights, ranges, True, done
+    )
+    done, even_a, odd_a = second_step(pos_a, even_a, odd_a, (other_b,))
+    other_b = along_c(ordered(other_b, done), -1)
+    (own_b,) = partials_of_core(1, len(PAIRS), order, 0, lefts, weights, ranges, False, done)
+    done, even_b, odd_b = first_step(own_b, other_b, ())
+    done_a, returned_a = third_step(PAIRS[0], pos_a, even_a, odd_a, done)
+    grad_down = weight_grad(hidden, g_all, done + done_a)
     done, even_b, odd_b = second_step(pos_b, even_b, odd_b, (grad_down,))
-    grad_gate = weight_grad(grad_pre_gate, x_all, (0, end), [], done)
+    grad_gate = weight_grad(grad_pre_gate, x_all, done)
     done, returned_b = third_step(PAIRS[1], pos_b, even_b, odd_b, (grad_gate,))
-    grad_up = weight_grad(grad_pre_up, x_all, (0, end), [], done)
+    grad_up = weight_grad(grad_pre_up, x_all, done)
     grad_tokens = add_up(returned_a + returned_b)
     return (grad_tokens, grad_gate.T[None], grad_up.T[None], grad_down[None])
 

time: 210 us -> 204 us (0.971)
  matrix products: 0 us -> 32.8 us
  Pallas kernels: 121 us -> 89.9 us
  waiting for transfers between devices: 45 us -> 36.9 us
    dot_general x0 -> x3, matrix products: none -> 32.8 us  [product(): return jnp.dot(left, right, preferred_element_type=jnp.float32)]
    pallas_call x4 -> x2, Pallas kernels: 35.3 us -> 17.4 us  [partials_of_core(): pl.pallas_call(kernel, grid_spec=pltpu.PrefetchScalarGridSpec(num_scalar_...]
    pallas_call x2 -> x1, Pallas kernels: 27.7 us -> 13.9 us  [partials(): pl.pallas_call(kernel, grid_spec=pltpu.PrefetchScalarGridSpec(num_scalar_...]
    ppermute x30, waiting for transfers between devices: 45 us -> 36.9 us  [shifted(): return lax.ppermute(value, axis, pairs)]
  transfers between devices with their start and end apart: 30 -> 30, of which waited for: 8 -> 6; matrix products, arithmetic and copies ran while one was open for 1% -> 18% of each run, Pallas kernels for 50% -> 42%
where the time goes in v3:
time: 204 us; the launch traced here: 203 us
  Pallas kernels  89.9 us (44%)
  waiting for transfers between devices  36.9 us (18%)
  matrix products  32.8 us (16%)
  starting transfers between devices  29.8 us (15%)
  other arithmetic  6.59 us (3%)
  local copies, waits for them, and re-layouts  6.25 us (3%)
    pallas_call x2, Pallas kernels, hidden_units(): pl.pallas_call(kernel, grid_spec=pltpu.PrefetchScalarGridSpec(num_scalar_...  40.2 us
    ppermute x30, waiting for transfers between devices, shifted(): return lax.ppermute(value, axis, pairs)  36.9 us
    dot_general x3, matrix products, product(): return jnp.dot(left, right, preferred_element_type=jnp.float32)  32.8 us
    ppermute x30, starting transfers between devices, shifted(): return lax.ppermute(value, axis, pairs)  29.8 us
    pallas_call x7, Pallas kernels, whole_call(): pl.pallas_call(body, in_specs=[ANY] * skipped + [SMEM] * len(scalars) + [...  18.4 us
    pallas_call x2, Pallas kernels, partials_of_core(): pl.pallas_call(kernel, grid_spec=pltpu.PrefetchScalarGridSpec(num_scalar_...  17.4 us
    pallas_call x1, Pallas kernels, partials(): pl.pallas_call(kernel, grid_spec=pltpu.PrefetchScalarGridSpec(num_scalar_...  13.9 us
    unnamed x60, local copies, waits for them, and re-layouts  6.25 us
  transfers between devices with their start and end apart: 30, of which 6 were waited for; matrix products, arithmetic and copies ran while one was open for 18% of the time, Pallas kernels for 42%

profile of v3, /device:TPU:0, one launch (start us, length us, event | category | flops | bytes accessed | tf_op | source)
XLA Modules:
  0.0 203.0 jit_solution(14429781045253454567)
XLA Ops:
  0.6 1.8 shard_map.102.refs_1_
  2.5 3.0 %collective-permute-start.1 = (bf16[272,768]{1,0:T(8,128)(2,1)}, bf16[272,768]{1,0:T(8,128)(2,1)S(1)}, u32[]{:S(2)}, u32[]{:S(2)}) collective-permute-start(bf16[272,768]{1,0:T(8,128)(2,1)} %shard_map.102.refs_1_), channel_id=1, source_target_pairs={{0,8},{4,12},{8,16},{12,20},{16,24},{20,28},{24,0},{28,4},{1,9},{5... | collective-permute-start | bytes 1253384 | tf_op jit(solution)/shard_map/ppermute | solution.py:55
  5.5 1.5 collective-permute-start
  7.0 10.4 %collective-permute-done.1.refs_3_ = bf16[272,768]{1,0:T(8,128)(2,1)S(1)} collective-permute-done((bf16[272,768]{1,0:T(8,128)(2,1)}, bf16[272,768]{1,0:T(8,128)(2,1)S(1)}, u32[]{:S(2)}, u32[]{:S(2)}) %collective-permute-start.1) | collective-permute-done | bytes 417824 | tf_op jit(solution)/shard_map/ppermute | solution.py:55
  17.4 1.5 collective-permute-start.2
  18.9 1.7 collective-permute-start.7
  21.3 6.9 %collective-permute-done.2.refs_4_ = bf16[272,768]{1,0:T(8,128)(2,1)S(1)} collective-permute-done((bf16[272,768]{1,0:T(8,128)(2,1)S(1)}, bf16[272,768]{1,0:T(8,128)(2,1)S(1)}, u32[]{:S(2)}, u32[]{:S(2)}) %collective-permute-start.2) | collective-permute-done | bytes 417824 | tf_op jit(solution)/shard_map/ppermute | solution.py:55
  28.9 3.5 %shard_map.103 = (bf16[2,384,768]{2,1,0:T(8,128)(2,1)}, bf16[2,192,768]{2,1,0:T(8,128)(2,1)}, bf16[2,192,768]{2,1,0:T(8,128)(2,1)}, s32[2,2,1,128]{3,2,1,0:T(1,128)}) custom-call(s32[2]{0:T(128)} %pad_add_fusion.1.refs_0_.refs_3_, bf16[272,768]{1,0:T(8,128)(2,1)} %shard_map.102.refs_1_, bf16[272,768]{1,0:T(8,128)(2,1)} %copy-done.19, ...), custom_call_target="tpu_custom_call" | custom-call | bytes 1 | tf_op jit(solution)/shard_map/pallas_call | solution.py:65
  32.4 1.3 collective-permute-start.3
  33.7 1.5 collective-permute-start.4
  35.8 10.6 %collective-permute-done.5.refs_4_ = bf16[272,768]{1,0:T(8,128)(2,1)S(1)} collective-permute-done((bf16[272,768]{1,0:T(8,128)(2,1)}, bf16[272,768]{1,0:T(8,128)(2,1)S(1)}, u32[]{:S(2)}, u32[]{:S(2)}) %collective-permute-start.5) | collective-permute-done | bytes 417824 | tf_op jit(solution)/shard_map/ppermute | solution.py:55
  46.4 1.5 collective-permute-start.6
  47.9 7.3 %collective-permute-done.8.refs_7_ = bf16[272,768]{1,0:T(8,128)(2,1)S(1)} collective-permute-done((bf16[272,768]{1,0:T(8,128)(2,1)S(1)}, bf16[272,768]{1,0:T(8,128)(2,1)S(1)}, u32[]{:S(2)}, u32[]{:S(2)}) %collective-permute-start.8) | collective-permute-done | bytes 417824 | tf_op jit(solution)/shard_map/ppermute | solution.py:55
  57.1 3.5 %shard_map.104 = (bf16[2,384,768]{2,1,0:T(8,128)(2,1)}, bf16[2,192,768]{2,1,0:T(8,128)(2,1)}, bf16[2,192,768]{2,1,0:T(8,128)(2,1)}, s32[2,2,1,128]{3,2,1,0:T(1,128)}) custom-call(bf16[2,384,768]{2,1,0:T(8,128)(2,1)} %get-tuple-element.49.refs_0_, bf16[2,192,768]{2,1,0:T(8,128)(2,1)} %copy-done.8, bf16[2,192,768]{2,1,0:T(8,128)(2,1)} %copy-done.9, ...), custom_call_target="tpu_custom_call" | custom-call | bytes 1 | tf_op jit(solution)/shard_map/pallas_call | solution.py:65
  63.4 20.5 %shard_map.105 = (bf16[768,3072]{1,0:T(8,128)(2,1)}, bf16[768,3072]{1,0:T(8,128)(2,1)}, bf16[1344,768]{1,0:T(8,128)(2,1)}, bf16[1344,768]{1,0:T(8,128)(2,1)}, bf16[1344,768]{1,0:T(8,128)(2,1)}) custom-call(s32[4]{0:T(128)} %pad_add_fusion.order_ref, bf16[2,384,768]{2,1,0:T(8,128)(2,1)} %get-tuple-element.49.refs_0_, ...), custom_call_target="tpu_custom_call" | custom-call | flops 9512681472 | bytes 37306368 | tf_op jit(solution)/shard_map/pallas_call | solution.py:216
  85.0 13.9 %shard_map.106 = (bf16[2,384,768]{2,1,0:T(8,128)(2,1)}, bf16[2,384,768]{2,1,0:T(8,128)(2,1)}) custom-call(s32[4]{0:T(128)} %pad_add_fusion.order_ref, bf16[1344,768]{1,0:T(8,128)(2,1)} %get-tuple-element.62.gpg_ref.refs_12_, bf16[1344,768]{1,0:T(8,128)(2,1)} %get-tuple-element.63.gpu_ref.refs_13_, bf16[1344,3072]{1,0:T(8,128)(2,1)} %bitcast.36, ...), custom_call_target="tpu_custom_call" | custom-call | flops 6341787648 | bytes 20938752 | tf_op jit(solution)/shard_map/pallas_call | solution.py:261
  100.7 19.7 %shard_map.107 = (bf16[768,3072]{1,0:T(8,128)(2,1)}, bf16[768,3072]{1,0:T(8,128)(2,1)}, bf16[1344,768]{1,0:T(8,128)(2,1)}, bf16[1344,768]{1,0:T(8,128)(2,1)}, bf16[1344,768]{1,0:T(8,128)(2,1)}) custom-call(s32[4]{0:T(128)} %pad_add_fusion.order_ref, ...), custom_call_target="tpu_custom_call", output_to_operand_aliasing={{0}: (10, {}), {1}: (11, {}), {2}: (12, {}), {3}: (13, {}),... | custom-call | flops 9512681472 | bytes 37306368 | tf_op jit(solution)/shard_map/pallas_call | solution.py:216
  122.1 1.5 collective-permute-start.18
  124.2 8.9 %shard_map.108 = (bf16[2,384,768]{2,1,0:T(8,128)(2,1)}, bf16[384,1344]{1,0:T(8,128)(2,1)}, bf16[384,1344]{1,0:T(8,128)(2,1)}) custom-call(s32[4]{0:T(128)} %pad_add_fusion.order_ref, bf16[1344,768]{1,0:T(8,128)(2,1)} %get-tuple-element.89.lg_ref, bf16[1344,768]{1,0:T(8,128)(2,1)} %get-tuple-element.93.lu_ref, bf16[1344,3072]{1,0:T(8,128)(2,1)} %bitcast.38, ...), custom_call_target="tpu_custom_call" | custom-call | flops 3170893824 | bytes 11501568 | tf_op jit(solution)/shard_map/pallas_call | solution.py:301
  133.9 2.6 %shard_map.109 = (bf16[96,768]{1,0:T(8,128)(2,1)}, bf16[96,768]{1,0:T(8,128)(2,1)}, bf16[128,768]{1,0:T(8,128)(2,1)}, bf16[128,768]{1,0:T(8,128)(2,1)}) custom-call(bf16[2,384,768]{2,1,0:T(8,128)(2,1)} %get-tuple-element.79.refs_0_, s32[2,2,1,128]{3,2,1,0:T(1,128)} %get-tuple-element.74.refs_1_.refs_4_, bf16[192,768]{1,0:T(8,128)(2,1)} %get-tuple-element.101.refs_0_.refs_2_, ...), custom_call_target="tpu_custom_call" | custom-call | bytes 1 | tf_op jit(solution)/shard_map/pallas_call | solution.py:65
  136.5 1.5 collective-permute-start.21
  138.6 8.5 %shard_map.110 = bf16[2,384,768]{2,1,0:T(8,128)(2,1)} custom-call(s32[4]{0:T(128)} %pad_add_fusion.order_ref, bf16[384,1344]{1,0:T(8,128)(2,1)} %get-tuple-element.71.lg_ref, bf16[384,1344]{1,0:T(8,128)(2,1)} %get-tuple-element.72.lu_ref, bf16[1344,3072]{1,0:T(8,128)(2,1)} %bitcast.39, bf16[1344,3072]{1,0:T(8,128)(2,1)} %bitcast.44, ...), custom_call_target="tpu_custom_call" | custom-call | flops 3170893824 | bytes 11501568 | tf_op jit(solution)/shard_map/pallas_call | solution.py:301
  147.0 2.0 fusion.4
  149.0 1.5 collective-permute-start.24
  152.0 2.3 %shard_map.111 = (bf16[128,768]{1,0:T(8,128)(2,1)}, bf16[128,768]{1,0:T(8,128)(2,1)}) custom-call(bf16[192,768]{1,0:T(8,128)(2,1)} %get-tuple-element.97.refs_0_.refs_2_, bf16[192,768]{1,0:T(8,128)(2,1)} %copy-done.5, bf16[2,96,768]{2,1,0:T(8,128)(2,1)} %get-tuple-element.95.refs_2_.refs_4_, bf16[2,96,768]{2,1,0:T(8,128)(2,1)} %get-tuple-element.94.refs_3_, ...), custom_call_target="tpu_custom_call" | custom-call | bytes 1 | tf_op jit(solution)/shard_map/pallas_call | solution.py:65
  154.3 4.9 %collective-permute-start.23 = (bf16[128,768]{1,0:T(8,128)(2,1)}, bf16[128,768]{1,0:T(8,128)(2,1)S(1)}, u32[]{:S(2)}, u32[]{:S(2)}) collective-permute-start(bf16[128,768]{1,0:T(8,128)(2,1)} %get-tuple-element.81), channel_id=1, source_target_pairs={{0,24},{4,28},{8,0},{12,4},{16,8},{20,12},{24,16},{28,20},{1,25},{... | collective-permute-start | bytes 589832 | tf_op jit(solution)/shard_map/ppermute | solution.py:55
  159.2 10.6 %convolution_convert_fusion.2.refs_0_ = bf16[1344,3072]{1,0:T(8,128)(2,1)} fusion(bf16[1344,768]{1,0:T(8,128)(2,1)} %get-tuple-element.82, bf16[768,3072]{1,0:T(8,128)(2,1)S(1)} %bitcast.50), kind=kOutput, calls=%fused_computation.2 | convolution fusion | flops 6345916416 | bytes 15040512 | tf_op jit(solution)/shard_map/dot_general | solution.py:20
  170.5 2.6 %shard_map.112 = (bf16[96,768]{1,0:T(8,128)(2,1)}, bf16[96,768]{1,0:T(8,128)(2,1)}, bf16[128,768]{1,0:T(8,128)(2,1)}, bf16[128,768]{1,0:T(8,128)(2,1)}) custom-call(bf16[1344,3072]{1,0:T(8,128)(2,1)} %convolution_convert_fusion.2.refs_0_, s32[2,2,1,128]{3,2,1,0:T(1,128)} %get-tuple-element.84.refs_1_, bf16[192,768]{1,0:T(8,128)(2,1)} %get-tuple-element.97.refs_0_.refs_2_, ...), custom_call_target="tpu_custom_call" | custom-call | bytes 1 | tf_op jit(solution)/shard_map/pallas_call | solution.py:65
  173.1 1.5 collective-permute-start.26
  175.1 11.1 %convolution_convert_fusion.1.refs_0_ = bf16[1344,3072]{1,0:T(8,128)(2,1)} fusion(bf16[1344,768]{1,0:T(8,128)(2,1)S(1)} %copy-done, bf16[768,3072]{1,0:T(8,128)(2,1)} %get-tuple-element.90), kind=kOutput, calls=%fused_computation.1 | convolution fusion | flops 6345916416 | bytes 15040512 | tf_op jit(solution)/shard_map/dot_general | solution.py:20
  187.5 2.2 %shard_map.113 = (bf16[128,768]{1,0:T(8,128)(2,1)}, bf16[128,768]{1,0:T(8,128)(2,1)}) custom-call(bf16[1344,3072]{1,0:T(8,128)(2,1)} %convolution_convert_fusion.1.refs_0_, s32[2,2,1,128]{3,2,1,0:T(1,128)} %get-tuple-element.84.refs_1_, bf16[96,768]{1,0:T(8,128)(2,1)} %get-tuple-element.85.refs_2_, bf16[96,768]{1,0:T(8,128)(2,1)} %copy-done.26, ...), custom_call_target="tpu_custom_call" | custom-call | bytes 1 | tf_op jit(solution)/shard_map/pallas_call | solution.py:65
  190.3 11.1 %fusion = bf16[1,3072,1344]{1,2,0:T(8,128)(2,1)} fusion(bf16[1344,768]{1,0:T(8,128)(2,1)S(1)} %copy-done.1, bf16[768,3072]{1,0:T(8,128)(2,1)} %get-tuple-element.90), kind=kOutput, calls=%fused_computation.3 | convolution fusion | flops 6345916416 | bytes 15040512 | tf_op jit(solution)/shard_map/dot_general | solution.py:20
  (111 shorter events, 19.3 us)
Async XLA Ops:
  2.5 14.9 %collective-permute-start.1 = (bf16[272,768]{1,0:T(8,128)(2,1)}, bf16[272,768]{1,0:T(8,128)(2,1)S(1)}, u32[]{:S(2)}, u32[]{:S(2)}) collective-permute-start(bf16[272,768]{1,0:T(8,128)(2,1)} %shard_map.102.refs_1_), channel_id=1, source_target_pairs={{0,8},{4,12},{8,16},{12,20},{16,24},{20,28},{24,0},{28,4},{1,9},{5... | collective-permute-start | bytes 1253384 | tf_op jit(solution)/shard_map/ppermute | solution.py:55
  5.5 15.8 %collective-permute-start = (bf16[272,768]{1,0:T(8,128)(2,1)}, bf16[272,768]{1,0:T(8,128)(2,1)S(1)}, u32[]{:S(2)}, u32[]{:S(2)}) collective-permute-start(bf16[272,768]{1,0:T(8,128)(2,1)} %shard_map.102.refs_1_), channel_id=1, source_target_pairs={{0,4},{4,0},{8,12},{12,8},{16,20},{20,16},{24,28},{28,24},{1,5},{5... | collective-permute-start | bytes 1253384 | tf_op jit(solution)/shard_map/ppermute | solution.py:55
  17.4 10.8 %collective-permute-start.2 = (bf16[272,768]{1,0:T(8,128)(2,1)S(1)}, bf16[272,768]{1,0:T(8,128)(2,1)S(1)}, u32[]{:S(2)}, u32[]{:S(2)}) collective-permute-start(bf16[272,768]{1,0:T(8,128)(2,1)S(1)} %collective-permute-done.1.refs_3_), channel_id=1, source_target_pairs={{0,2},{1,3},{2,0},{3,1},{4,6},{5,7},{6,4},{7,5},{8,10},{9,11},{10,... | collective-permute-start | bytes 1253384 | tf_op jit(solution)/shard_map/ppermute | solution.py:55
  18.9 16.3 %collective-permute-start.7 = (bf16[272,768]{1,0:T(8,128)(2,1)}, bf16[272,768]{1,0:T(8,128)(2,1)S(1)}, u32[]{:S(2)}, u32[]{:S(2)}) collective-permute-start(bf16[272,768]{1,0:T(8,128)(2,1)} %shard_map.102.refs_1_), channel_id=1, source_target_pairs={{0,24},{4,28},{8,0},{12,4},{16,8},{20,12},{24,16},{28,20},{1,25},{... | collective-permute-start | bytes 1253384 | tf_op jit(solution)/shard_map/ppermute | solution.py:55
  20.6 25.8 %collective-permute-start.5 = (bf16[272,768]{1,0:T(8,128)(2,1)}, bf16[272,768]{1,0:T(8,128)(2,1)S(1)}, u32[]{:S(2)}, u32[]{:S(2)}) collective-permute-start(bf16[272,768]{1,0:T(8,128)(2,1)} %shard_map.102.refs_1_), channel_id=1, source_target_pairs={{0,16},{4,20},{8,24},{12,28},{16,0},{20,4},{24,8},{28,12},{1,17},{... | collective-permute-start | bytes 1253384 | tf_op jit(solution)/shard_map/ppermute | solution.py:55
  32.4 23.5 %collective-permute-start.3 = (bf16[2,192,768]{2,1,0:T(8,128)(2,1)}, bf16[2,192,768]{2,1,0:T(8,128)(2,1)S(1)}, u32[]{:S(2)}, u32[]{:S(2)}) collective-permute-start(bf16[2,192,768]{2,1,0:T(8,128)(2,1)} %get-tuple-element.50), channel_id=1, source_target_pairs={{0,2},{1,3},{2,0},{3,1},{4,6},{5,7},{6,4},{7,5},{8,10},{9,11},{10,... | collective-permute-start | bytes 1769480 | tf_op jit(solution)/shard_map/ppermute | solution.py:55
  33.7 22.2 %collective-permute-start.4 = (bf16[2,192,768]{2,1,0:T(8,128)(2,1)}, bf16[2,192,768]{2,1,0:T(8,128)(2,1)S(1)}, u32[]{:S(2)}, u32[]{:S(2)}) collective-permute-start(bf16[2,192,768]{2,1,0:T(8,128)(2,1)} %get-tuple-element.51), channel_id=1, source_target_pairs={{0,4},{4,0},{8,12},{12,8},{16,20},{20,16},{24,28},{28,24},{1,5},{5... | collective-permute-start | bytes 1769480 | tf_op jit(solution)/shard_map/ppermute | solution.py:55
  35.2 27.4 %collective-permute-start.12 = (bf16[2,384,768]{2,1,0:T(8,128)(2,1)}, bf16[2,384,768]{2,1,0:T(8,128)(2,1)}, u32[]{:S(2)}, u32[]{:S(2)}) collective-permute-start(bf16[2,384,768]{2,1,0:T(8,128)(2,1)} %get-tuple-element.49.refs_0_), channel_id=1, source_target_pairs={{0,1},{1,0},{2,3},{3,2},{4,5},{5,4},{6,7},{7,6},{8,9},{9,8},{10,11... | collective-permute-start | bytes 3538952 | tf_op jit(solution)/shard_map/ppermute | solution.py:55
  35.2 21.9 %copy-start.14 = (bf16[272,768]{1,0:T(8,128)(2,1)}, bf16[272,768]{1,0:T(8,128)(2,1)S(1)}, u32[]{:S(2)}) copy-start(bf16[272,768]{1,0:T(8,128)(2,1)S(1)} %collective-permute-done.7.refs_6_) | copy-start | bytes 1253380
  35.2 20.0 %collective-permute-start.8 = (bf16[272,768]{1,0:T(8,128)(2,1)S(1)}, bf16[272,768]{1,0:T(8,128)(2,1)S(1)}, u32[]{:S(2)}, u32[]{:S(2)}) collective-permute-start(bf16[272,768]{1,0:T(8,128)(2,1)S(1)} %collective-permute-done.7.refs_6_), channel_id=1, source_target_pairs={{0,2},{1,3},{2,0},{3,1},{4,6},{5,7},{6,4},{7,5},{8,10},{9,11},{10,... | collective-permute-start | bytes 1253384 | tf_op jit(solution)/shard_map/ppermute | solution.py:55
  46.4 9.5 %collective-permute-start.6 = (bf16[272,768]{1,0:T(8,128)(2,1)S(1)}, bf16[272,768]{1,0:T(8,128)(2,1)S(1)}, u32[]{:S(2)}, u32[]{:S(2)}) collective-permute-start(bf16[272,768]{1,0:T(8,128)(2,1)S(1)} %collective-permute-done.5.refs_4_), channel_id=1, source_target_pairs={{0,4},{4,0},{8,12},{12,8},{16,20},{20,16},{24,28},{28,24},{1,5},{5... | collective-permute-start | bytes 1253384 | tf_op jit(solution)/shard_map/ppermute | solution.py:55
  55.9 6.7 %collective-permute-start.13 = (bf16[2,192,768]{2,1,0:T(8,128)(2,1)S(1)}, bf16[2,192,768]{2,1,0:T(8,128)(2,1)S(1)}, u32[]{:S(2)}, u32[]{:S(2)}) collective-permute-start(bf16[2,192,768]{2,1,0:T(8,128)(2,1)S(1)} %collective-permute-done.3.refs_1_.refs_2_), channel_id=1, source_target_pairs={{0,1},{1,0},{2,3},{3,2},{4,5},{5,4},{6,7},{7,6},{8,9},{9,8},{10,11... | collective-permute-start | bytes 1769480 | tf_op jit(solution)/shard_map/ppermute | solution.py:55
  56.0 6.6 %collective-permute-start.14 = (bf16[2,192,768]{2,1,0:T(8,128)(2,1)S(1)}, bf16[2,192,768]{2,1,0:T(8,128)(2,1)}, u32[]{:S(2)}, u32[]{:S(2)}) collective-permute-start(bf16[2,192,768]{2,1,0:T(8,128)(2,1)S(1)} %collective-permute-done.4.refs_2_.refs_4_), channel_id=1, source_target_pairs={{0,1},{1,0},{2,3},{3,2},{4,5},{5,4},{6,7},{7,6},{8,9},{9,8},{10,11... | collective-permute-start | bytes 1769480 | tf_op jit(solution)/shard_map/ppermute | solution.py:55
  60.6 23.3 %collective-permute-start.10 = (bf16[2,192,768]{2,1,0:T(8,128)(2,1)}, bf16[2,192,768]{2,1,0:T(8,128)(2,1)S(1)}, u32[]{:S(2)}, u32[]{:S(2)}) collective-permute-start(bf16[2,192,768]{2,1,0:T(8,128)(2,1)} %get-tuple-element.53), channel_id=1, source_target_pairs={{0,2},{1,3},{2,0},{3,1},{4,6},{5,7},{6,4},{7,5},{8,10},{9,11},{10,... | collective-permute-start | bytes 1769480 | tf_op jit(solution)/shard_map/ppermute | solution.py:55
  61.6 22.4 %collective-permute-start.11 = (bf16[2,192,768]{2,1,0:T(8,128)(2,1)}, bf16[2,192,768]{2,1,0:T(8,128)(2,1)S(1)}, u32[]{:S(2)}, u32[]{:S(2)}) collective-permute-start(bf16[2,192,768]{2,1,0:T(8,128)(2,1)} %get-tuple-element.54), channel_id=1, source_target_pairs={{0,4},{4,0},{8,12},{12,8},{16,20},{20,16},{24,28},{28,24},{1,5},{5... | collective-permute-start | bytes 1769480 | tf_op jit(solution)/shard_map/ppermute | solution.py:55
  62.6 36.7 %collective-permute-start.9 = (bf16[2,384,768]{2,1,0:T(8,128)(2,1)}, bf16[2,384,768]{2,1,0:T(8,128)(2,1)S(1)}, u32[]{:S(2)}, u32[]{:S(2)}) collective-permute-start(bf16[2,384,768]{2,1,0:T(8,128)(2,1)} %get-tuple-element.52.refs_9_.refs_0_), channel_id=1, source_target_pairs={{0,1},{1,0},{2,3},{3,2},{4,5},{5,4},{6,7},{7,6},{8,9},{9,8},{10,11... | collective-permute-start | bytes 3538952 | tf_op jit(solution)/shard_map/ppermute | solution.py:55
  84.0 15.3 %collective-permute-start.15 = (bf16[2,192,768]{2,1,0:T(8,128)(2,1)S(1)}, bf16[2,192,768]{2,1,0:T(8,128)(2,1)S(1)}, u32[]{:S(2)}, u32[]{:S(2)}) collective-permute-start(bf16[2,192,768]{2,1,0:T(8,128)(2,1)S(1)} %collective-permute-done.10.refs_0_.refs_2_), channel_id=1, source_target_pairs={{0,1},{1,0},{2,3},{3,2},{4,5},{5,4},{6,7},{7,6},{8,9},{9,8},{10,11... | collective-permute-start | bytes 1769480 | tf_op jit(solution)/shard_map/ppermute | solution.py:55
  84.5 14.8 %collective-permute-start.16 = (bf16[2,192,768]{2,1,0:T(8,128)(2,1)S(1)}, bf16[2,192,768]{2,1,0:T(8,128)(2,1)S(1)}, u32[]{:S(2)}, u32[]{:S(2)}) collective-permute-start(bf16[2,192,768]{2,1,0:T(8,128)(2,1)S(1)} %collective-permute-done.11.refs_1_.refs_4_), channel_id=1, source_target_pairs={{0,1},{1,0},{2,3},{3,2},{4,5},{5,4},{6,7},{7,6},{8,9},{9,8},{10,11... | collective-permute-start | bytes 1769480 | tf_op jit(solution)/shard_map/ppermute | solution.py:55
  98.9 21.5 %collective-permute-start.17 = (bf16[2,384,768]{2,1,0:T(8,128)(2,1)}, bf16[2,384,768]{2,1,0:T(8,128)(2,1)S(1)}, u32[]{:S(2)}, u32[]{:S(2)}) collective-permute-start(bf16[2,384,768]{2,1,0:T(8,128)(2,1)} %get-tuple-element.67), channel_id=1, source_target_pairs={{0,1},{1,0},{2,3},{3,2},{4,5},{5,4},{6,7},{7,6},{8,9},{9,8},{10,11... | collective-permute-start | bytes 3538952 | tf_op jit(solution)/shard_map/ppermute | solution.py:55
  122.1 11.0 %collective-permute-start.18 = (bf16[192,768]{1,0:T(8,128)(2,1)S(1)}, bf16[192,768]{1,0:T(8,128)(2,1)S(1)}, u32[]{:S(2)}, u32[]{:S(2)}) collective-permute-start(bf16[192,768]{1,0:T(8,128)(2,1)S(1)} %get-tuple-element.100.refs_1_), channel_id=1, source_target_pairs={{0,2},{1,3},{2,0},{3,1},{4,6},{5,7},{6,4},{7,5},{8,10},{9,11},{10,... | collective-permute-start | bytes 884744 | tf_op jit(solution)/shard_map/ppermute | solution.py:55
  123.6 9.5 %collective-permute-start.19 = (bf16[2,96,768]{2,1,0:T(8,128)(2,1)S(1)}, bf16[2,96,768]{2,1,0:T(8,128)(2,1)S(1)}, u32[]{:S(2)}, u32[]{:S(2)}) collective-permute-start(bf16[2,96,768]{2,1,0:T(8,128)(2,1)S(1)} %get-tuple-element.98.refs_3_), channel_id=1, source_target_pairs={{0,4},{4,0},{8,12},{12,8},{16,20},{20,16},{24,28},{28,24},{1,5},{5... | collective-permute-start | bytes 884744 | tf_op jit(solution)/shard_map/ppermute | solution.py:55
  133.9 25.3 %slice-start = ((s8[4718592]{0:T(1024)(128)(4,1)}), s8[4194304]{0:T(1024)(128)(4,1)S(1)}, s32[]{:S(2)}) async-start(s8[4718592]{0:T(1024)(128)(4,1)} %bitcast.49), calls=%async_computation | async-start | bytes 8388608
  136.5 10.5 %collective-permute-start.20 = (bf16[2,384,768]{2,1,0:T(8,128)(2,1)}, bf16[2,384,768]{2,1,0:T(8,128)(2,1)S(1)}, u32[]{:S(2)}, u32[]{:S(2)}) collective-permute-start(bf16[2,384,768]{2,1,0:T(8,128)(2,1)} %get-tuple-element.79.refs_0_), channel_id=1, source_target_pairs={{0,1},{1,0},{2,3},{3,2},{4,5},{5,4},{6,7},{7,6},{8,9},{9,8},{10,11... | collective-permute-start | bytes 3538952 | tf_op jit(solution)/shard_map/ppermute | solution.py:55
  136.5 15.5 %collective-permute-start.21 = (bf16[96,768]{1,0:T(8,128)(2,1)}, bf16[96,768]{1,0:T(8,128)(2,1)}, u32[]{:S(2)}, u32[]{:S(2)}) collective-permute-start(bf16[96,768]{1,0:T(8,128)(2,1)} %get-tuple-element.76.refs_1_), channel_id=1, source_target_pairs={{0,4},{4,0},{8,12},{12,8},{16,20},{20,16},{24,28},{28,24},{1,5},{5... | collective-permute-start | bytes 442376 | tf_op jit(solution)/shard_map/ppermute | solution.py:55
  138.1 14.0 %collective-permute-start.22 = (bf16[128,768]{1,0:T(8,128)(2,1)}, bf16[128,768]{1,0:T(8,128)(2,1)}, u32[]{:S(2)}, u32[]{:S(2)}) collective-permute-start(bf16[128,768]{1,0:T(8,128)(2,1)} %get-tuple-element.78.refs_3_), channel_id=1, source_target_pairs={{0,2},{1,3},{2,0},{3,1},{4,6},{5,7},{6,4},{7,5},{8,10},{9,11},{10,... | collective-permute-start | bytes 589832 | tf_op jit(solution)/shard_map/ppermute | solution.py:55
  149.0 20.8 %collective-permute-start.24 = (bf16[192,768]{1,0:T(8,128)(2,1)S(1)}, bf16[192,768]{1,0:T(8,128)(2,1)}, u32[]{:S(2)}, u32[]{:S(2)}) collective-permute-start(bf16[192,768]{1,0:T(8,128)(2,1)S(1)} %get-tuple-element.96.refs_1_), channel_id=1, source_target_pairs={{0,2},{1,3},{2,0},{3,1},{4,6},{5,7},{6,4},{7,5},{8,10},{9,11},{10,... | collective-permute-start | bytes 884744 | tf_op jit(solution)/shard_map/ppermute | solution.py:55
  151.5 18.3 %collective-permute-start.25 = (bf16[2,96,768]{2,1,0:T(8,128)(2,1)}, bf16[2,96,768]{2,1,0:T(8,128)(2,1)S(1)}, u32[]{:S(2)}, u32[]{:S(2)}) collective-permute-start(bf16[2,96,768]{2,1,0:T(8,128)(2,1)} %get-tuple-element.94.refs_3_), channel_id=1, source_target_pairs={{0,4},{4,0},{8,12},{12,8},{16,20},{20,16},{24,28},{28,24},{1,5},{5... | collective-permute-start | bytes 884744 | tf_op jit(solution)/shard_map/ppermute | solution.py:55
  154.3 47.1 %collective-permute-start.23 = (bf16[128,768]{1,0:T(8,128)(2,1)}, bf16[128,768]{1,0:T(8,128)(2,1)S(1)}, u32[]{:S(2)}, u32[]{:S(2)}) collective-permute-start(bf16[128,768]{1,0:T(8,128)(2,1)} %get-tuple-element.81), channel_id=1, source_target_pairs={{0,24},{4,28},{8,0},{12,4},{16,8},{20,12},{24,16},{28,20},{1,25},{... | collective-permute-start | bytes 589832 | tf_op jit(solution)/shard_map/ppermute | solution.py:55
  173.1 13.1 %collective-permute-start.26 = (bf16[96,768]{1,0:T(8,128)(2,1)}, bf16[96,768]{1,0:T(8,128)(2,1)S(1)}, u32[]{:S(2)}, u32[]{:S(2)}) collective-permute-start(bf16[96,768]{1,0:T(8,128)(2,1)} %get-tuple-element.86), channel_id=1, source_target_pairs={{0,4},{4,0},{8,12},{12,8},{16,20},{20,16},{24,28},{28,24},{1,5},{5... | collective-permute-start | bytes 442376 | tf_op jit(solution)/shard_map/ppermute | solution.py:55
  174.6 11.6 %collective-permute-start.27 = (bf16[128,768]{1,0:T(8,128)(2,1)}, bf16[128,768]{1,0:T(8,128)(2,1)S(1)}, u32[]{:S(2)}, u32[]{:S(2)}) collective-permute-start(bf16[128,768]{1,0:T(8,128)(2,1)} %get-tuple-element.88), channel_id=1, source_target_pairs={{0,2},{1,3},{2,0},{3,1},{4,6},{5,7},{6,4},{7,5},{8,10},{9,11},{10,... | collective-permute-start | bytes 589832 | tf_op jit(solution)/shard_map/ppermute | solution.py:55
  189.7 12.5 %collective-permute-start.28 = (bf16[128,768]{1,0:T(8,128)(2,1)}, bf16[128,768]{1,0:T(8,128)(2,1)S(1)}, u32[]{:S(2)}, u32[]{:S(2)}) collective-permute-start(bf16[128,768]{1,0:T(8,128)(2,1)} %get-tuple-element.91), channel_id=1, source_target_pairs={{0,16},{4,20},{8,24},{12,28},{16,0},{20,4},{24,8},{28,12},{1,17},{... | collective-permute-start | bytes 589832 | tf_op jit(solution)/shard_map/ppermute | solution.py:55
  189.7 12.5 %collective-permute-start.29 = (bf16[128,768]{1,0:T(8,128)(2,1)}, bf16[128,768]{1,0:T(8,128)(2,1)S(1)}, u32[]{:S(2)}, u32[]{:S(2)}) collective-permute-start(bf16[128,768]{1,0:T(8,128)(2,1)} %get-tuple-element.92), channel_id=1, source_target_pairs={{0,8},{4,12},{8,16},{12,20},{16,24},{20,28},{24,0},{28,4},{1,9},{5... | collective-permute-start | bytes 589832 | tf_op jit(solution)/shard_map/ppermute | solution.py:55
  (28 other events, 117.6 us)

commit v4 on v3

--- a/solution.py
+++ b/solution.py
@@ -72,29 +72,28 @@
     )(*after, *scalars, *args)
 
 
-def pack(tokens, grad_out, probs, expert_ids):
+def pack(tokens, probs, expert_ids):
     tok_rows, width = tokens.shape
 
-    def kernel(t_ref, g_ref, p_ref, id_ref, out_ref):
+    def kernel(t_ref, p_ref, id_ref, out_ref):
         out_ref[:tok_rows, :] = t_ref[...]
-        out_ref[tok_rows : 2 * tok_rows, :] = g_ref[...]
         rest = p_ref[...]
         rows = [id_ref[...].astype(jnp.float32)]
         for _ in range(3):
             part = rest.astype(jnp.bfloat16).astype(jnp.float32)
             rows.append(part)
             rest = rest - part
-        out_ref[2 * tok_rows :, :] = jnp.zeros((ROUTING_ROWS, width), jnp.bfloat16)
-        out_ref[2 * tok_rows :, :tok_rows] = jnp.concatenate(rows, axis=0).astype(jnp.bfloat16)
+        out_ref[tok_rows:, :] = jnp.zeros((ROUTING_ROWS, width), jnp.bfloat16)
+        out_ref[tok_rows:, :tok_rows] = jnp.concatenate(rows, axis=0).astype(jnp.bfloat16)
 
     assert 4 * probs.shape[0] == ROUTING_ROWS
     return whole_call(
-        kernel, [tokens, grad_out, probs, expert_ids], [half(2 * tok_rows + ROUTING_ROWS, width)]
+        kernel, [tokens, probs, expert_ids], [half(tok_rows + ROUTING_ROWS, width)]
     )[0]
 
 
 def routes(ref, tok_rows, expert):
-    rows = ref[2 * tok_rows :, :tok_rows].astype(jnp.float32)
+    rows = ref[tok_rows:, :tok_rows].astype(jnp.float32)
     top = ROUTING_ROWS // 4
     hit = rows[:top] == expert.astype(jnp.float32)
     weights = rows[top : 2 * top] + rows[2 * top : 3 * top] + rows[3 * top :]
@@ -117,43 +116,41 @@
     return hits(pos, capacity).astype(jnp.float32).astype(jnp.bfloat16)
 
 
-def pick_pair(experts, even, odd, capacity, after):
-    blocks, ranges = len(even), len(odd)
-    tok_rows, width = (even[0].shape[0] - ROUTING_ROWS) // 2, even[0].shape[1]
+def pick_pair(experts, held_in, held_grad, capacity, after):
+    steps, blocks, ranges = len(held_in), len(held_in[0]), len(held_grad[0])
+    tok_rows, width = held_grad[0][0].shape
+    rows = steps * blocks * capacity
+    flat_in = [a for group in held_in for a in group]
+    flat_grad = [a for group in held_grad for a in group]
 
     def kernel(e_ref, *refs):
-        even_refs, refs = refs[:blocks], refs[blocks:]
-        odd_refs, refs = refs[:ranges], refs[ranges:]
-        keep_ref, even_out, odd_out, pos_ref = refs[0], refs[1], refs[2:-1], refs[-1]
-
-        def picked(ref, pos, prob):
-            hit = hits(pos, capacity)
-            chosen = hit.astype(jnp.float32).astype(jnp.bfloat16)
-            weight = jnp.sum(jnp.where(hit, prob, 0.0), axis=1, keepdims=True)
-            rows = product(chosen, ref[:tok_rows, :])
-            grads = product(chosen, ref[tok_rows : 2 * tok_rows, :])
-            return rows.astype(jnp.bfloat16), (weight * grads).astype(jnp.bfloat16)
-
-        for dx in range(blocks):
-            pos, prob = routes(even_refs[dx], tok_rows, e_ref[0])
-            rows = slice(dx * capacity, (dx + 1) * capacity)
-            for i, value in enumerate(picked(even_refs[dx], pos, prob)):
-                keep_ref[i, rows, :] = value
-                even_out[i, rows, :] = value
-            pos_ref[1, dx] = routes(even_refs[0], tok_rows, e_ref[dx])[0]
-        for dx in range(blocks):
-            pos, prob = routes(odd_refs[0], tok_rows, e_ref[dx])
-            pos_ref[0, dx] = pos
-            for dy in range(ranges):
-                start = (blocks + dy if dx == 0 else dy) * capacity
-                out_ref = keep_ref if dx == 0 else odd_out[dx - 1]
-                for i, value in enumerate(picked(odd_refs[dy], pos, prob)):
-                    out_ref[i, start : start + capacity, :] = value
-
-    shapes = [half(2, (blocks + ranges) * capacity, width), half(2, blocks * capacity, width)]
-    shapes += [half(2, ranges * capacity, width)] * (blocks - 1)
-    shapes += [jax.ShapeDtypeStruct((2, blocks, 1, tok_rows), jnp.int32)]
-    outs = whole_call(kernel, [*even, *odd], shapes, experts, after)
+        in_refs, refs = refs[: len(flat_in)], refs[len(flat_in) :]
+        grad_refs, refs = refs[: len(flat_grad)], refs[len(flat_grad) :]
+        keep_ref, in_out, grad_out, pos_ref = refs[0], refs[1], refs[2:-1], refs[-1]
+        for i, ref in enumerate(in_refs):
+            pos, _ = routes(ref, tok_rows, e_ref[0])
+            chosen = hits(pos, capacity).astype(jnp.float32).astype(jnp.bfloat16)
+            value = product(chosen, ref[:tok_rows, :]).astype(jnp.bfloat16)
+            keep_ref[i * capacity : (i + 1) * capacity, :] = value
+            in_out[i * capacity : (i + 1) * capacity, :] = value
+        for k in range(steps):
+            for dx in range(blocks):
+                pos, prob = routes(in_refs[k * blocks], tok_rows, e_ref[dx])
+                pos_ref[k, dx] = pos
+                hit = hits(pos, capacity)
+                chosen = hit.astype(jnp.float32).astype(jnp.bfloat16)
+                weight = jnp.sum(jnp.where(hit, prob, 0.0), axis=1, keepdims=True)
+                for dy in range(ranges):
+                    start = (dy * steps + k) * capacity + (rows if dx == 0 else 0)
+                    out_ref = keep_ref if dx == 0 else grad_out[dx - 1]
+                    value = weight * product(chosen, grad_refs[k * ranges + dy][...])
+                    out_ref[start : start + capacity, :] = value.astype(jnp.bfloat16)
+
+    grad_rows = ranges * steps * capacity
+    shapes = [half(rows + grad_rows, width), half(rows, width)]
+    shapes += [half(grad_rows, width)] * (blocks - 1)
+    shapes += [jax.ShapeDtypeStruct((steps, blocks, 1, tok_rows), jnp.int32)]
+    outs = whole_call(kernel, [*flat_in, *flat_grad], shapes, experts, after)
     return outs[:-1], outs[-1]
 
 
@@ -164,7 +161,7 @@
 def hidden_units(chunk, chunks, order, names, pieces, weights, sizes, carried, after):
     ff, full = weights[0].shape
     blocks, ranges, capacity = sizes
-    tile, width, k_rows = ff // TILES, pieces[0].shape[2], blocks * capacity
+    tile, width, k_rows = ff // TILES, pieces[0].shape[1], blocks * capacity
     rows, n_in = 2 * k_rows, len(pieces)
 
     def kernel(order_ref, *refs):
@@ -176,25 +173,22 @@
             at = order_ref[dc * ranges + dy] * width
             return pl.ds(pl.multiple_of(at, width), width)
 
-        def put(out_ref, i):
-            for (kind, d, dc), ref in zip(names, in_refs):
-                if kind == "even":
-                    out_ref[:k_rows, columns(dc, d)] = ref[i]
-                    continue
-                start = k_rows + d * capacity
-                first = k_rows if kind == "keep" else 0
-                if kind == "keep":
-                    out_ref[:k_rows, columns(dc, 0)] = ref[i, :k_rows, :]
-                for dy in range(ranges):
-                    at = first + dy * capacity
-                    out_ref[start : start + capacity, columns(dc, dy)] = ref[
-                        i, at : at + capacity, :
-                    ]
+        def put_grad(d, dc, ref, first):
+            for dy in range(ranges):
+                for k in range(2):
+                    start = k * k_rows + d * capacity
+                    at = first + (dy * 2 + k) * capacity
+                    g_ref[start : start + capacity, columns(dc, dy)] = ref[at : at + capacity, :]
 
         @pl.when(pl.program_id(0) == 0)
         def _():
-            put(x_ref, 0)
-            put(g_ref, 1)
+            for (kind, d, dc), ref in zip(names, in_refs):
+                if kind == "grad":
+                    put_grad(d, dc, ref, 0)
+                else:
+                    x_ref[:, columns(dc, d)] = ref[:rows, :]
+                    if kind == "keep":
+                        put_grad(0, dc, ref, rows)
 
         gate = right_product(x_ref[...], wg_ref[...])
         up = right_product(x_ref[...], wu_ref[...])
@@ -354,9 +348,9 @@
                 value += even_refs[dy][rows, :].astype(jnp.float32)
             out_refs[dx][...] = value.astype(jnp.bfloat16)
         for dy in range(ranges):
-            value = spread(pos_ref[0, 0], odd_refs[0][dy])
+            value = spread(pos_ref[1, 0], odd_refs[0][dy])
             for dx in range(1, blocks):
-                value += spread(pos_ref[0, dx], odd_refs[dx][dy])
+                value += spread(pos_ref[1, dx], odd_refs[dx][dy])
             out_refs[blocks + dy][...] = value.astype(jnp.bfloat16)
 
     shapes = [half(capacity, width)] * blocks + [half(tok_rows, width)] * ranges
@@ -371,9 +365,9 @@
     def kernel(pos_ref, *refs):
         even_refs, refs = refs[:blocks], refs[blocks:]
         odd_refs, out_refs = refs[:ranges], refs[ranges:]
-        value = spread(pos_ref[1, 0], even_refs[0][...])
+        value = spread(pos_ref[0, 0], even_refs[0][...])
         for dx in range(1, blocks):
-            value += spread(pos_ref[1, dx], even_refs[dx][...])
+            value += spread(pos_ref[0, dx], even_refs[dx][...])
         out_refs[0][...] = value.astype(jnp.bfloat16)
         value = odd_refs[0][...].astype(jnp.float32)
         for dy in range(1, ranges):
@@ -451,21 +445,26 @@
         return names, arrays
 
     sizes = (blocks, ranges, capacity)
-    packed = pack(tokens, grad_out, probs.T, expert_ids.T)
-    line = [along_z(packed, k) for k in range(DEPTH)]
+    packed = pack(tokens, probs.T, expert_ids.T)
+
+    def z_line(value):
+        near = along_z(value, 1)
+        return [value, near, along_z(near, 1), along_z(value, 3)]
+
+    in_line, grad_line = z_line(packed), z_line(grad_out)
 
     def first_hops(pair):
-        even = [along_x(line[pair[0]], dx) for dx in range(blocks)]
-        return even, [along_y(line[pair[1]], dy) for dy in range(ranges)]
-
-    def gathered(even, odd, after):
-        outs, pos = pick_pair(own_experts, even, odd, capacity, after)
+        held_in = [[along_x(in_line[k], dx) for dx in range(blocks)] for k in pair]
+        return held_in, [[along_y(grad_line[k], dy) for dy in range(ranges)] for k in pair]
+
+    def gathered(held_in, held_grad, after):
+        outs, pos = pick_pair(own_experts, held_in, held_grad, capacity, after)
         names, arrays = [("keep", 0)], [outs[0]]
         for dy in range(1, ranges):
-            names.append(("even", dy))
+            names.append(("in", dy))
             arrays.append(along_y(outs[1], dy))
         for dx in range(1, blocks):
-            names.append(("odd", dx))
+            names.append(("grad", dx))
             arrays.append(along_x(outs[1 + dx], dx))
         return pos, names, arrays
 
@@ -494,9 +493,10 @@
         return tuple(outs), [along_z(a, -k) for k, a in zip(pair, outs)]
 
     pos_a, names, arrays_a = gathered(*first_hops(PAIRS[0]), ())
-    even_b, odd_b = first_hops(PAIRS[1])
-    pos_b, names, arrays_b = gathered(even_b, odd_b, tuple(arrays_a))
-    arrays_a = [arrays_a[0], *ordered(tuple(arrays_a[1:]), (*even_b[1:], *odd_b[1:]))]
+    held_b = first_hops(PAIRS[1])
+    pos_b, names, arrays_b = gathered(*held_b, tuple(arrays_a))
+    before = tuple(a for held in held_b for group in held for a in group[1:])
+    arrays_a = [arrays_a[0], *ordered(tuple(arrays_a[1:]), before)]
     carried = units(0, names, arrays_a, [], (arrays_b[0],))
     arrays_b = [arrays_b[0], *ordered(tuple(arrays_b[1:]), (carried[2],))]
     parts_a = sums(0, carried, tuple(arrays_b[1:]))

time: 204 us -> 207 us (1.015)
  starting transfers between devices: 29.8 us -> 39.9 us
  waiting for transfers between devices: 36.9 us -> 28.7 us
    ppermute x30 -> x37, starting transfers between devices: 29.8 us -> 39.9 us  [shifted(): return lax.ppermute(value, axis, pairs)]
    ppermute x30 -> x37, waiting for transfers between devices: 36.9 us -> 28.7 us  [shifted(): return lax.ppermute(value, axis, pairs)]
    unnamed x60 -> x74, local copies, waits for them, and re-layouts: 6.25 us -> 6.76 us
  transfers between devices with their start and end apart: 30 -> 37, of which waited for: 6 -> 8; matrix products, arithmetic and copies ran while one was open for 18% -> 18% of each run, Pallas kernels for 42% -> 42%
where the time goes in v4:
time: 207 us
  Pallas kernels  90.9 us (44%)
  starting transfers between devices  39.9 us (19%)
  matrix products  32.8 us (16%)
  waiting for transfers between devices  28.7 us (14%)
  local copies, waits for them, and re-layouts  6.76 us (3%)
  other arithmetic  6.63 us (3%)
    pallas_call x2, Pallas kernels, hidden_units(): pl.pallas_call(kernel, grid_spec=pltpu.PrefetchScalarGridSpec(num_scalar_...  40.1 us
    ppermute x37, starting transfers between devices, shifted(): return lax.ppermute(value, axis, pairs)  39.9 us
    dot_general x3, matrix products, product(): return jnp.dot(left, right, preferred_element_type=jnp.float32)  32.8 us
    ppermute x37, waiting for transfers between devices, shifted(): return lax.ppermute(value, axis, pairs)  28.7 us
    pallas_call x7, Pallas kernels, whole_call(): pl.pallas_call(body, in_specs=[ANY] * skipped + [SMEM] * len(scalars) + [...  19.6 us
    pallas_call x2, Pallas kernels, partials_of_core(): pl.pallas_call(kernel, grid_spec=pltpu.PrefetchScalarGridSpec(num_scalar_...  17.4 us
    pallas_call x1, Pallas kernels, partials(): pl.pallas_call(kernel, grid_spec=pltpu.PrefetchScalarGridSpec(num_scalar_...  13.7 us
    unnamed x74, local copies, waits for them, and re-layouts  6.76 us
  transfers between devices with their start and end apart: 37, of which 8 were waited for; matrix products, arithmetic and copies ran while one was open for 18% of the time, Pallas kernels for 42%

profile of v4, /device:TPU:0, one launch (start us, length us, event | category | flops | bytes accessed | tf_op | source)
XLA Modules:
  0.0 206.6 jit_solution(12067541606272302474)
XLA Ops:
  2.3 3.0 %collective-permute-start.1 = (bf16[144,768]{1,0:T(8,128)(2,1)}, bf16[144,768]{1,0:T(8,128)(2,1)S(1)}, u32[]{:S(2)}, u32[]{:S(2)}) collective-permute-start(bf16[144,768]{1,0:T(8,128)(2,1)} %shard_map.102.refs_1_), channel_id=1, source_target_pairs={{0,8},{4,12},{8,16},{12,20},{16,24},{20,28},{24,0},{28,4},{1,9},{5... | collective-permute-start | bytes 663560 | tf_op jit(solution)/shard_map/ppermute | solution.py:55
  9.9 2.2 %collective-permute-start.14 = (bf16[128,768]{1,0:T(8,128)(2,1)}, bf16[128,768]{1,0:T(8,128)(2,1)S(1)}, u32[]{:S(2)}, u32[]{:S(2)}) collective-permute-start(bf16[128,768]{1,0:T(8,128)(2,1)} %refs_5_.1), channel_id=1, source_target_pairs={{0,24},{4,28},{8,0},{12,4},{16,8},{20,12},{24,16},{28,20},{1,25},{... | collective-permute-start | bytes 589832 | tf_op jit(solution)/shard_map/ppermute | solution.py:55
  12.1 1.8 collective-permute-done.1.refs_3_
  13.9 1.7 collective-permute-start.2
  15.7 2.4 %collective-permute-done.4.refs_7_ = bf16[128,768]{1,0:T(8,128)(2,1)S(1)} collective-permute-done((bf16[128,768]{1,0:T(8,128)(2,1)}, bf16[128,768]{1,0:T(8,128)(2,1)S(1)}, u32[]{:S(2)}, u32[]{:S(2)}) %collective-permute-start.4) | collective-permute-done | bytes 196640 | tf_op jit(solution)/shard_map/ppermute | solution.py:55
  18.0 7.5 %collective-permute-start.10 = (bf16[144,768]{1,0:T(8,128)(2,1)}, bf16[144,768]{1,0:T(8,128)(2,1)S(1)}, u32[]{:S(2)}, u32[]{:S(2)}) collective-permute-start(bf16[144,768]{1,0:T(8,128)(2,1)} %shard_map.102.refs_1_), channel_id=1, source_target_pairs={{0,24},{4,28},{8,0},{12,4},{16,8},{20,12},{24,16},{28,20},{1,25},{... | collective-permute-start | bytes 663560 | tf_op jit(solution)/shard_map/ppermute | solution.py:55
  28.2 3.0 %collective-permute-done.5.refs_8_ = bf16[128,768]{1,0:T(8,128)(2,1)S(1)} collective-permute-done((bf16[128,768]{1,0:T(8,128)(2,1)S(1)}, bf16[128,768]{1,0:T(8,128)(2,1)S(1)}, u32[]{:S(2)}, u32[]{:S(2)}) %collective-permute-start.5) | collective-permute-done | bytes 196640 | tf_op jit(solution)/shard_map/ppermute | solution.py:55
  32.6 4.1 %shard_map.103 = (bf16[768,768]{1,0:T(8,128)(2,1)}, bf16[384,768]{1,0:T(8,128)(2,1)}, bf16[384,768]{1,0:T(8,128)(2,1)}, s32[2,2,1,128]{3,2,1,0:T(1,128)}) custom-call(s32[2]{0:T(128)} %pad_add_fusion.1.refs_0_.refs_3_, bf16[144,768]{1,0:T(8,128)(2,1)} %shard_map.102.refs_1_, bf16[144,768]{1,0:T(8,128)(2,1)} %copy-done.18, bf16[144,768]{1,0:T(8,128)(2,1)} %copy-done.17, ...), custom_call_target="tpu_custom_call" | custom-call | bytes 1 | tf_op jit(solution)/shard_map/pallas_call | solution.py:65
  36.7 1.7 collective-permute-start.6
  40.6 9.1 %collective-permute-done.8.refs_4_ = bf16[144,768]{1,0:T(8,128)(2,1)S(1)} collective-permute-done((bf16[144,768]{1,0:T(8,128)(2,1)}, bf16[144,768]{1,0:T(8,128)(2,1)S(1)}, u32[]{:S(2)}, u32[]{:S(2)}) %collective-permute-start.8) | collective-permute-done | bytes 221216 | tf_op jit(solution)/shard_map/ppermute | solution.py:55
  50.3 4.1 %collective-permute-done.11.refs_7_ = bf16[144,768]{1,0:T(8,128)(2,1)S(1)} collective-permute-done((bf16[144,768]{1,0:T(8,128)(2,1)S(1)}, bf16[144,768]{1,0:T(8,128)(2,1)S(1)}, u32[]{:S(2)}, u32[]{:S(2)}) %collective-permute-start.11) | collective-permute-done | bytes 221216 | tf_op jit(solution)/shard_map/ppermute | solution.py:55
  54.7 5.3 %collective-permute-done.13.refs_9_ = bf16[128,768]{1,0:T(8,128)(2,1)S(1)} collective-permute-done((bf16[128,768]{1,0:T(8,128)(2,1)S(1)}, bf16[128,768]{1,0:T(8,128)(2,1)S(1)}, u32[]{:S(2)}, u32[]{:S(2)}) %collective-permute-start.13) | collective-permute-done | bytes 196640 | tf_op jit(solution)/shard_map/ppermute | solution.py:55
  61.4 4.2 %shard_map.104 = (bf16[768,768]{1,0:T(8,128)(2,1)}, bf16[384,768]{1,0:T(8,128)(2,1)}, bf16[384,768]{1,0:T(8,128)(2,1)}, s32[2,2,1,128]{3,2,1,0:T(1,128)}) custom-call(bf16[768,768]{1,0:T(8,128)(2,1)} %get-tuple-element.49.refs_0_, bf16[384,768]{1,0:T(8,128)(2,1)} %copy-done.8, bf16[384,768]{1,0:T(8,128)(2,1)} %copy-done.9, s32[2]{0:T(128)} %pad_add_fusion.1.refs_0_.refs_3_, ...), custom_call_target="tpu_custom_call" | custom-call | bytes 1 | tf_op jit(solution)/shard_map/pallas_call | solution.py:65
  65.9 2.4 %collective-permute-start.18 = (bf16[384,768]{1,0:T(8,128)(2,1)}, bf16[384,768]{1,0:T(8,128)(2,1)S(1)}, u32[]{:S(2)}, u32[]{:S(2)}) collective-permute-start(bf16[384,768]{1,0:T(8,128)(2,1)} %get-tuple-element.54), channel_id=1, source_target_pairs={{0,4},{4,0},{8,12},{12,8},{16,20},{20,16},{24,28},{28,24},{1,5},{5... | collective-permute-start | bytes 1769480 | tf_op jit(solution)/shard_map/ppermute | solution.py:55
  69.1 20.5 %shard_map.105 = (bf16[768,3072]{1,0:T(8,128)(2,1)}, bf16[768,3072]{1,0:T(8,128)(2,1)}, bf16[1344,768]{1,0:T(8,128)(2,1)}, bf16[1344,768]{1,0:T(8,128)(2,1)}, bf16[1344,768]{1,0:T(8,128)(2,1)}) custom-call(s32[4]{0:T(128)} %pad_add_fusion.order_ref, bf16[768,768]{1,0:T(8,128)(2,1)} %get-tuple-element.49.refs_0_, ...), custom_call_target="tpu_custom_call" | custom-call | flops 9512681472 | bytes 37306368 | tf_op jit(solution)/shard_map/pallas_call | solution.py:210
  90.6 13.7 %shard_map.106 = (bf16[2,384,768]{2,1,0:T(8,128)(2,1)}, bf16[2,384,768]{2,1,0:T(8,128)(2,1)}) custom-call(s32[4]{0:T(128)} %pad_add_fusion.order_ref, bf16[1344,768]{1,0:T(8,128)(2,1)} %get-tuple-element.62.gpg_ref.refs_12_, bf16[1344,768]{1,0:T(8,128)(2,1)} %get-tuple-element.63.gpu_ref.refs_13_, bf16[1344,3072]{1,0:T(8,128)(2,1)} %bitcast.36, ...), custom_call_target="tpu_custom_call" | custom-call | flops 6341787648 | bytes 20938752 | tf_op jit(solution)/shard_map/pallas_call | solution.py:255
  105.8 19.7 %shard_map.107 = (bf16[768,3072]{1,0:T(8,128)(2,1)}, bf16[768,3072]{1,0:T(8,128)(2,1)}, bf16[1344,768]{1,0:T(8,128)(2,1)}, bf16[1344,768]{1,0:T(8,128)(2,1)}, bf16[1344,768]{1,0:T(8,128)(2,1)}) custom-call(s32[4]{0:T(128)} %pad_add_fusion.order_ref, ...), custom_call_target="tpu_custom_call", output_to_operand_aliasing={{0}: (10, {}), {1}: (11, {}), {2}: (12, {}), {3}: (13, {}),... | custom-call | flops 9512681472 | bytes 37306368 | tf_op jit(solution)/shard_map/pallas_call | solution.py:210
  127.2 1.7 collective-permute-start.25
  128.9 9.0 %shard_map.108 = (bf16[2,384,768]{2,1,0:T(8,128)(2,1)}, bf16[384,1344]{1,0:T(8,128)(2,1)}, bf16[384,1344]{1,0:T(8,128)(2,1)}) custom-call(s32[4]{0:T(128)} %pad_add_fusion.order_ref, bf16[1344,768]{1,0:T(8,128)(2,1)} %get-tuple-element.89.lg_ref, bf16[1344,768]{1,0:T(8,128)(2,1)} %get-tuple-element.93.lu_ref, bf16[1344,3072]{1,0:T(8,128)(2,1)} %bitcast.38, ...), custom_call_target="tpu_custom_call" | custom-call | flops 3170893824 | bytes 11501568 | tf_op jit(solution)/shard_map/pallas_call | solution.py:295
  138.7 2.6 %shard_map.109 = (bf16[96,768]{1,0:T(8,128)(2,1)}, bf16[96,768]{1,0:T(8,128)(2,1)}, bf16[128,768]{1,0:T(8,128)(2,1)}, bf16[128,768]{1,0:T(8,128)(2,1)}) custom-call(bf16[2,384,768]{2,1,0:T(8,128)(2,1)} %get-tuple-element.79.refs_0_, s32[2,2,1,128]{3,2,1,0:T(1,128)} %get-tuple-element.74.refs_1_.refs_4_, bf16[192,768]{1,0:T(8,128)(2,1)} %get-tuple-element.101.refs_0_.refs_2_, ...), custom_call_target="tpu_custom_call" | custom-call | bytes 1 | tf_op jit(solution)/shard_map/pallas_call | solution.py:65
  141.5 1.9 collective-permute-start.28
  143.6 8.5 %shard_map.110 = bf16[2,384,768]{2,1,0:T(8,128)(2,1)} custom-call(s32[4]{0:T(128)} %pad_add_fusion.order_ref, bf16[384,1344]{1,0:T(8,128)(2,1)} %get-tuple-element.71.lg_ref, bf16[384,1344]{1,0:T(8,128)(2,1)} %get-tuple-element.72.lu_ref, bf16[1344,3072]{1,0:T(8,128)(2,1)} %bitcast.39, bf16[1344,3072]{1,0:T(8,128)(2,1)} %bitcast.44, ...), custom_call_target="tpu_custom_call" | custom-call | flops 3170893824 | bytes 11501568 | tf_op jit(solution)/shard_map/pallas_call | solution.py:295
  152.1 2.0 fusion.4
  154.1 1.7 collective-permute-start.31
  157.0 2.2 %shard_map.111 = (bf16[128,768]{1,0:T(8,128)(2,1)}, bf16[128,768]{1,0:T(8,128)(2,1)}) custom-call(bf16[192,768]{1,0:T(8,128)(2,1)} %get-tuple-element.97.refs_0_.refs_2_, bf16[192,768]{1,0:T(8,128)(2,1)} %copy-done.5, bf16[2,96,768]{2,1,0:T(8,128)(2,1)} %get-tuple-element.95.refs_2_.refs_4_, bf16[2,96,768]{2,1,0:T(8,128)(2,1)} %get-tuple-element.94.refs_3_, ...), custom_call_target="tpu_custom_call" | custom-call | bytes 1 | tf_op jit(solution)/shard_map/pallas_call | solution.py:65
  160.3 10.6 %convolution_convert_fusion.2.refs_0_ = bf16[1344,3072]{1,0:T(8,128)(2,1)} fusion(bf16[1344,768]{1,0:T(8,128)(2,1)} %get-tuple-element.82, bf16[768,3072]{1,0:T(8,128)(2,1)S(1)} %bitcast.50), kind=kOutput, calls=%fused_computation.2 | convolution fusion | flops 6345916416 | bytes 15040512 | tf_op jit(solution)/shard_map/dot_general | solution.py:20
  171.6 2.6 %shard_map.112 = (bf16[96,768]{1,0:T(8,128)(2,1)}, bf16[96,768]{1,0:T(8,128)(2,1)}, bf16[128,768]{1,0:T(8,128)(2,1)}, bf16[128,768]{1,0:T(8,128)(2,1)}) custom-call(bf16[1344,3072]{1,0:T(8,128)(2,1)} %convolution_convert_fusion.2.refs_0_, s32[2,2,1,128]{3,2,1,0:T(1,128)} %get-tuple-element.84.refs_1_, bf16[192,768]{1,0:T(8,128)(2,1)} %get-tuple-element.97.refs_0_.refs_2_, ...), custom_call_target="tpu_custom_call" | custom-call | bytes 1 | tf_op jit(solution)/shard_map/pallas_call | solution.py:65
  174.2 1.7 collective-permute-start.33
  176.4 11.1 %convolution_convert_fusion.1.refs_0_ = bf16[1344,3072]{1,0:T(8,128)(2,1)} fusion(bf16[1344,768]{1,0:T(8,128)(2,1)S(1)} %copy-done, bf16[768,3072]{1,0:T(8,128)(2,1)} %get-tuple-element.90), kind=kOutput, calls=%fused_computation.1 | convolution fusion | flops 6345916416 | bytes 15040512 | tf_op jit(solution)/shard_map/dot_general | solution.py:20
  188.8 2.2 %shard_map.113 = (bf16[128,768]{1,0:T(8,128)(2,1)}, bf16[128,768]{1,0:T(8,128)(2,1)}) custom-call(bf16[1344,3072]{1,0:T(8,128)(2,1)} %convolution_convert_fusion.1.refs_0_, s32[2,2,1,128]{3,2,1,0:T(1,128)} %get-tuple-element.84.refs_1_, bf16[96,768]{1,0:T(8,128)(2,1)} %get-tuple-element.85.refs_2_, bf16[96,768]{1,0:T(8,128)(2,1)} %copy-done.33, ...), custom_call_target="tpu_custom_call" | custom-call | bytes 1 | tf_op jit(solution)/shard_map/pallas_call | solution.py:65
  192.0 11.1 %fusion = bf16[1,3072,1344]{1,2,0:T(8,128)(2,1)} fusion(bf16[1344,768]{1,0:T(8,128)(2,1)S(1)} %copy-done.1, bf16[768,3072]{1,0:T(8,128)(2,1)} %get-tuple-element.90), kind=kOutput, calls=%fused_computation.3 | convolution fusion | flops 6345916416 | bytes 15040512 | tf_op jit(solution)/shard_map/dot_general | solution.py:20
  203.1 2.7 %collective-permute-done.35 = bf16[128,768]{1,0:T(8,128)(2,1)S(1)} collective-permute-done((bf16[128,768]{1,0:T(8,128)(2,1)}, bf16[128,768]{1,0:T(8,128)(2,1)S(1)}, u32[]{:S(2)}, u32[]{:S(2)}) %collective-permute-start.35) | collective-permute-done | bytes 196640 | tf_op jit(solution)/shard_map/ppermute | solution.py:55
  (139 shorter events, 27.6 us)
Async XLA Ops:
  2.3 11.7 %collective-permute-start.1 = (bf16[144,768]{1,0:T(8,128)(2,1)}, bf16[144,768]{1,0:T(8,128)(2,1)S(1)}, u32[]{:S(2)}, u32[]{:S(2)}) collective-permute-start(bf16[144,768]{1,0:T(8,128)(2,1)} %shard_map.102.refs_1_), channel_id=1, source_target_pairs={{0,8},{4,12},{8,16},{12,20},{16,24},{20,28},{24,0},{28,4},{1,9},{5... | collective-permute-start | bytes 663560 | tf_op jit(solution)/shard_map/ppermute | solution.py:55
  5.3 12.7 %collective-permute-start.4 = (bf16[128,768]{1,0:T(8,128)(2,1)}, bf16[128,768]{1,0:T(8,128)(2,1)S(1)}, u32[]{:S(2)}, u32[]{:S(2)}) collective-permute-start(bf16[128,768]{1,0:T(8,128)(2,1)} %refs_5_.1), channel_id=1, source_target_pairs={{0,8},{4,12},{8,16},{12,20},{16,24},{20,28},{24,0},{28,4},{1,9},{5... | collective-permute-start | bytes 589832 | tf_op jit(solution)/shard_map/ppermute | solution.py:55
  6.9 18.6 %collective-permute-start.3 = (bf16[128,768]{1,0:T(8,128)(2,1)}, bf16[128,768]{1,0:T(8,128)(2,1)S(1)}, u32[]{:S(2)}, u32[]{:S(2)}) collective-permute-start(bf16[128,768]{1,0:T(8,128)(2,1)} %refs_5_.1), channel_id=1, source_target_pairs={{0,2},{1,3},{2,0},{3,1},{4,6},{5,7},{6,4},{7,5},{8,10},{9,11},{10,... | collective-permute-start | bytes 589832 | tf_op jit(solution)/shard_map/ppermute | solution.py:55
  8.4 18.7 %collective-permute-start = (bf16[144,768]{1,0:T(8,128)(2,1)}, bf16[144,768]{1,0:T(8,128)(2,1)S(1)}, u32[]{:S(2)}, u32[]{:S(2)}) collective-permute-start(bf16[144,768]{1,0:T(8,128)(2,1)} %shard_map.102.refs_1_), channel_id=1, source_target_pairs={{0,4},{4,0},{8,12},{12,8},{16,20},{20,16},{24,28},{28,24},{1,5},{5... | collective-permute-start | bytes 663560 | tf_op jit(solution)/shard_map/ppermute | solution.py:55
  9.9 17.1 %collective-permute-start.14 = (bf16[128,768]{1,0:T(8,128)(2,1)}, bf16[128,768]{1,0:T(8,128)(2,1)S(1)}, u32[]{:S(2)}, u32[]{:S(2)}) collective-permute-start(bf16[128,768]{1,0:T(8,128)(2,1)} %refs_5_.1), channel_id=1, source_target_pairs={{0,24},{4,28},{8,0},{12,4},{16,8},{20,12},{24,16},{28,20},{1,25},{... | collective-permute-start | bytes 589832 | tf_op jit(solution)/shard_map/ppermute | solution.py:55
  13.9 17.2 %collective-permute-start.2 = (bf16[144,768]{1,0:T(8,128)(2,1)S(1)}, bf16[144,768]{1,0:T(8,128)(2,1)S(1)}, u32[]{:S(2)}, u32[]{:S(2)}) collective-permute-start(bf16[144,768]{1,0:T(8,128)(2,1)S(1)} %collective-permute-done.1.refs_3_), channel_id=1, source_target_pairs={{0,4},{4,0},{8,12},{12,8},{16,20},{20,16},{24,28},{28,24},{1,5},{5... | collective-permute-start | bytes 663560 | tf_op jit(solution)/shard_map/ppermute | solution.py:55
  18.0 21.8 %collective-permute-start.10 = (bf16[144,768]{1,0:T(8,128)(2,1)}, bf16[144,768]{1,0:T(8,128)(2,1)S(1)}, u32[]{:S(2)}, u32[]{:S(2)}) collective-permute-start(bf16[144,768]{1,0:T(8,128)(2,1)} %shard_map.102.refs_1_), channel_id=1, source_target_pairs={{0,24},{4,28},{8,0},{12,4},{16,8},{20,12},{24,16},{28,20},{1,25},{... | collective-permute-start | bytes 663560 | tf_op jit(solution)/shard_map/ppermute | solution.py:55
  27.0 12.8 %collective-permute-start.12 = (bf16[128,768]{1,0:T(8,128)(2,1)S(1)}, bf16[128,768]{1,0:T(8,128)(2,1)S(1)}, u32[]{:S(2)}, u32[]{:S(2)}) collective-permute-start(bf16[128,768]{1,0:T(8,128)(2,1)S(1)} %collective-permute-done.4.refs_7_), channel_id=1, source_target_pairs={{0,8},{4,12},{8,16},{12,20},{16,24},{20,28},{24,0},{28,4},{1,9},{5... | collective-permute-start | bytes 589832 | tf_op jit(solution)/shard_map/ppermute | solution.py:55
  27.1 12.9 %collective-permute-start.15 = (bf16[128,768]{1,0:T(8,128)(2,1)S(1)}, bf16[128,768]{1,0:T(8,128)(2,1)S(1)}, u32[]{:S(2)}, u32[]{:S(2)}) collective-permute-start(bf16[128,768]{1,0:T(8,128)(2,1)S(1)} %collective-permute-done.14.refs_10_), channel_id=1, source_target_pairs={{0,2},{1,3},{2,0},{3,1},{4,6},{5,7},{6,4},{7,5},{8,10},{9,11},{10,... | collective-permute-start | bytes 589832 | tf_op jit(solution)/shard_map/ppermute | solution.py:55
  36.7 23.4 %collective-permute-start.6 = (bf16[384,768]{1,0:T(8,128)(2,1)}, bf16[384,768]{1,0:T(8,128)(2,1)S(1)}, u32[]{:S(2)}, u32[]{:S(2)}) collective-permute-start(bf16[384,768]{1,0:T(8,128)(2,1)} %get-tuple-element.50), channel_id=1, source_target_pairs={{0,2},{1,3},{2,0},{3,1},{4,6},{5,7},{6,4},{7,5},{8,10},{9,11},{10,... | collective-permute-start | bytes 1769480 | tf_op jit(solution)/shard_map/ppermute | solution.py:55
  38.4 21.7 %collective-permute-start.7 = (bf16[384,768]{1,0:T(8,128)(2,1)}, bf16[384,768]{1,0:T(8,128)(2,1)S(1)}, u32[]{:S(2)}, u32[]{:S(2)}) collective-permute-start(bf16[384,768]{1,0:T(8,128)(2,1)} %get-tuple-element.51), channel_id=1, source_target_pairs={{0,4},{4,0},{8,12},{12,8},{16,20},{20,16},{24,28},{28,24},{1,5},{5... | collective-permute-start | bytes 1769480 | tf_op jit(solution)/shard_map/ppermute | solution.py:55
  39.9 28.4 %collective-permute-start.19 = (bf16[768,768]{1,0:T(8,128)(2,1)}, bf16[768,768]{1,0:T(8,128)(2,1)}, u32[]{:S(2)}, u32[]{:S(2)}) collective-permute-start(bf16[768,768]{1,0:T(8,128)(2,1)} %get-tuple-element.49.refs_0_), channel_id=1, source_target_pairs={{0,1},{1,0},{2,3},{3,2},{4,5},{5,4},{6,7},{7,6},{8,9},{9,8},{10,11... | collective-permute-start | bytes 3538952 | tf_op jit(solution)/shard_map/ppermute | solution.py:55
  39.9 9.8 %collective-permute-start.8 = (bf16[144,768]{1,0:T(8,128)(2,1)}, bf16[144,768]{1,0:T(8,128)(2,1)S(1)}, u32[]{:S(2)}, u32[]{:S(2)}) collective-permute-start(bf16[144,768]{1,0:T(8,128)(2,1)} %copy-done.17), channel_id=1, source_target_pairs={{0,8},{4,12},{8,16},{12,20},{16,24},{20,28},{24,0},{28,4},{1,9},{5... | collective-permute-start | bytes 663560 | tf_op jit(solution)/shard_map/ppermute | solution.py:55
  40.0 14.4 %collective-permute-start.11 = (bf16[144,768]{1,0:T(8,128)(2,1)S(1)}, bf16[144,768]{1,0:T(8,128)(2,1)S(1)}, u32[]{:S(2)}, u32[]{:S(2)}) collective-permute-start(bf16[144,768]{1,0:T(8,128)(2,1)S(1)} %collective-permute-done.10.refs_6_), channel_id=1, source_target_pairs={{0,4},{4,0},{8,12},{12,8},{16,20},{20,16},{24,28},{28,24},{1,5},{5... | collective-permute-start | bytes 663560 | tf_op jit(solution)/shard_map/ppermute | solution.py:55
  49.7 10.3 %collective-permute-start.9 = (bf16[144,768]{1,0:T(8,128)(2,1)S(1)}, bf16[144,768]{1,0:T(8,128)(2,1)S(1)}, u32[]{:S(2)}, u32[]{:S(2)}) collective-permute-start(bf16[144,768]{1,0:T(8,128)(2,1)S(1)} %collective-permute-done.8.refs_4_), channel_id=1, source_target_pairs={{0,4},{4,0},{8,12},{12,8},{16,20},{20,16},{24,28},{28,24},{1,5},{5... | collective-permute-start | bytes 663560 | tf_op jit(solution)/shard_map/ppermute | solution.py:55
  65.5 24.1 %collective-permute-start.17 = (bf16[384,768]{1,0:T(8,128)(2,1)}, bf16[384,768]{1,0:T(8,128)(2,1)S(1)}, u32[]{:S(2)}, u32[]{:S(2)}) collective-permute-start(bf16[384,768]{1,0:T(8,128)(2,1)} %get-tuple-element.53), channel_id=1, source_target_pairs={{0,2},{1,3},{2,0},{3,1},{4,6},{5,7},{6,4},{7,5},{8,10},{9,11},{10,... | collective-permute-start | bytes 1769480 | tf_op jit(solution)/shard_map/ppermute | solution.py:55
  65.9 23.7 %collective-permute-start.18 = (bf16[384,768]{1,0:T(8,128)(2,1)}, bf16[384,768]{1,0:T(8,128)(2,1)S(1)}, u32[]{:S(2)}, u32[]{:S(2)}) collective-permute-start(bf16[384,768]{1,0:T(8,128)(2,1)} %get-tuple-element.54), channel_id=1, source_target_pairs={{0,4},{4,0},{8,12},{12,8},{16,20},{20,16},{24,28},{28,24},{1,5},{5... | collective-permute-start | bytes 1769480 | tf_op jit(solution)/shard_map/ppermute | solution.py:55
  68.3 36.1 %collective-permute-start.16 = (bf16[768,768]{1,0:T(8,128)(2,1)}, bf16[768,768]{1,0:T(8,128)(2,1)S(1)}, u32[]{:S(2)}, u32[]{:S(2)}) collective-permute-start(bf16[768,768]{1,0:T(8,128)(2,1)} %get-tuple-element.52.refs_9_.refs_0_), channel_id=1, source_target_pairs={{0,1},{1,0},{2,3},{3,2},{4,5},{5,4},{6,7},{7,6},{8,9},{9,8},{10,11... | collective-permute-start | bytes 3538952 | tf_op jit(solution)/shard_map/ppermute | solution.py:55
  89.6 14.8 %collective-permute-start.22 = (bf16[384,768]{1,0:T(8,128)(2,1)S(1)}, bf16[384,768]{1,0:T(8,128)(2,1)S(1)}, u32[]{:S(2)}, u32[]{:S(2)}) collective-permute-start(bf16[384,768]{1,0:T(8,128)(2,1)S(1)} %collective-permute-done.17.refs_0_.refs_2_), channel_id=1, source_target_pairs={{0,1},{1,0},{2,3},{3,2},{4,5},{5,4},{6,7},{7,6},{8,9},{9,8},{10,11... | collective-permute-start | bytes 1769480 | tf_op jit(solution)/shard_map/ppermute | solution.py:55
  89.7 14.7 %collective-permute-start.23 = (bf16[384,768]{1,0:T(8,128)(2,1)S(1)}, bf16[384,768]{1,0:T(8,128)(2,1)S(1)}, u32[]{:S(2)}, u32[]{:S(2)}) collective-permute-start(bf16[384,768]{1,0:T(8,128)(2,1)S(1)} %collective-permute-done.18.refs_1_.refs_4_), channel_id=1, source_target_pairs={{0,1},{1,0},{2,3},{3,2},{4,5},{5,4},{6,7},{7,6},{8,9},{9,8},{10,11... | collective-permute-start | bytes 1769480 | tf_op jit(solution)/shard_map/ppermute | solution.py:55
  104.4 21.1 %collective-permute-start.24 = (bf16[2,384,768]{2,1,0:T(8,128)(2,1)}, bf16[2,384,768]{2,1,0:T(8,128)(2,1)S(1)}, u32[]{:S(2)}, u32[]{:S(2)}) collective-permute-start(bf16[2,384,768]{2,1,0:T(8,128)(2,1)} %get-tuple-element.67), channel_id=1, source_target_pairs={{0,1},{1,0},{2,3},{3,2},{4,5},{5,4},{6,7},{7,6},{8,9},{9,8},{10,11... | collective-permute-start | bytes 3538952 | tf_op jit(solution)/shard_map/ppermute | solution.py:55
  127.2 10.6 %collective-permute-start.25 = (bf16[192,768]{1,0:T(8,128)(2,1)S(1)}, bf16[192,768]{1,0:T(8,128)(2,1)S(1)}, u32[]{:S(2)}, u32[]{:S(2)}) collective-permute-start(bf16[192,768]{1,0:T(8,128)(2,1)S(1)} %get-tuple-element.100.refs_1_), channel_id=1, source_target_pairs={{0,2},{1,3},{2,0},{3,1},{4,6},{5,7},{6,4},{7,5},{8,10},{9,11},{10,... | collective-permute-start | bytes 884744 | tf_op jit(solution)/shard_map/ppermute | solution.py:55
  141.3 10.8 %collective-permute-start.27 = (bf16[2,384,768]{2,1,0:T(8,128)(2,1)}, bf16[2,384,768]{2,1,0:T(8,128)(2,1)S(1)}, u32[]{:S(2)}, u32[]{:S(2)}) collective-permute-start(bf16[2,384,768]{2,1,0:T(8,128)(2,1)} %get-tuple-element.79.refs_0_), channel_id=1, source_target_pairs={{0,1},{1,0},{2,3},{3,2},{4,5},{5,4},{6,7},{7,6},{8,9},{9,8},{10,11... | collective-permute-start | bytes 3538952 | tf_op jit(solution)/shard_map/ppermute | solution.py:55
  141.5 15.5 %collective-permute-start.28 = (bf16[96,768]{1,0:T(8,128)(2,1)}, bf16[96,768]{1,0:T(8,128)(2,1)}, u32[]{:S(2)}, u32[]{:S(2)}) collective-permute-start(bf16[96,768]{1,0:T(8,128)(2,1)} %get-tuple-element.76.refs_1_), channel_id=1, source_target_pairs={{0,4},{4,0},{8,12},{12,8},{16,20},{20,16},{24,28},{28,24},{1,5},{5... | collective-permute-start | bytes 442376 | tf_op jit(solution)/shard_map/ppermute | solution.py:55
  143.3 13.6 %collective-permute-start.29 = (bf16[128,768]{1,0:T(8,128)(2,1)}, bf16[128,768]{1,0:T(8,128)(2,1)}, u32[]{:S(2)}, u32[]{:S(2)}) collective-permute-start(bf16[128,768]{1,0:T(8,128)(2,1)} %get-tuple-element.78.refs_3_), channel_id=1, source_target_pairs={{0,2},{1,3},{2,0},{3,1},{4,6},{5,7},{6,4},{7,5},{8,10},{9,11},{10,... | collective-permute-start | bytes 589832 | tf_op jit(solution)/shard_map/ppermute | solution.py:55
  154.1 16.8 %collective-permute-start.31 = (bf16[192,768]{1,0:T(8,128)(2,1)S(1)}, bf16[192,768]{1,0:T(8,128)(2,1)}, u32[]{:S(2)}, u32[]{:S(2)}) collective-permute-start(bf16[192,768]{1,0:T(8,128)(2,1)S(1)} %get-tuple-element.96.refs_1_), channel_id=1, source_target_pairs={{0,2},{1,3},{2,0},{3,1},{4,6},{5,7},{6,4},{7,5},{8,10},{9,11},{10,... | collective-permute-start | bytes 884744 | tf_op jit(solution)/shard_map/ppermute | solution.py:55
  156.8 14.1 %collective-permute-start.32 = (bf16[2,96,768]{2,1,0:T(8,128)(2,1)}, bf16[2,96,768]{2,1,0:T(8,128)(2,1)S(1)}, u32[]{:S(2)}, u32[]{:S(2)}) collective-permute-start(bf16[2,96,768]{2,1,0:T(8,128)(2,1)} %get-tuple-element.94.refs_3_), channel_id=1, source_target_pairs={{0,4},{4,0},{8,12},{12,8},{16,20},{20,16},{24,28},{28,24},{1,5},{5... | collective-permute-start | bytes 884744 | tf_op jit(solution)/shard_map/ppermute | solution.py:55
  159.2 43.9 %collective-permute-start.30 = (bf16[128,768]{1,0:T(8,128)(2,1)}, bf16[128,768]{1,0:T(8,128)(2,1)S(1)}, u32[]{:S(2)}, u32[]{:S(2)}) collective-permute-start(bf16[128,768]{1,0:T(8,128)(2,1)} %get-tuple-element.81), channel_id=1, source_target_pairs={{0,24},{4,28},{8,0},{12,4},{16,8},{20,12},{24,16},{28,20},{1,25},{... | collective-permute-start | bytes 589832 | tf_op jit(solution)/shard_map/ppermute | solution.py:55
  174.2 13.2 %collective-permute-start.33 = (bf16[96,768]{1,0:T(8,128)(2,1)}, bf16[96,768]{1,0:T(8,128)(2,1)S(1)}, u32[]{:S(2)}, u32[]{:S(2)}) collective-permute-start(bf16[96,768]{1,0:T(8,128)(2,1)} %get-tuple-element.86), channel_id=1, source_target_pairs={{0,4},{4,0},{8,12},{12,8},{16,20},{20,16},{24,28},{28,24},{1,5},{5... | collective-permute-start | bytes 442376 | tf_op jit(solution)/shard_map/ppermute | solution.py:55
  175.9 11.6 %collective-permute-start.34 = (bf16[128,768]{1,0:T(8,128)(2,1)}, bf16[128,768]{1,0:T(8,128)(2,1)S(1)}, u32[]{:S(2)}, u32[]{:S(2)}) collective-permute-start(bf16[128,768]{1,0:T(8,128)(2,1)} %get-tuple-element.88), channel_id=1, source_target_pairs={{0,2},{1,3},{2,0},{3,1},{4,6},{5,7},{6,4},{7,5},{8,10},{9,11},{10,... | collective-permute-start | bytes 589832 | tf_op jit(solution)/shard_map/ppermute | solution.py:55
  191.0 14.8 %collective-permute-start.35 = (bf16[128,768]{1,0:T(8,128)(2,1)}, bf16[128,768]{1,0:T(8,128)(2,1)S(1)}, u32[]{:S(2)}, u32[]{:S(2)}) collective-permute-start(bf16[128,768]{1,0:T(8,128)(2,1)} %get-tuple-element.91), channel_id=1, source_target_pairs={{0,16},{4,20},{8,24},{12,28},{16,0},{20,4},{24,8},{28,12},{1,17},{... | collective-permute-start | bytes 589832 | tf_op jit(solution)/shard_map/ppermute | solution.py:55
  191.0 14.8 %collective-permute-start.36 = (bf16[128,768]{1,0:T(8,128)(2,1)}, bf16[128,768]{1,0:T(8,128)(2,1)S(1)}, u32[]{:S(2)}, u32[]{:S(2)}) collective-permute-start(bf16[128,768]{1,0:T(8,128)(2,1)} %get-tuple-element.92), channel_id=1, source_target_pairs={{0,8},{4,12},{8,16},{12,20},{16,24},{20,28},{24,0},{28,4},{1,9},{5... | collective-permute-start | bytes 589832 | tf_op jit(solution)/shard_map/ppermute | solution.py:55
  (42 other events, 302.9 us)

commit v5 on v3

--- a/solution.py
+++ b/solution.py
@@ -339,48 +339,62 @@
     return left_product(chosen, rows)
 
 
-def second_returns(pos, even, odd, after):
-    ranges, blocks = len(even), len(odd)
-    tok_rows, width = pos.shape[3], even[0].shape[1]
-    capacity = even[0].shape[0] // blocks
-
-    def kernel(pos_ref, *refs):
-        even_refs, refs = refs[:ranges], refs[ranges:]
-        odd_refs, out_refs = refs[:blocks], refs[blocks:]
-        for dx in range(blocks):
-            rows = slice(dx * capacity, (dx + 1) * capacity)
-            value = even_refs[0][rows, :].astype(jnp.float32)
-            for dy in range(1, ranges):
-                value += even_refs[dy][rows, :].astype(jnp.float32)
-            out_refs[dx][...] = value.astype(jnp.bfloat16)
-        for dy in range(ranges):
-            value = spread(pos_ref[0, 0], odd_refs[0][dy])
-            for dx in range(1, blocks):
-                value += spread(pos_ref[0, dx], odd_refs[dx][dy])
-            out_refs[blocks + dy][...] = value.astype(jnp.bfloat16)
-
-    shapes = [half(capacity, width)] * blocks + [half(tok_rows, width)] * ranges
-    outs = whole_call(kernel, [pos, *even, *odd], shapes, after=after)
-    return outs[:blocks], outs[blocks:]
-
-
-def third_returns(pos, even, odd, after):
-    blocks, ranges = len(even), len(odd)
-    tok_rows, width = pos.shape[3], even[0].shape[1]
-
-    def kernel(pos_ref, *refs):
-        even_refs, refs = refs[:blocks], refs[blocks:]
-        odd_refs, out_refs = refs[:ranges], refs[ranges:]
-        value = spread(pos_ref[1, 0], even_refs[0][...])
+def second_sums(pos_ref, even_refs, odd_refs, out_refs):
+    ranges, blocks = len(even_refs), len(odd_refs)
+    capacity = even_refs[0].shape[0] // blocks
+    for dx in range(blocks):
+        rows = slice(dx * capacity, (dx + 1) * capacity)
+        value = even_refs[0][rows, :].astype(jnp.float32)
+        for dy in range(1, ranges):
+            value += even_refs[dy][rows, :].astype(jnp.float32)
+        out_refs[dx][...] = value.astype(jnp.bfloat16)
+    for dy in range(ranges):
+        value = spread(pos_ref[0, 0], odd_refs[0][dy])
         for dx in range(1, blocks):
-            value += spread(pos_ref[1, dx], even_refs[dx][...])
-        out_refs[0][...] = value.astype(jnp.bfloat16)
-        value = odd_refs[0][...].astype(jnp.float32)
-        for dy in range(1, ranges):
-            value += odd_refs[dy][...].astype(jnp.float32)
-        out_refs[1][...] = value.astype(jnp.bfloat16)
-
-    return whole_call(kernel, [pos, *even, *odd], [half(tok_rows, width)] * 2, after=after)
+            value += spread(pos_ref[0, dx], odd_refs[dx][dy])
+        out_refs[blocks + dy][...] = value.astype(jnp.bfloat16)
+
+
+def third_sums(pos_ref, even_refs, odd_refs, out_refs):
+    value = spread(pos_ref[1, 0], even_refs[0][...])
+    for dx in range(1, len(even_refs)):
+        value += spread(pos_ref[1, dx], even_refs[dx][...])
+    out_refs[0][...] = value.astype(jnp.bfloat16)
+    value = odd_refs[0][...].astype(jnp.float32)
+    for ref in odd_refs[1:]:
+        value += ref[...].astype(jnp.float32)
+    out_refs[1][...] = value.astype(jnp.bfloat16)
+
+
+def return_sums(second, third, after):
+    args, shapes, works = [], [], []
+    for body, held in ((second_sums, second), (third_sums, third)):
+        if held is None:
+            continue
+        pos, even, odd = held
+        tok_rows, width = pos.shape[3], even[0].shape[1]
+        outs = [half(tok_rows, width)] * 2
+        if body is second_sums:
+            outs = [half(even[0].shape[0] // len(odd), width)] * len(odd)
+            outs += [half(tok_rows, width)] * len(even)
+        works.append((body, len(args), len(even), len(odd), len(shapes), len(outs)))
+        args += [pos, *even, *odd]
+        shapes += outs
+
+    def kernel(*refs):
+        in_refs, out_refs = refs[: len(args)], refs[len(args) :]
+        for body, at, evens, odds, out_at, count in works:
+            even_at = at + 1
+            odd_at = even_at + evens
+            body(
+                in_refs[at],
+                in_refs[even_at:odd_at],
+                in_refs[odd_at : odd_at + odds],
+                out_refs[out_at : out_at + count],
+            )
+
+    outs = whole_call(kernel, args, shapes, after=after)
+    return [outs[out_at : out_at + count] for *_, out_at, count in works]
 
 
 def add_up(parts):
@@ -452,7 +466,8 @@
 
     sizes = (blocks, ranges, capacity)
     packed = pack(tokens, grad_out, probs.T, expert_ids.T)
-    line = [along_z(packed, k) for k in range(DEPTH)]
+    near = along_z(packed, 1)
+    line = [packed, near, along_z(near, 1), along_z(packed, DEPTH - 1)]
 
     def first_hops(pair):
         even = [along_x(line[pair[0]], dx) for dx in range(blocks)]
@@ -484,14 +499,12 @@
         arrived = [along_y(a, -dy) for dy, a in enumerate(even)]
         return (*even, *odd), arrived, [along_x(a, -dx) for dx, a in enumerate(odd)]
 
-    def second_step(pos, even, odd, after):
-        even, odd = second_returns(pos, even, odd, after)
-        arrived = [along_x(a, -dx) for dx, a in enumerate(even)]
-        return (*even, *odd), arrived, [along_y(a, -dy) for dy, a in enumerate(odd)]
-
-    def third_step(pair, pos, even, odd, after):
-        outs = third_returns(pos, even, odd, after)
-        return tuple(outs), [along_z(a, -k) for k, a in zip(pair, outs)]
+    def second_hops(outs):
+        arrived = [along_x(a, -dx) for dx, a in enumerate(outs[:blocks])]
+        return arrived, [along_y(a, -dy) for dy, a in enumerate(outs[blocks:])]
+
+    def third_hops(pair, outs):
+        return [along_z(a, -k) for k, a in zip(pair, outs)]
 
     pos_a, names, arrays_a = gathered(*first_hops(PAIRS[0]), ())
     even_b, odd_b = first_hops(PAIRS[1])
@@ -506,17 +519,20 @@
     other_b, *lefts = partials_of_core(
         1, len(PAIRS), order, 1, carried[3:], weights, ranges, True, done
     )
-    done, even_a, odd_a = second_step(pos_a, even_a, odd_a, (other_b,))
+    (done,) = return_sums((pos_a, even_a, odd_a), None, (other_b,))
+    even_a, odd_a = second_hops(done)
     other_b = along_c(ordered(other_b, done), -1)
     (own_b,) = partials_of_core(1, len(PAIRS), order, 0, lefts, weights, ranges, False, done)
     done, even_b, odd_b = first_step(own_b, other_b, ())
-    done_a, returned_a = third_step(PAIRS[0], pos_a, even_a, odd_a, done)
-    grad_down = weight_grad(hidden, g_all, done + done_a)
-    done, even_b, odd_b = second_step(pos_b, even_b, odd_b, (grad_down,))
-    grad_gate = weight_grad(grad_pre_gate, x_all, done)
-    done, returned_b = third_step(PAIRS[1], pos_b, even_b, odd_b, (grad_gate,))
-    grad_up = weight_grad(grad_pre_up, x_all, done)
-    grad_tokens = add_up(returned_a + returned_b)
+    grad_down = weight_grad(hidden, g_all, done)
+    second, third = return_sums((pos_b, even_b, odd_b), (pos_a, even_a, odd_a), (grad_down,))
+    even_b, odd_b = second_hops(second)
+    returned = third_hops(PAIRS[0], third)
+    grad_gate = weight_grad(grad_pre_gate, x_all, (*second, *third))
+    (third,) = return_sums(None, (pos_b, even_b, odd_b), (grad_gate,))
+    grad_up = weight_grad(grad_pre_up, x_all, third)
+    returned += third_hops(PAIRS[1], third)
+    grad_tokens = add_up(returned)
     return (grad_tokens, grad_gate.T[None], grad_up.T[None], grad_down[None])
 
 

time: 204 us -> 199 us (0.975)
    pallas_call x7 -> x6, Pallas kernels: 18.4 us -> 16.7 us  [whole_call(): pl.pallas_call(body, in_specs=[ANY] * skipped + [SMEM] * len(scalars) + [...]
    unnamed x60 -> x62, local copies, waits for them, and re-layouts: 6.25 us -> 6.37 us
  transfers between devices with their start and end apart: 30 -> 30, of which waited for: 6 -> 5; matrix products, arithmetic and copies ran while one was open for 18% -> 18% of each run, Pallas kernels for 42% -> 41%
where the time goes in v5:
time: 199 us
  Pallas kernels  88.2 us (44%)
  waiting for transfers between devices  35.7 us (18%)
  matrix products  31.2 us (16%)
  starting transfers between devices  30 us (15%)
  other arithmetic  6.73 us (3%)
  local copies, waits for them, and re-layouts  6.37 us (3%)
    pallas_call x2, Pallas kernels, hidden_units(): pl.pallas_call(kernel, grid_spec=pltpu.PrefetchScalarGridSpec(num_scalar_...  40.2 us
    ppermute x30, waiting for transfers between devices, shifted(): return lax.ppermute(value, axis, pairs)  35.7 us
    dot_general x3, matrix products, product(): return jnp.dot(left, right, preferred_element_type=jnp.float32)  31.2 us
    ppermute x30, starting transfers between devices, shifted(): return lax.ppermute(value, axis, pairs)  30 us
    pallas_call x2, Pallas kernels, partials_of_core(): pl.pallas_call(kernel, grid_spec=pltpu.PrefetchScalarGridSpec(num_scalar_...  17.5 us
    pallas_call x6, Pallas kernels, whole_call(): pl.pallas_call(body, in_specs=[ANY] * skipped + [SMEM] * len(scalars) + [...  16.7 us
    pallas_call x1, Pallas kernels, partials(): pl.pallas_call(kernel, grid_spec=pltpu.PrefetchScalarGridSpec(num_scalar_...  13.8 us
    unnamed x62, local copies, waits for them, and re-layouts  6.37 us
  transfers between devices with their start and end apart: 30, of which 5 were waited for; matrix products, arithmetic and copies ran while one was open for 18% of the time, Pallas kernels for 41%

profile of v5, /device:TPU:0, one launch (start us, length us, event | category | flops | bytes accessed | tf_op | source)
XLA Modules:
  0.0 199.0 jit_solution(7595765221343817293)
XLA Ops:
  0.6 1.8 shard_map.102.refs_1_
  2.4 3.0 %collective-permute-start.1 = (bf16[272,768]{1,0:T(8,128)(2,1)}, bf16[272,768]{1,0:T(8,128)(2,1)S(1)}, u32[]{:S(2)}, u32[]{:S(2)}) collective-permute-start(bf16[272,768]{1,0:T(8,128)(2,1)} %shard_map.102.refs_1_), channel_id=1, source_target_pairs={{0,8},{4,12},{8,16},{12,20},{16,24},{20,28},{24,0},{28,4},{1,9},{5... | collective-permute-start | bytes 1253384 | tf_op jit(solution)/shard_map/ppermute | solution.py:55
  5.5 1.5 collective-permute-start
  7.0 10.4 %collective-permute-done.1.refs_3_ = bf16[272,768]{1,0:T(8,128)(2,1)S(1)} collective-permute-done((bf16[272,768]{1,0:T(8,128)(2,1)}, bf16[272,768]{1,0:T(8,128)(2,1)S(1)}, u32[]{:S(2)}, u32[]{:S(2)}) %collective-permute-start.1) | collective-permute-done | bytes 417824 | tf_op jit(solution)/shard_map/ppermute | solution.py:55
  17.3 1.5 collective-permute-start.2
  18.9 1.7 collective-permute-start.7
  21.6 6.6 %collective-permute-done.2.refs_4_ = bf16[272,768]{1,0:T(8,128)(2,1)S(1)} collective-permute-done((bf16[272,768]{1,0:T(8,128)(2,1)S(1)}, bf16[272,768]{1,0:T(8,128)(2,1)S(1)}, u32[]{:S(2)}, u32[]{:S(2)}) %collective-permute-start.2) | collective-permute-done | bytes 417824 | tf_op jit(solution)/shard_map/ppermute | solution.py:55
  28.9 3.5 %shard_map.103 = (bf16[2,384,768]{2,1,0:T(8,128)(2,1)}, bf16[2,192,768]{2,1,0:T(8,128)(2,1)}, bf16[2,192,768]{2,1,0:T(8,128)(2,1)}, s32[2,2,1,128]{3,2,1,0:T(1,128)}) custom-call(s32[2]{0:T(128)} %pad_add_fusion.1.refs_0_.refs_3_, bf16[272,768]{1,0:T(8,128)(2,1)} %shard_map.102.refs_1_, bf16[272,768]{1,0:T(8,128)(2,1)} %copy-done.19, ...), custom_call_target="tpu_custom_call" | custom-call | bytes 1 | tf_op jit(solution)/shard_map/pallas_call | solution.py:65
  32.4 1.3 collective-permute-start.3
  33.7 1.5 collective-permute-start.4
  35.2 3.9 %collective-permute-start.8 = (bf16[272,768]{1,0:T(8,128)(2,1)S(1)}, bf16[272,768]{1,0:T(8,128)(2,1)S(1)}, u32[]{:S(2)}, u32[]{:S(2)}) collective-permute-start(bf16[272,768]{1,0:T(8,128)(2,1)S(1)} %collective-permute-done.7.refs_6_), channel_id=1, source_target_pairs={{0,2},{1,3},{2,0},{3,1},{4,6},{5,7},{6,4},{7,5},{8,10},{9,11},{10,... | collective-permute-start | bytes 1253384 | tf_op jit(solution)/shard_map/ppermute | solution.py:55
  39.9 15.3 %collective-permute-done.8.refs_7_ = bf16[272,768]{1,0:T(8,128)(2,1)S(1)} collective-permute-done((bf16[272,768]{1,0:T(8,128)(2,1)S(1)}, bf16[272,768]{1,0:T(8,128)(2,1)S(1)}, u32[]{:S(2)}, u32[]{:S(2)}) %collective-permute-start.8) | collective-permute-done | bytes 417824 | tf_op jit(solution)/shard_map/ppermute | solution.py:55
  57.2 3.5 %shard_map.104 = (bf16[2,384,768]{2,1,0:T(8,128)(2,1)}, bf16[2,192,768]{2,1,0:T(8,128)(2,1)}, bf16[2,192,768]{2,1,0:T(8,128)(2,1)}, s32[2,2,1,128]{3,2,1,0:T(1,128)}) custom-call(bf16[2,384,768]{2,1,0:T(8,128)(2,1)} %get-tuple-element.49.refs_0_, bf16[2,192,768]{2,1,0:T(8,128)(2,1)} %copy-done.8, bf16[2,192,768]{2,1,0:T(8,128)(2,1)} %copy-done.9, ...), custom_call_target="tpu_custom_call" | custom-call | bytes 1 | tf_op jit(solution)/shard_map/pallas_call | solution.py:65
  63.6 20.5 %shard_map.105 = (bf16[768,3072]{1,0:T(8,128)(2,1)}, bf16[768,3072]{1,0:T(8,128)(2,1)}, bf16[1344,768]{1,0:T(8,128)(2,1)}, bf16[1344,768]{1,0:T(8,128)(2,1)}, bf16[1344,768]{1,0:T(8,128)(2,1)}) custom-call(s32[4]{0:T(128)} %pad_add_fusion.order_ref, bf16[2,384,768]{2,1,0:T(8,128)(2,1)} %get-tuple-element.49.refs_0_, ...), custom_call_target="tpu_custom_call" | custom-call | flops 9512681472 | bytes 37306368 | tf_op jit(solution)/shard_map/pallas_call | solution.py:216
  85.1 13.8 %shard_map.106 = (bf16[2,384,768]{2,1,0:T(8,128)(2,1)}, bf16[2,384,768]{2,1,0:T(8,128)(2,1)}) custom-call(s32[4]{0:T(128)} %pad_add_fusion.order_ref, bf16[1344,768]{1,0:T(8,128)(2,1)} %get-tuple-element.62.gpg_ref.refs_12_, bf16[1344,768]{1,0:T(8,128)(2,1)} %get-tuple-element.63.gpu_ref.refs_13_, bf16[1344,3072]{1,0:T(8,128)(2,1)} %bitcast.36, ...), custom_call_target="tpu_custom_call" | custom-call | flops 6341787648 | bytes 20938752 | tf_op jit(solution)/shard_map/pallas_call | solution.py:261
  99.5 1.0 copy-done.5
  100.9 19.7 %shard_map.107 = (bf16[768,3072]{1,0:T(8,128)(2,1)}, bf16[768,3072]{1,0:T(8,128)(2,1)}, bf16[1344,768]{1,0:T(8,128)(2,1)}, bf16[1344,768]{1,0:T(8,128)(2,1)}, bf16[1344,768]{1,0:T(8,128)(2,1)}) custom-call(s32[4]{0:T(128)} %pad_add_fusion.order_ref, ...), custom_call_target="tpu_custom_call", output_to_operand_aliasing={{0}: (10, {}), {1}: (11, {}), {2}: (12, {}), {3}: (13, {}),... | custom-call | flops 9512681472 | bytes 37306368 | tf_op jit(solution)/shard_map/pallas_call | solution.py:216
  122.3 1.5 collective-permute-start.18
  124.3 9.0 %shard_map.108 = (bf16[2,384,768]{2,1,0:T(8,128)(2,1)}, bf16[384,1344]{1,0:T(8,128)(2,1)}, bf16[384,1344]{1,0:T(8,128)(2,1)}) custom-call(s32[4]{0:T(128)} %pad_add_fusion.order_ref, bf16[1344,768]{1,0:T(8,128)(2,1)} %get-tuple-element.89.lg_ref, bf16[1344,768]{1,0:T(8,128)(2,1)} %get-tuple-element.93.lu_ref, bf16[1344,3072]{1,0:T(8,128)(2,1)} %bitcast.38, ...), custom_call_target="tpu_custom_call" | custom-call | flops 3170893824 | bytes 11501568 | tf_op jit(solution)/shard_map/pallas_call | solution.py:301
  134.2 2.6 %shard_map.109 = (bf16[96,768]{1,0:T(8,128)(2,1)}, bf16[96,768]{1,0:T(8,128)(2,1)}, bf16[128,768]{1,0:T(8,128)(2,1)}, bf16[128,768]{1,0:T(8,128)(2,1)}) custom-call(bf16[2,384,768]{2,1,0:T(8,128)(2,1)} %get-tuple-element.79.refs_0_, s32[2,2,1,128]{3,2,1,0:T(1,128)} %get-tuple-element.74.refs_1_.refs_6_, bf16[192,768]{1,0:T(8,128)(2,1)} %get-tuple-element.101.refs_0_.refs_2_, ...), custom_call_target="tpu_custom_call" | custom-call | bytes 1 | tf_op jit(solution)/shard_map/pallas_call | solution.py:65
  136.8 1.6 collective-permute-start.23
  138.8 8.4 %shard_map.110 = bf16[2,384,768]{2,1,0:T(8,128)(2,1)} custom-call(s32[4]{0:T(128)} %pad_add_fusion.order_ref, bf16[384,1344]{1,0:T(8,128)(2,1)} %get-tuple-element.71.lg_ref, bf16[384,1344]{1,0:T(8,128)(2,1)} %get-tuple-element.72.lu_ref, bf16[1344,3072]{1,0:T(8,128)(2,1)} %bitcast.39, bf16[1344,3072]{1,0:T(8,128)(2,1)} %bitcast.44, ...), custom_call_target="tpu_custom_call" | custom-call | flops 3170893824 | bytes 11501568 | tf_op jit(solution)/shard_map/pallas_call | solution.py:301
  147.2 2.0 %fusion.4 = (bf16[192,768]{1,0:T(8,128)(2,1)S(1)}, bf16[192,768]{1,0:T(8,128)(2,1)}) fusion(bf16[2,384,768]{2,1,0:T(8,128)(2,1)S(1)} %collective-permute-done.20, bf16[2,384,768]{2,1,0:T(8,128)(2,1)} %shard_map.110), kind=kLoop, calls=%fused_computation.16 | loop fusion | flops 1179648 | bytes 1769472 | tf_op jit(solution)/shard_map/convert_element_type | solution.py:329
  149.3 1.6 collective-permute-start.21
  152.3 9.1 %convolution_convert_fusion.2.refs_0_ = bf16[1344,3072]{1,0:T(8,128)(2,1)} fusion(bf16[1344,768]{1,0:T(8,128)(2,1)S(1)} %copy-done.4, bf16[768,3072]{1,0:T(8,128)(2,1)S(1)} %bitcast.50), kind=kOutput, calls=%fused_computation.2 | convolution fusion | flops 6345916416 | bytes 15040512 | tf_op jit(solution)/shard_map/dot_general | solution.py:20
  162.2 3.1 %shard_map.111 = (bf16[96,768]{1,0:T(8,128)(2,1)}, bf16[96,768]{1,0:T(8,128)(2,1)}, bf16[128,768]{1,0:T(8,128)(2,1)}, bf16[128,768]{1,0:T(8,128)(2,1)}, bf16[128...) custom-call(bf16[1344,3072]{1,0:T(8,128)(2,1)} %convolution_convert_fusion.2.refs_0_, ...), custom_call_target="tpu_custom_call" | custom-call | bytes 1 | tf_op jit(solution)/shard_map/pallas_call | solution.py:65
  165.3 1.5 collective-permute-start.26
  166.8 1.6 collective-permute-start.25
  168.9 11.1 %convolution_convert_fusion.1.refs_0_ = bf16[1344,3072]{1,0:T(8,128)(2,1)} fusion(bf16[1344,768]{1,0:T(8,128)(2,1)S(1)} %copy-done, bf16[768,3072]{1,0:T(8,128)(2,1)} %get-tuple-element.90), kind=kOutput, calls=%fused_computation.1 | convolution fusion | flops 6345916416 | bytes 15040512 | tf_op jit(solution)/shard_map/dot_general | solution.py:20
  181.3 2.3 %shard_map.112 = (bf16[128,768]{1,0:T(8,128)(2,1)}, bf16[128,768]{1,0:T(8,128)(2,1)}) custom-call(bf16[1344,3072]{1,0:T(8,128)(2,1)} %convolution_convert_fusion.1.refs_0_, s32[2,2,1,128]{3,2,1,0:T(1,128)} %get-tuple-element.82.refs_1_, bf16[96,768]{1,0:T(8,128)(2,1)} %get-tuple-element.85.refs_2_, bf16[96,768]{1,0:T(8,128)(2,1)} %copy-done.27, ...), custom_call_target="tpu_custom_call" | custom-call | bytes 1 | tf_op jit(solution)/shard_map/pallas_call | solution.py:65
  184.5 11.1 %fusion = bf16[1,3072,1344]{1,2,0:T(8,128)(2,1)} fusion(bf16[1344,768]{1,0:T(8,128)(2,1)S(1)} %copy-done.1, bf16[768,3072]{1,0:T(8,128)(2,1)} %get-tuple-element.90), kind=kOutput, calls=%fused_computation.3 | convolution fusion | flops 6345916416 | bytes 15040512 | tf_op jit(solution)/shard_map/dot_general | solution.py:20
  195.6 2.6 %collective-permute-done.28 = bf16[128,768]{1,0:T(8,128)(2,1)S(1)} collective-permute-done((bf16[128,768]{1,0:T(8,128)(2,1)}, bf16[128,768]{1,0:T(8,128)(2,1)S(1)}, u32[]{:S(2)}, u32[]{:S(2)}) %collective-permute-start.28) | collective-permute-done | bytes 196640 | tf_op jit(solution)/shard_map/ppermute | solution.py:55
  (112 shorter events, 18.6 us)
Async XLA Ops:
  2.4 14.9 %collective-permute-start.1 = (bf16[272,768]{1,0:T(8,128)(2,1)}, bf16[272,768]{1,0:T(8,128)(2,1)S(1)}, u32[]{:S(2)}, u32[]{:S(2)}) collective-permute-start(bf16[272,768]{1,0:T(8,128)(2,1)} %shard_map.102.refs_1_), channel_id=1, source_target_pairs={{0,8},{4,12},{8,16},{12,20},{16,24},{20,28},{24,0},{28,4},{1,9},{5... | collective-permute-start | bytes 1253384 | tf_op jit(solution)/shard_map/ppermute | solution.py:55
  5.5 16.1 %collective-permute-start = (bf16[272,768]{1,0:T(8,128)(2,1)}, bf16[272,768]{1,0:T(8,128)(2,1)S(1)}, u32[]{:S(2)}, u32[]{:S(2)}) collective-permute-start(bf16[272,768]{1,0:T(8,128)(2,1)} %shard_map.102.refs_1_), channel_id=1, source_target_pairs={{0,4},{4,0},{8,12},{12,8},{16,20},{20,16},{24,28},{28,24},{1,5},{5... | collective-permute-start | bytes 1253384 | tf_op jit(solution)/shard_map/ppermute | solution.py:55
  17.3 10.8 %collective-permute-start.2 = (bf16[272,768]{1,0:T(8,128)(2,1)S(1)}, bf16[272,768]{1,0:T(8,128)(2,1)S(1)}, u32[]{:S(2)}, u32[]{:S(2)}) collective-permute-start(bf16[272,768]{1,0:T(8,128)(2,1)S(1)} %collective-permute-done.1.refs_3_), channel_id=1, source_target_pairs={{0,2},{1,3},{2,0},{3,1},{4,6},{5,7},{6,4},{7,5},{8,10},{9,11},{10,... | collective-permute-start | bytes 1253384 | tf_op jit(solution)/shard_map/ppermute | solution.py:55
  18.9 16.3 %collective-permute-start.7 = (bf16[272,768]{1,0:T(8,128)(2,1)}, bf16[272,768]{1,0:T(8,128)(2,1)S(1)}, u32[]{:S(2)}, u32[]{:S(2)}) collective-permute-start(bf16[272,768]{1,0:T(8,128)(2,1)} %shard_map.102.refs_1_), channel_id=1, source_target_pairs={{0,24},{4,28},{8,0},{12,4},{16,8},{20,12},{24,16},{28,20},{1,25},{... | collective-permute-start | bytes 1253384 | tf_op jit(solution)/shard_map/ppermute | solution.py:55
  20.6 18.5 %collective-permute-start.5 = (bf16[272,768]{1,0:T(8,128)(2,1)S(1)}, bf16[272,768]{1,0:T(8,128)(2,1)S(1)}, u32[]{:S(2)}, u32[]{:S(2)}) collective-permute-start(bf16[272,768]{1,0:T(8,128)(2,1)S(1)} %collective-permute-done.1.refs_3_), channel_id=1, source_target_pairs={{0,8},{4,12},{8,16},{12,20},{16,24},{20,28},{24,0},{28,4},{1,9},{5... | collective-permute-start | bytes 1253384 | tf_op jit(solution)/shard_map/ppermute | solution.py:55
  32.4 23.5 %collective-permute-start.3 = (bf16[2,192,768]{2,1,0:T(8,128)(2,1)}, bf16[2,192,768]{2,1,0:T(8,128)(2,1)S(1)}, u32[]{:S(2)}, u32[]{:S(2)}) collective-permute-start(bf16[2,192,768]{2,1,0:T(8,128)(2,1)} %get-tuple-element.50), channel_id=1, source_target_pairs={{0,2},{1,3},{2,0},{3,1},{4,6},{5,7},{6,4},{7,5},{8,10},{9,11},{10,... | collective-permute-start | bytes 1769480 | tf_op jit(solution)/shard_map/ppermute | solution.py:55
  33.7 22.2 %collective-permute-start.4 = (bf16[2,192,768]{2,1,0:T(8,128)(2,1)}, bf16[2,192,768]{2,1,0:T(8,128)(2,1)S(1)}, u32[]{:S(2)}, u32[]{:S(2)}) collective-permute-start(bf16[2,192,768]{2,1,0:T(8,128)(2,1)} %get-tuple-element.51), channel_id=1, source_target_pairs={{0,4},{4,0},{8,12},{12,8},{16,20},{20,16},{24,28},{28,24},{1,5},{5... | collective-permute-start | bytes 1769480 | tf_op jit(solution)/shard_map/ppermute | solution.py:55
  35.2 27.5 %collective-permute-start.12 = (bf16[2,384,768]{2,1,0:T(8,128)(2,1)}, bf16[2,384,768]{2,1,0:T(8,128)(2,1)}, u32[]{:S(2)}, u32[]{:S(2)}) collective-permute-start(bf16[2,384,768]{2,1,0:T(8,128)(2,1)} %get-tuple-element.49.refs_0_), channel_id=1, source_target_pairs={{0,1},{1,0},{2,3},{3,2},{4,5},{5,4},{6,7},{7,6},{8,9},{9,8},{10,11... | collective-permute-start | bytes 3538952 | tf_op jit(solution)/shard_map/ppermute | solution.py:55
  35.2 22.0 %copy-start.14 = (bf16[272,768]{1,0:T(8,128)(2,1)}, bf16[272,768]{1,0:T(8,128)(2,1)S(1)}, u32[]{:S(2)}) copy-start(bf16[272,768]{1,0:T(8,128)(2,1)S(1)} %collective-permute-done.7.refs_6_) | copy-start | bytes 1253380
  35.2 20.0 %collective-permute-start.8 = (bf16[272,768]{1,0:T(8,128)(2,1)S(1)}, bf16[272,768]{1,0:T(8,128)(2,1)S(1)}, u32[]{:S(2)}, u32[]{:S(2)}) collective-permute-start(bf16[272,768]{1,0:T(8,128)(2,1)S(1)} %collective-permute-done.7.refs_6_), channel_id=1, source_target_pairs={{0,2},{1,3},{2,0},{3,1},{4,6},{5,7},{6,4},{7,5},{8,10},{9,11},{10,... | collective-permute-start | bytes 1253384 | tf_op jit(solution)/shard_map/ppermute | solution.py:55
  39.1 16.8 %collective-permute-start.6 = (bf16[272,768]{1,0:T(8,128)(2,1)S(1)}, bf16[272,768]{1,0:T(8,128)(2,1)S(1)}, u32[]{:S(2)}, u32[]{:S(2)}) collective-permute-start(bf16[272,768]{1,0:T(8,128)(2,1)S(1)} %collective-permute-done.5.refs_4_), channel_id=1, source_target_pairs={{0,4},{4,0},{8,12},{12,8},{16,20},{20,16},{24,28},{28,24},{1,5},{5... | collective-permute-start | bytes 1253384 | tf_op jit(solution)/shard_map/ppermute | solution.py:55
  55.9 6.8 %collective-permute-start.13 = (bf16[2,192,768]{2,1,0:T(8,128)(2,1)S(1)}, bf16[2,192,768]{2,1,0:T(8,128)(2,1)S(1)}, u32[]{:S(2)}, u32[]{:S(2)}) collective-permute-start(bf16[2,192,768]{2,1,0:T(8,128)(2,1)S(1)} %collective-permute-done.3.refs_1_.refs_2_), channel_id=1, source_target_pairs={{0,1},{1,0},{2,3},{3,2},{4,5},{5,4},{6,7},{7,6},{8,9},{9,8},{10,11... | collective-permute-start | bytes 1769480 | tf_op jit(solution)/shard_map/ppermute | solution.py:55
  56.0 6.7 %collective-permute-start.14 = (bf16[2,192,768]{2,1,0:T(8,128)(2,1)S(1)}, bf16[2,192,768]{2,1,0:T(8,128)(2,1)}, u32[]{:S(2)}, u32[]{:S(2)}) collective-permute-start(bf16[2,192,768]{2,1,0:T(8,128)(2,1)S(1)} %collective-permute-done.4.refs_2_.refs_4_), channel_id=1, source_target_pairs={{0,1},{1,0},{2,3},{3,2},{4,5},{5,4},{6,7},{7,6},{8,9},{9,8},{10,11... | collective-permute-start | bytes 1769480 | tf_op jit(solution)/shard_map/ppermute | solution.py:55
  60.7 23.3 %collective-permute-start.10 = (bf16[2,192,768]{2,1,0:T(8,128)(2,1)}, bf16[2,192,768]{2,1,0:T(8,128)(2,1)S(1)}, u32[]{:S(2)}, u32[]{:S(2)}) collective-permute-start(bf16[2,192,768]{2,1,0:T(8,128)(2,1)} %get-tuple-element.53), channel_id=1, source_target_pairs={{0,2},{1,3},{2,0},{3,1},{4,6},{5,7},{6,4},{7,5},{8,10},{9,11},{10,... | collective-permute-start | bytes 1769480 | tf_op jit(solution)/shard_map/ppermute | solution.py:55
  61.7 22.4 %collective-permute-start.11 = (bf16[2,192,768]{2,1,0:T(8,128)(2,1)}, bf16[2,192,768]{2,1,0:T(8,128)(2,1)S(1)}, u32[]{:S(2)}, u32[]{:S(2)}) collective-permute-start(bf16[2,192,768]{2,1,0:T(8,128)(2,1)} %get-tuple-element.54), channel_id=1, source_target_pairs={{0,4},{4,0},{8,12},{12,8},{16,20},{20,16},{24,28},{28,24},{1,5},{5... | collective-permute-start | bytes 1769480 | tf_op jit(solution)/shard_map/ppermute | solution.py:55
  62.7 36.7 %collective-permute-start.9 = (bf16[2,384,768]{2,1,0:T(8,128)(2,1)}, bf16[2,384,768]{2,1,0:T(8,128)(2,1)S(1)}, u32[]{:S(2)}, u32[]{:S(2)}) collective-permute-start(bf16[2,384,768]{2,1,0:T(8,128)(2,1)} %get-tuple-element.52.refs_9_.refs_0_), channel_id=1, source_target_pairs={{0,1},{1,0},{2,3},{3,2},{4,5},{5,4},{6,7},{7,6},{8,9},{9,8},{10,11... | collective-permute-start | bytes 3538952 | tf_op jit(solution)/shard_map/ppermute | solution.py:55
  84.1 15.3 %collective-permute-start.15 = (bf16[2,192,768]{2,1,0:T(8,128)(2,1)S(1)}, bf16[2,192,768]{2,1,0:T(8,128)(2,1)S(1)}, u32[]{:S(2)}, u32[]{:S(2)}) collective-permute-start(bf16[2,192,768]{2,1,0:T(8,128)(2,1)S(1)} %collective-permute-done.10.refs_0_.refs_2_), channel_id=1, source_target_pairs={{0,1},{1,0},{2,3},{3,2},{4,5},{5,4},{6,7},{7,6},{8,9},{9,8},{10,11... | collective-permute-start | bytes 1769480 | tf_op jit(solution)/shard_map/ppermute | solution.py:55
  84.7 14.8 %collective-permute-start.16 = (bf16[2,192,768]{2,1,0:T(8,128)(2,1)S(1)}, bf16[2,192,768]{2,1,0:T(8,128)(2,1)S(1)}, u32[]{:S(2)}, u32[]{:S(2)}) collective-permute-start(bf16[2,192,768]{2,1,0:T(8,128)(2,1)S(1)} %collective-permute-done.11.refs_1_.refs_4_), channel_id=1, source_target_pairs={{0,1},{1,0},{2,3},{3,2},{4,5},{5,4},{6,7},{7,6},{8,9},{9,8},{10,11... | collective-permute-start | bytes 1769480 | tf_op jit(solution)/shard_map/ppermute | solution.py:55
  98.9 21.6 %collective-permute-start.17 = (bf16[2,384,768]{2,1,0:T(8,128)(2,1)}, bf16[2,384,768]{2,1,0:T(8,128)(2,1)S(1)}, u32[]{:S(2)}, u32[]{:S(2)}) collective-permute-start(bf16[2,384,768]{2,1,0:T(8,128)(2,1)} %get-tuple-element.68), channel_id=1, source_target_pairs={{0,1},{1,0},{2,3},{3,2},{4,5},{5,4},{6,7},{7,6},{8,9},{9,8},{10,11... | collective-permute-start | bytes 3538952 | tf_op jit(solution)/shard_map/ppermute | solution.py:55
  100.9 19.7 %copy-start.2 = (bf16[2,384,768]{2,1,0:T(8,128)(2,1)S(1)}, bf16[2,384,768]{2,1,0:T(8,128)(2,1)}, u32[]{:S(2)}) copy-start(bf16[2,384,768]{2,1,0:T(8,128)(2,1)} %get-tuple-element.69.refs_14_) | copy-start | bytes 3538948
  122.3 11.1 %collective-permute-start.18 = (bf16[192,768]{1,0:T(8,128)(2,1)S(1)}, bf16[192,768]{1,0:T(8,128)(2,1)S(1)}, u32[]{:S(2)}, u32[]{:S(2)}) collective-permute-start(bf16[192,768]{1,0:T(8,128)(2,1)S(1)} %get-tuple-element.100.refs_1_), channel_id=1, source_target_pairs={{0,2},{1,3},{2,0},{3,1},{4,6},{5,7},{6,4},{7,5},{8,10},{9,11},{10,... | collective-permute-start | bytes 884744 | tf_op jit(solution)/shard_map/ppermute | solution.py:55
  123.8 9.6 %collective-permute-start.19 = (bf16[2,96,768]{2,1,0:T(8,128)(2,1)S(1)}, bf16[2,96,768]{2,1,0:T(8,128)(2,1)S(1)}, u32[]{:S(2)}, u32[]{:S(2)}) collective-permute-start(bf16[2,96,768]{2,1,0:T(8,128)(2,1)S(1)} %get-tuple-element.98.refs_3_), channel_id=1, source_target_pairs={{0,4},{4,0},{8,12},{12,8},{16,20},{20,16},{24,28},{28,24},{1,5},{5... | collective-permute-start | bytes 884744 | tf_op jit(solution)/shard_map/ppermute | solution.py:55
  136.8 10.5 %collective-permute-start.20 = (bf16[2,384,768]{2,1,0:T(8,128)(2,1)}, bf16[2,384,768]{2,1,0:T(8,128)(2,1)S(1)}, u32[]{:S(2)}, u32[]{:S(2)}) collective-permute-start(bf16[2,384,768]{2,1,0:T(8,128)(2,1)} %get-tuple-element.79.refs_0_), channel_id=1, source_target_pairs={{0,1},{1,0},{2,3},{3,2},{4,5},{5,4},{6,7},{7,6},{8,9},{9,8},{10,11... | collective-permute-start | bytes 3538952 | tf_op jit(solution)/shard_map/ppermute | solution.py:55
  136.8 24.6 %collective-permute-start.23 = (bf16[96,768]{1,0:T(8,128)(2,1)}, bf16[96,768]{1,0:T(8,128)(2,1)}, u32[]{:S(2)}, u32[]{:S(2)}) collective-permute-start(bf16[96,768]{1,0:T(8,128)(2,1)} %get-tuple-element.76.refs_1_), channel_id=1, source_target_pairs={{0,4},{4,0},{8,12},{12,8},{16,20},{20,16},{24,28},{28,24},{1,5},{5... | collective-permute-start | bytes 442376 | tf_op jit(solution)/shard_map/ppermute | solution.py:55
  138.3 23.0 %collective-permute-start.24 = (bf16[128,768]{1,0:T(8,128)(2,1)}, bf16[128,768]{1,0:T(8,128)(2,1)}, u32[]{:S(2)}, u32[]{:S(2)}) collective-permute-start(bf16[128,768]{1,0:T(8,128)(2,1)} %get-tuple-element.78.refs_3_), channel_id=1, source_target_pairs={{0,2},{1,3},{2,0},{3,1},{4,6},{5,7},{6,4},{7,5},{8,10},{9,11},{10,... | collective-permute-start | bytes 589832 | tf_op jit(solution)/shard_map/ppermute | solution.py:55
  149.3 12.1 %collective-permute-start.21 = (bf16[192,768]{1,0:T(8,128)(2,1)S(1)}, bf16[192,768]{1,0:T(8,128)(2,1)S(1)}, u32[]{:S(2)}, u32[]{:S(2)}) collective-permute-start(bf16[192,768]{1,0:T(8,128)(2,1)S(1)} %get-tuple-element.96), channel_id=1, source_target_pairs={{0,2},{1,3},{2,0},{3,1},{4,6},{5,7},{6,4},{7,5},{8,10},{9,11},{10,... | collective-permute-start | bytes 884744 | tf_op jit(solution)/shard_map/ppermute | solution.py:55
  151.8 9.7 %collective-permute-start.22 = (bf16[2,96,768]{2,1,0:T(8,128)(2,1)S(1)}, bf16[2,96,768]{2,1,0:T(8,128)(2,1)S(1)}, u32[]{:S(2)}, u32[]{:S(2)}) collective-permute-start(bf16[2,96,768]{2,1,0:T(8,128)(2,1)S(1)} %get-tuple-element.94), channel_id=1, source_target_pairs={{0,4},{4,0},{8,12},{12,8},{16,20},{20,16},{24,28},{28,24},{1,5},{5... | collective-permute-start | bytes 884744 | tf_op jit(solution)/shard_map/ppermute | solution.py:55
  165.3 14.6 %collective-permute-start.26 = (bf16[96,768]{1,0:T(8,128)(2,1)}, bf16[96,768]{1,0:T(8,128)(2,1)S(1)}, u32[]{:S(2)}, u32[]{:S(2)}) collective-permute-start(bf16[96,768]{1,0:T(8,128)(2,1)} %get-tuple-element.86), channel_id=1, source_target_pairs={{0,4},{4,0},{8,12},{12,8},{16,20},{20,16},{24,28},{28,24},{1,5},{5... | collective-permute-start | bytes 442376 | tf_op jit(solution)/shard_map/ppermute | solution.py:55
  166.8 28.8 %collective-permute-start.25 = (bf16[128,768]{1,0:T(8,128)(2,1)}, bf16[128,768]{1,0:T(8,128)(2,1)S(1)}, u32[]{:S(2)}, u32[]{:S(2)}) collective-permute-start(bf16[128,768]{1,0:T(8,128)(2,1)} %get-tuple-element.84), channel_id=1, source_target_pairs={{0,24},{4,28},{8,0},{12,4},{16,8},{20,12},{24,16},{28,20},{1,25},{... | collective-permute-start | bytes 589832 | tf_op jit(solution)/shard_map/ppermute | solution.py:55
  168.4 11.5 %collective-permute-start.27 = (bf16[128,768]{1,0:T(8,128)(2,1)}, bf16[128,768]{1,0:T(8,128)(2,1)S(1)}, u32[]{:S(2)}, u32[]{:S(2)}) collective-permute-start(bf16[128,768]{1,0:T(8,128)(2,1)} %get-tuple-element.88), channel_id=1, source_target_pairs={{0,2},{1,3},{2,0},{3,1},{4,6},{5,7},{6,4},{7,5},{8,10},{9,11},{10,... | collective-permute-start | bytes 589832 | tf_op jit(solution)/shard_map/ppermute | solution.py:55
  183.5 14.7 %collective-permute-start.28 = (bf16[128,768]{1,0:T(8,128)(2,1)}, bf16[128,768]{1,0:T(8,128)(2,1)S(1)}, u32[]{:S(2)}, u32[]{:S(2)}) collective-permute-start(bf16[128,768]{1,0:T(8,128)(2,1)} %get-tuple-element.91), channel_id=1, source_target_pairs={{0,16},{4,20},{8,24},{12,28},{16,0},{20,4},{24,8},{28,12},{1,17},{... | collective-permute-start | bytes 589832 | tf_op jit(solution)/shard_map/ppermute | solution.py:55
  183.5 14.7 %collective-permute-start.29 = (bf16[128,768]{1,0:T(8,128)(2,1)}, bf16[128,768]{1,0:T(8,128)(2,1)S(1)}, u32[]{:S(2)}, u32[]{:S(2)}) collective-permute-start(bf16[128,768]{1,0:T(8,128)(2,1)} %get-tuple-element.92), channel_id=1, source_target_pairs={{0,8},{4,12},{8,16},{12,20},{16,24},{20,28},{24,0},{28,4},{1,9},{5... | collective-permute-start | bytes 589832 | tf_op jit(solution)/shard_map/ppermute | solution.py:55
  (29 other events, 124.1 us)
